TPU v7x, 128 devices: a whole 4x4x4 slice. The times are simulated.
128 devices in a mesh: gx: 16 (over y, x_lo, core), gy: 8 (over x_hi, z).
Axes of the slice: x: 4 (x_hi: 2, x_lo: 2; x = x_hi * 2 + x_lo), y: 4, z: 4, core: 2. Of those that a mesh axis runs over, the one named last changes fastest.
Arguments:
- fields: float32 [4, 16, 512, 1024], P(None, None, 'gx', 'gy'), may hold values from -4 to 4
- solid_mask: int32 [16, 512, 1024], P(None, 'gx', 'gy'), may hold values 0 or 1
Outputs:
- advanced: float32 [4, 16, 512, 1024], P(None, None, 'gx', 'gy')
Inputs may be any that keep to these rules, and one draw needn't show every extreme that they name: `solid_mask`: 1 marks a solid voxel, 0 a pore voxel.
All inputs are finite; a program needn't handle non-finite values. No bound on the sum of `solid_mask` on one device may be relied on, other than what follows from the above.
Results may differ from a plain program's by a relative error of at most 0.00002.
Values sent between devices are 32-bit elements; how exact they have to be, the bound alone decides.
No kernel may reach another device: no remote copies, remote signals or barrier semaphores. Data moves between devices by JAX's collectives and lax.ppermute only.
A program may use at most 192 MiB of HBM per device.

v0:
```python
import jax
import jax.numpy as jnp
from jax import lax
from jax.sharding import PartitionSpec as P

STEPS = 2


viscosity = 0.05
penalty = 10.0
forcing = 0.5
sound_sq = 2.25
time_step = 0.2


def padded_2(block, sides, width):
    for axis, dim in sides:
        count = lax.axis_size(axis)
        forward = [(i, i + 1) for i in range(count - 1)]
        forward.append((count - 1, 0))
        backward = [(target, source) for source, target in forward]
        low = lax.ppermute(
            lax.slice_in_dim(block, block.shape[dim] - width, None, axis=dim), axis, forward
        )
        high = lax.ppermute(lax.slice_in_dim(block, 0, width, axis=dim), axis, backward)
        block = jnp.concatenate([low, block, high], axis=dim)
    return block


def combine(center, grad_z, grad_x, grad_y, laplace, solid):
    speed = center[0:3]
    advect = center[0] * grad_x[0:3] + center[1] * grad_y[0:3] + center[2] * grad_z[0:3]
    pressure_grad = jnp.stack([grad_x[3], grad_y[3], grad_z[3]])
    drive = jnp.array([forcing, 0.0, 0.0], jnp.float32)[:, None, None, None]
    momentum = -advect - pressure_grad + viscosity * laplace - penalty * solid * speed + drive
    pressure = -sound_sq * (grad_x[0] + grad_y[1] + grad_z[2])
    return jnp.concatenate([momentum, pressure[None]], axis=0)


def first_pair(plus_one, minus_one, plus_two, minus_two):
    return (8.0 * (plus_one - minus_one) - (plus_two - minus_two)) / 12.0


def second_pair(plus_one, minus_one, plus_two, minus_two, middle):
    return (16.0 * (plus_one + minus_one) - (plus_two + minus_two) - 30.0 * middle) / 12.0


def tendency(padded, solid):
    rows_out = padded.shape[2] - 4
    cols_out = padded.shape[3] - 4
    layers = padded.shape[1]

    def window(off_x, off_y):
        return padded[:, :, 2 + off_x : 2 + off_x + rows_out, 2 + off_y : 2 + off_y + cols_out]

    center = window(0, 0)
    wrapped = jnp.concatenate([center[:, layers - 2 :], center, center[:, :2]], axis=1)
    above, below = (wrapped[:, 3 : 3 + layers], wrapped[:, 1 : 1 + layers])
    above_two, below_two = (wrapped[:, 4 : 4 + layers], wrapped[:, 0:layers])
    east, west, east_two, west_two = (window(1, 0), window(-1, 0), window(2, 0), window(-2, 0))
    north, south, north_two, south_two = (window(0, 1), window(0, -1), window(0, 2), window(0, -2))
    grad_z = first_pair(above, below, above_two, below_two)
    grad_x = first_pair(east, west, east_two, west_two)
    grad_y = first_pair(north, south, north_two, south_two)
    speed = center[0:3]
    lap_z = second_pair(above[0:3], below[0:3], above_two[0:3], below_two[0:3], speed)
    lap_x = second_pair(east[0:3], west[0:3], east_two[0:3], west_two[0:3], speed)
    lap_y = second_pair(north[0:3], south[0:3], north_two[0:3], south_two[0:3], speed)
    laplace = lap_z + lap_x + lap_y
    return combine(center, grad_z, grad_x, grad_y, laplace, solid)


def body(fields, solid_mask):
    solid = solid_mask.astype(jnp.float32)
    state = fields

    def evaluate(current):
        padded = padded_2(current, (("gx", 2), ("gy", 3)), 2)
        return tendency(padded, solid)

    for step in range(STEPS):
        section_one = state + time_step * evaluate(state)
        section_two = 0.75 * state + 0.25 * (section_one + time_step * evaluate(section_one))
        state = state / 3.0 + 2.0 / 3.0 * (section_two + time_step * evaluate(section_two))
    return state


def solution(mesh):
    return jax.shard_map(
        body,
        mesh=mesh,
        in_specs=(P(None, None, "gx", "gy"), P(None, "gx", "gy")),
        out_specs=P(None, None, "gx", "gy"),
        check_vma=False,
    )
```

profile of v0, /device:TPU:0, one launch (start us, length us, event | category | flops | bytes accessed | tf_op | source)
XLA Modules:
  0.0 549.5 jit_solution(3367854735158438061)
XLA Ops:
  1.7 3.5 collective-permute-start
  10.5 4.1 fusion.250
  14.7 3.8 copy.351
  27.0 8.9 %subtract_multiply_fusion = f32[4,16,32,128]{2,1,3,0:T(8,128)} fusion(f32[4,16,32,128]{2,1,3,0:T(8,128)} %copy.352, f32[4,16,32,128]{2,1,3,0:T(8,128)} %copy.353, f32[4,16,32,128]{2,1,3,0:T(8,128)} %copy.350, f32[4,16,32,128]{2,1,3,0:T(8,128)} %copy.351), kind=kLoop, calls=%fused_computation.197 | loop fusion | flops 1310720 | bytes 5242880 | tf_op jit(solution)/shard_map/div | solution.py:41
  47.1 3.3 copy.355
  50.4 3.2 copy.357
  61.0 2.9 copy.297
  65.2 6.3 %collective-permute-start.2 = (f32[4,16,36,2]{2,1,3,0:T(8,128)S(1)}, f32[4,16,36,2]{2,1,3,0:T(8,128)S(1)}, u32[]{:S(2)}, u32[]{:S(2)}) collective-permute-start(f32[4,16,36,2]{2,1,3,0:T(8,128)S(1)} %get-tuple-element.27), channel_id=1, source_target_pairs={{1,0},{2,1},{3,2},{4,3},{5,4},{6,5},{7,6},{0,7},{9,8},{10,9},{11,1... | collective-permute-start | bytes 55304 | tf_op jit(solution)/shard_map/ppermute | solution.py:25
  71.7 9.1 %fusion.79 = f32[4,16,32,128]{2,1,3,0:T(8,128)} fusion(f32[4,16,2,128]{2,1,3,0:T(8,128)S(1)} %copy-done.25, f32[4,16,32,128]{2,1,3,0:T(8,128)S(1)} %copy-done.12, f32[4,16,2,128]{2,1,3,0:T(8,128)S(1)} %copy-done.20), kind=kLoop, calls=%fused_computation.174 | loop fusion | flops 2359296 | bytes 2228224 | tf_op jit(solution)/shard_map/div | solution.py:41
  80.8 6.6 %pad_maximum_fusion = (f32[4,16,36,130]{2,1,3,0:T(8,128)}, f32[4,16,36,130]{2,1,3,0:T(8,128)}) fusion(f32[4,16,36,2]{2,1,3,0:T(8,128)S(1)} %collective-permute-done.2, f32[4,16,2,128]{2,1,3,0:T(8,128)S(1)} %copy-done.25, f32[4,16,32,128]{2,1,3,0:T(8,128)S(1)} %copy-done.12, f32[4,16,2,128]{2,1,3,0:T(8,128)S(1)} %copy-done.20, ...), kind=kLoop, calls=%fused_computation.60 | loop fusion | flops 1797120 | bytes 3612672 | tf_op jit(solution)/shard_map/concatenate | solution.py:26
  87.4 8.5 %fusion.76 = f32[4,16,32,128]{2,1,3,0:T(8,128)S(1)} fusion(f32[4,16,36,130]{2,1,3,0:T(8,128)} %get-tuple-element.26, f32[4,16,36,130]{2,1,3,0:T(8,128)} %get-tuple-element.25), kind=kLoop, calls=%fused_computation.169 | loop fusion | flops 1310720 | bytes 5242880 | tf_op jit(solution)/shard_map/div | solution.py:41
  98.9 21.9 %fusion.165 = f32[3,16,32,128]{2,1,3,0:T(8,128)} fusion(f32[4,16,2,128]{2,1,3,0:T(8,128)} %copy.299, f32[4,16,32,128]{2,1,3,0:T(8,128)S(1)} %copy-done.12, f32[4,16,2,128]{2,1,3,0:T(8,128)} %copy.297, f32[4,16,36,130]{2,1,3,0:T(8,128)} %get-tuple-element.26, f32[4,16,36,130]{2,1,3,0:T(8,128)} %get-tuple-element.25, ...), kind=kLoop, calls=%fused_computation.292 | loop fusion | flops 7077888 | bytes 19530240 | tf_op jit(solution)/shard_map/add | solution.py:35
  125.6 4.6 fusion.275
  130.2 3.1 copy.319
  133.3 3.1 copy.317
  136.4 3.0 collective-permute-start.4
  139.4 3.6 fusion.276
  152.3 6.0 %collective-permute-start.6 = (f32[4,16,36,2]{2,1,3,0:T(8,128)S(1)}, f32[4,16,36,2]{2,1,3,0:T(8,128)S(1)}, u32[]{:S(2)}, u32[]{:S(2)}) collective-permute-start(f32[4,16,36,2]{2,1,3,0:T(8,128)S(1)} %get-tuple-element.23), channel_id=1, source_target_pairs={{1,0},{2,1},{3,2},{4,3},{5,4},{6,5},{7,6},{0,7},{9,8},{10,9},{11,1... | collective-permute-start | bytes 55304 | tf_op jit(solution)/shard_map/ppermute | solution.py:25
  158.3 13.4 %fusion.73 = (f32[4,16,32,128]{2,1,3,0:T(8,128)}, f32[4,16,32,128]{2,1,3,0:T(8,128)}) fusion(f32[4,16,2,128]{2,1,3,0:T(8,128)S(1)} %copy-done.22, f32[4,16,32,128]{2,1,3,0:T(8,128)S(1)} %copy-done.9, f32[4,16,2,128]{2,1,3,0:T(8,128)S(1)} %copy-done.16, f32[4,2,32,128]{2,1,3,0:T(2,128)} %get-tuple-element.93, f32[4,2,32,128]{2,1,3,0:T(2,128)} %get-tuple-element.92), kind=kLoop, calls=%fused_computation.164 | loop fusion | flops 4718592 | bytes 3538944 | tf_op jit(solution)/shard_map/div | solution.py:41
  171.8 5.8 %pad_maximum_fusion.1 = (f32[4,16,36,130]{2,1,3,0:T(8,128)S(1)}, f32[4,16,36,130]{2,1,3,0:T(8,128)}) fusion(f32[4,16,36,2]{2,1,3,0:T(8,128)S(1)} %collective-permute-done.6, f32[4,16,2,128]{2,1,3,0:T(8,128)S(1)} %copy-done.22, f32[4,16,32,128]{2,1,3,0:T(8,128)S(1)} %copy-done.9, f32[4,16,2,128]{2,1,3,0:T(8,128)S(1)} %copy-done.16, ...), kind=kLoop, calls=%fused_computation.62 | loop fusion | flops 1797120 | bytes 3612672 | tf_op jit(solution)/shard_map/concatenate | solution.py:26
  177.6 8.3 %fusion.70 = f32[4,16,32,128]{2,1,3,0:T(8,128)S(1)} fusion(f32[4,16,36,130]{2,1,3,0:T(8,128)} %get-tuple-element.22, f32[4,16,36,130]{2,1,3,0:T(8,128)S(1)} %get-tuple-element.21), kind=kLoop, calls=%fused_computation.159 | loop fusion | flops 1310720 | bytes 5242880 | tf_op jit(solution)/shard_map/div | solution.py:41
  189.4 16.5 %fusion.153 = f32[3,16,32,128]{2,1,3,0:T(8,128)} fusion(f32[4,16,2,128]{2,1,3,0:T(8,128)S(1)} %copy-done.16, f32[4,16,32,128]{2,1,3,0:T(8,128)S(1)} %copy-done.9, f32[4,16,2,128]{2,1,3,0:T(8,128)} %copy.318, f32[4,2,32,128]{2,1,3,0:T(2,128)S(1)} %copy-done.63, f32[4,2,32,128]{2,1,3,0:T(2,128)S(1)} %copy-done.62, f32[4,16,36,130]{2,1,3,0:T(8,128)} %get-tuple-element.22, ...), kind=kLoop, calls=%fused_computation.280 | loop fusion | flops 7864320 | bytes 21561856 | tf_op jit(solution)/shard_map/add | solution.py:35
  205.9 4.3 fusion.84
  212.2 4.6 fusion.272
  216.8 3.1 copy.325
  219.9 3.1 copy.323
  223.8 3.6 fusion.273
  236.7 6.0 %collective-permute-start.10 = (f32[4,16,36,2]{2,1,3,0:T(8,128)S(1)}, f32[4,16,36,2]{2,1,3,0:T(8,128)S(1)}, u32[]{:S(2)}, u32[]{:S(2)}) collective-permute-start(f32[4,16,36,2]{2,1,3,0:T(8,128)S(1)} %get-tuple-element.19), channel_id=1, source_target_pairs={{1,0},{2,1},{3,2},{4,3},{5,4},{6,5},{7,6},{0,7},{9,8},{10,9},{11,1... | collective-permute-start | bytes 55304 | tf_op jit(solution)/shard_map/ppermute | solution.py:25
  242.7 13.4 %fusion.67 = (f32[4,16,32,128]{2,1,3,0:T(8,128)}, f32[4,16,32,128]{2,1,3,0:T(8,128)}) fusion(f32[4,16,2,128]{2,1,3,0:T(8,128)S(1)} %copy-done.23, f32[4,16,32,128]{2,1,3,0:T(8,128)S(1)} %copy-done.7, f32[4,16,2,128]{2,1,3,0:T(8,128)S(1)} %copy-done.18, f32[4,2,32,128]{2,1,3,0:T(2,128)} %get-tuple-element.80, f32[4,2,32,128]{2,1,3,0:T(2,128)} %get-tuple-element.79), kind=kLoop, calls=%fused_computation.154 | loop fusion | flops 4718592 | bytes 3538944 | tf_op jit(solution)/shard_map/div | solution.py:41
  256.1 5.8 %pad_maximum_fusion.2 = (f32[4,16,36,130]{2,1,3,0:T(8,128)S(1)}, f32[4,16,36,130]{2,1,3,0:T(8,128)}) fusion(f32[4,16,36,2]{2,1,3,0:T(8,128)S(1)} %collective-permute-done.10, f32[4,16,2,128]{2,1,3,0:T(8,128)S(1)} %copy-done.23, f32[4,16,32,128]{2,1,3,0:T(8,128)S(1)} %copy-done.7, f32[4,16,2,128]{2,1,3,0:T(8,128)S(1)} %copy-done.18, ...), kind=kLoop, calls=%fused_computation.64 | loop fusion | flops 1797120 | bytes 3612672 | tf_op jit(solution)/shard_map/concatenate | solution.py:26
  261.9 8.3 %fusion.64 = f32[4,16,32,128]{2,1,3,0:T(8,128)S(1)} fusion(f32[4,16,36,130]{2,1,3,0:T(8,128)} %get-tuple-element.18, f32[4,16,36,130]{2,1,3,0:T(8,128)S(1)} %get-tuple-element.17), kind=kLoop, calls=%fused_computation.149 | loop fusion | flops 1310720 | bytes 5242880 | tf_op jit(solution)/shard_map/div | solution.py:41
  273.4 16.4 %fusion.141 = f32[3,16,32,128]{2,1,3,0:T(8,128)} fusion(f32[4,16,2,128]{2,1,3,0:T(8,128)S(1)} %copy-done.18, f32[4,16,32,128]{2,1,3,0:T(8,128)S(1)} %copy-done.7, f32[4,16,2,128]{2,1,3,0:T(8,128)} %copy.324, f32[4,2,32,128]{2,1,3,0:T(2,128)S(1)} %copy-done.65, f32[4,2,32,128]{2,1,3,0:T(2,128)S(1)} %copy-done.64, f32[4,16,36,130]{2,1,3,0:T(8,128)} %get-tuple-element.18, ...), kind=kLoop, calls=%fused_computation.268 | loop fusion | flops 7864320 | bytes 21561856 | tf_op jit(solution)/shard_map/add | solution.py:35
  289.8 2.9 fusion.87
  294.7 4.7 fusion.269
  299.4 3.1 copy.331
  302.5 3.1 copy.329
  306.4 3.6 fusion.270
  312.2 2.9 copy.332
  319.3 6.0 %collective-permute-start.14 = (f32[4,16,36,2]{2,1,3,0:T(8,128)S(1)}, f32[4,16,36,2]{2,1,3,0:T(8,128)S(1)}, u32[]{:S(2)}, u32[]{:S(2)}) collective-permute-start(f32[4,16,36,2]{2,1,3,0:T(8,128)S(1)} %get-tuple-element.15), channel_id=1, source_target_pairs={{1,0},{2,1},{3,2},{4,3},{5,4},{6,5},{7,6},{0,7},{9,8},{10,9},{11,1... | collective-permute-start | bytes 55304 | tf_op jit(solution)/shard_map/ppermute | solution.py:25
  325.4 13.5 %fusion.61 = (f32[4,16,32,128]{2,1,3,0:T(8,128)}, f32[4,16,32,128]{2,1,3,0:T(8,128)}) fusion(f32[4,16,2,128]{2,1,3,0:T(8,128)S(1)} %copy-done.24, f32[4,16,32,128]{2,1,3,0:T(8,128)S(1)} %copy-done.1, f32[4,16,2,128]{2,1,3,0:T(8,128)S(1)} %copy-done.19, f32[4,2,32,128]{2,1,3,0:T(2,128)} %get-tuple-element.67, f32[4,2,32,128]{2,1,3,0:T(2,128)} %get-tuple-element.66), kind=kLoop, calls=%fused_computation.144 | loop fusion | flops 4718592 | bytes 3538944 | tf_op jit(solution)/shard_map/div | solution.py:41
  338.8 5.8 %pad_maximum_fusion.3 = (f32[4,16,36,130]{2,1,3,0:T(8,128)S(1)}, f32[4,16,36,130]{2,1,3,0:T(8,128)}) fusion(f32[4,16,36,2]{2,1,3,0:T(8,128)S(1)} %collective-permute-done.14, f32[4,16,2,128]{2,1,3,0:T(8,128)S(1)} %copy-done.24, f32[4,16,32,128]{2,1,3,0:T(8,128)S(1)} %copy-done.1, f32[4,16,2,128]{2,1,3,0:T(8,128)S(1)} %copy-done.19, ...), kind=kLoop, calls=%fused_computation.66 | loop fusion | flops 1797120 | bytes 3612672 | tf_op jit(solution)/shard_map/concatenate | solution.py:26
  344.7 8.3 %fusion.58 = f32[4,16,32,128]{2,1,3,0:T(8,128)S(1)} fusion(f32[4,16,36,130]{2,1,3,0:T(8,128)} %get-tuple-element.14, f32[4,16,36,130]{2,1,3,0:T(8,128)S(1)} %get-tuple-element.13), kind=kLoop, calls=%fused_computation.139 | loop fusion | flops 1310720 | bytes 5242880 | tf_op jit(solution)/shard_map/div | solution.py:41
  356.1 15.3 %fusion.129 = f32[3,16,32,128]{2,1,3,0:T(8,128)} fusion(f32[4,16,2,128]{2,1,3,0:T(8,128)S(1)} %copy-done.19, f32[4,16,32,128]{2,1,3,0:T(8,128)S(1)} %copy-done.1, f32[4,16,2,128]{2,1,3,0:T(8,128)S(1)} %copy-done.24, f32[4,2,32,128]{2,1,3,0:T(2,128)S(1)} %copy-done.67, f32[4,2,32,128]{2,1,3,0:T(2,128)S(1)} %copy-done.66, ...), kind=kLoop, calls=%fused_computation.256 | loop fusion | flops 7864320 | bytes 25690624 | tf_op jit(solution)/shard_map/add | solution.py:35
  375.8 4.6 fusion.266
  380.4 3.1 copy.337
  383.5 3.1 copy.335
  390.0 3.2 collective-permute-done.17
  400.3 6.0 %collective-permute-start.18 = (f32[4,16,36,2]{2,1,3,0:T(8,128)S(1)}, f32[4,16,36,2]{2,1,3,0:T(8,128)S(1)}, u32[]{:S(2)}, u32[]{:S(2)}) collective-permute-start(f32[4,16,36,2]{2,1,3,0:T(8,128)S(1)} %get-tuple-element.11), channel_id=1, source_target_pairs={{1,0},{2,1},{3,2},{4,3},{5,4},{6,5},{7,6},{0,7},{9,8},{10,9},{11,1... | collective-permute-start | bytes 55304 | tf_op jit(solution)/shard_map/ppermute | solution.py:25
  406.4 14.5 %fusion.55 = (f32[4,16,32,128]{2,1,3,0:T(8,128)}, f32[4,16,32,128]{2,1,3,0:T(8,128)}) fusion(f32[4,16,2,128]{2,1,3,0:T(8,128)} %copy.336, f32[4,16,32,128]{2,1,3,0:T(8,128)S(1)} %copy-done.11, f32[4,16,2,128]{2,1,3,0:T(8,128)S(1)} %copy-done.17, f32[4,2,32,128]{2,1,3,0:T(2,128)S(1)} %get-tuple-element.54, f32[4,2,32,128]{2,1,3,0:T(2,128)S(1)} %get-tuple-element.53), kind=kLoop, calls=%fused_computation.134 | loop fusion | flops 4718592 | bytes 3538944 | tf_op jit(solution)/shard_map/div | solution.py:41
  420.9 9.0 %pad_maximum_fusion.4 = (f32[4,16,36,130]{2,1,3,0:T(8,128)S(1)}, f32[4,16,36,130]{2,1,3,0:T(8,128)}) fusion(f32[4,16,36,2]{2,1,3,0:T(8,128)S(1)} %collective-permute-done.18, f32[4,16,2,128]{2,1,3,0:T(8,128)} %copy.336, f32[4,16,32,128]{2,1,3,0:T(8,128)S(1)} %copy-done.11, f32[4,16,2,128]{2,1,3,0:T(8,128)S(1)} %copy-done.17, ...), kind=kLoop, calls=%fused_computation.68 | loop fusion | flops 1797120 | bytes 3612672 | tf_op jit(solution)/shard_map/concatenate | solution.py:26
  429.8 8.3 %fusion.52 = f32[4,16,32,128]{2,1,3,0:T(8,128)S(1)} fusion(f32[4,16,36,130]{2,1,3,0:T(8,128)} %get-tuple-element.10, f32[4,16,36,130]{2,1,3,0:T(8,128)S(1)} %get-tuple-element.9), kind=kLoop, calls=%fused_computation.129 | loop fusion | flops 1310720 | bytes 5242880 | tf_op jit(solution)/shard_map/div | solution.py:41
  441.5 16.5 %fusion.117 = f32[3,16,32,128]{2,1,3,0:T(8,128)} fusion(f32[4,16,2,128]{2,1,3,0:T(8,128)S(1)} %copy-done.17, f32[4,16,32,128]{2,1,3,0:T(8,128)S(1)} %copy-done.11, f32[4,16,2,128]{2,1,3,0:T(8,128)} %copy.336, f32[4,2,32,128]{2,1,3,0:T(2,128)S(1)} %get-tuple-element.54, f32[4,2,32,128]{2,1,3,0:T(2,128)S(1)} %get-tuple-element.53, ...), kind=kLoop, calls=%fused_computation.244 | loop fusion | flops 7864320 | bytes 21561856 | tf_op jit(solution)/shard_map/add | solution.py:35
  458.0 4.0 fusion.91
  464.0 4.6 fusion.263
  468.6 3.1 copy.343
  471.7 3.1 copy.341
  475.4 3.6 fusion.264
  487.9 5.7 %collective-permute-start.22 = (f32[4,16,36,2]{2,1,3,0:T(8,128)S(1)}, f32[4,16,36,2]{2,1,3,0:T(8,128)S(1)}, u32[]{:S(2)}, u32[]{:S(2)}) collective-permute-start(f32[4,16,36,2]{2,1,3,0:T(8,128)S(1)} %get-tuple-element.7), channel_id=1, source_target_pairs={{1,0},{2,1},{3,2},{4,3},{5,4},{6,5},{7,6},{0,7},{9,8},{10,9},{11,1... | collective-permute-start | bytes 55304 | tf_op jit(solution)/shard_map/ppermute | solution.py:25
  493.6 13.2 %fusion.49 = (f32[4,16,32,128]{2,1,3,0:T(8,128)}, f32[4,16,32,128]{2,1,3,0:T(8,128)}) fusion(f32[4,16,2,128]{2,1,3,0:T(8,128)S(1)} %copy-done.21, f32[4,16,32,128]{2,1,3,0:T(8,128)S(1)} %copy-done.5, f32[4,16,2,128]{2,1,3,0:T(8,128)S(1)} %copy-done.15, f32[4,2,32,128]{2,1,3,0:T(2,128)} %get-tuple-element.41, f32[4,2,32,128]{2,1,3,0:T(2,128)} %get-tuple-element.40), kind=kLoop, calls=%fused_computation.124 | loop fusion | flops 4718592 | bytes 3538944 | tf_op jit(solution)/shard_map/div | solution.py:41
  506.8 5.8 %pad_maximum_fusion.5 = (f32[4,16,36,130]{2,1,3,0:T(8,128)S(1)}, f32[4,16,36,130]{2,1,3,0:T(8,128)}) fusion(f32[4,16,36,2]{2,1,3,0:T(8,128)S(1)} %collective-permute-done.22, f32[4,16,2,128]{2,1,3,0:T(8,128)S(1)} %copy-done.21, f32[4,16,32,128]{2,1,3,0:T(8,128)S(1)} %copy-done.5, f32[4,16,2,128]{2,1,3,0:T(8,128)S(1)} %copy-done.15, ...), kind=kLoop, calls=%fused_computation.70 | loop fusion | flops 1797120 | bytes 3612672 | tf_op jit(solution)/shard_map/concatenate | solution.py:26
  512.7 8.3 %fusion.46 = f32[4,16,32,128]{2,1,3,0:T(8,128)S(1)} fusion(f32[4,16,36,130]{2,1,3,0:T(8,128)} %get-tuple-element.6, f32[4,16,36,130]{2,1,3,0:T(8,128)S(1)} %get-tuple-element.5), kind=kLoop, calls=%fused_computation.119 | loop fusion | flops 1310720 | bytes 5242880 | tf_op jit(solution)/shard_map/div | solution.py:41
  524.1 16.2 %fusion.105 = f32[3,16,32,128]{2,1,3,0:T(8,128)} fusion(f32[4,16,2,128]{2,1,3,0:T(8,128)S(1)} %copy-done.15, f32[4,16,32,128]{2,1,3,0:T(8,128)S(1)} %copy-done.5, f32[4,16,2,128]{2,1,3,0:T(8,128)} %copy.342, f32[4,2,32,128]{2,1,3,0:T(2,128)S(1)} %copy-done.61, f32[4,2,32,128]{2,1,3,0:T(2,128)S(1)} %copy-done.60, f32[4,16,36,130]{2,1,3,0:T(8,128)} %get-tuple-element.6, ...), kind=kLoop, calls=%fused_computation.232 | loop fusion | flops 7864320 | bytes 21561856 | tf_op jit(solution)/shard_map/add | solution.py:35
  540.4 4.9 fusion.94
  545.3 3.8 copy.347
  (230 shorter events, 115.9 us)
Async XLA Ops:
  1.7 59.3 %collective-permute-start = (f32[4,16,2,128]{3,1,2,0:T(8,128)}, f32[4,16,2,128]{3,1,2,0:T(8,128)S(1)}, u32[]{:S(2)}, u32[]{:S(2)}) collective-permute-start(f32[4,16,2,128]{3,1,2,0:T(8,128)} %copy.348), channel_id=1, source_target_pairs={{8,0},{16,8},{24,16},{32,24},{40,32},{48,40},{56,48},{64,56},{72,6... | collective-permute-start | bytes 196616 | tf_op jit(solution)/shard_map/ppermute | solution.py:25
  5.8 52.3 %collective-permute-start.1 = (f32[4,16,2,128]{3,1,2,0:T(8,128)}, f32[4,16,2,128]{3,1,2,0:T(8,128)S(1)}, u32[]{:S(2)}, u32[]{:S(2)}) collective-permute-start(f32[4,16,2,128]{3,1,2,0:T(8,128)} %copy.349), channel_id=1, source_target_pairs={{0,8},{8,16},{16,24},{24,32},{32,40},{40,48},{48,56},{56,64},{64,7... | collective-permute-start | bytes 196616 | tf_op jit(solution)/shard_map/ppermute | solution.py:22
  27.0 9.0 %copy-start.55 = (f32[4,16,32,128]{3,2,1,0:T(8,128)S(1)}, f32[4,16,32,128]{3,2,1,0:T(8,128)}, u32[]{:S(2)}) copy-start(f32[4,16,32,128]{3,2,1,0:T(8,128)} %param.8) | copy-start | bytes 3145732
  37.5 8.2 %copy-start.70 = (f32[16,32,128]{2,1,0:T(8,128)S(1)}, f32[16,32,128]{2,1,0:T(8,128)}, u32[]{:S(2)}) copy-start(f32[16,32,128]{2,1,0:T(8,128)} %get-tuple-element.108) | copy-start | bytes 786436
  40.9 58.0 %copy-start.31 = (f32[16,32,128]{1,0,2:T(8,128)}, f32[16,32,128]{1,0,2:T(8,128)S(1)}, u32[]{:S(2)}) copy-start(f32[16,32,128]{1,0,2:T(8,128)S(1)} %copy.315) | copy-start | bytes 786436
  63.9 7.7 %copy-start.12 = (f32[4,16,32,128]{2,1,3,0:T(8,128)S(1)}, f32[4,16,32,128]{2,1,3,0:T(8,128)}, u32[]{:S(2)}) copy-start(f32[4,16,32,128]{2,1,3,0:T(8,128)} %copy.292) | copy-start | bytes 3145732
  63.9 7.7 %copy-start.20 = (f32[4,16,2,128]{2,1,3,0:T(8,128)S(1)}, f32[4,16,2,128]{2,1,3,0:T(8,128)}, u32[]{:S(2)}) copy-start(f32[4,16,2,128]{2,1,3,0:T(8,128)} %copy.299) | copy-start | bytes 196612
  63.9 7.8 %copy-start.25 = (f32[4,16,2,128]{2,1,3,0:T(8,128)S(1)}, f32[4,16,2,128]{2,1,3,0:T(8,128)}, u32[]{:S(2)}) copy-start(f32[4,16,2,128]{2,1,3,0:T(8,128)} %copy.297) | copy-start | bytes 196612
  65.2 15.6 %collective-permute-start.2 = (f32[4,16,36,2]{2,1,3,0:T(8,128)S(1)}, f32[4,16,36,2]{2,1,3,0:T(8,128)S(1)}, u32[]{:S(2)}, u32[]{:S(2)}) collective-permute-start(f32[4,16,36,2]{2,1,3,0:T(8,128)S(1)} %get-tuple-element.27), channel_id=1, source_target_pairs={{1,0},{2,1},{3,2},{4,3},{5,4},{6,5},{7,6},{0,7},{9,8},{10,9},{11,1... | collective-permute-start | bytes 55304 | tf_op jit(solution)/shard_map/ppermute | solution.py:25
  71.5 9.3 %collective-permute-start.3 = (f32[4,16,36,2]{2,1,3,0:T(8,128)S(1)}, f32[4,16,36,2]{2,1,3,0:T(8,128)S(1)}, u32[]{:S(2)}, u32[]{:S(2)}) collective-permute-start(f32[4,16,36,2]{2,1,3,0:T(8,128)S(1)} %get-tuple-element.28), channel_id=1, source_target_pairs={{0,1},{1,2},{2,3},{3,4},{4,5},{5,6},{6,7},{7,0},{8,9},{9,10},{10,1... | collective-permute-start | bytes 55304 | tf_op jit(solution)/shard_map/ppermute | solution.py:22
  87.4 8.5 %copy-start.37 = (f32[4,16,32,128]{2,1,3,0:T(8,128)S(1)}, f32[4,16,32,128]{2,1,3,0:T(8,128)}, u32[]{:S(2)}) copy-start(f32[4,16,32,128]{2,1,3,0:T(8,128)} %subtract_multiply_fusion) | copy-start | bytes 3145732
  87.4 8.5 %copy-start.39 = (f32[4,16,32,128]{2,1,3,0:T(8,128)S(1)}, f32[4,16,32,128]{2,1,3,0:T(8,128)}, u32[]{:S(2)}) copy-start(f32[4,16,32,128]{2,1,3,0:T(8,128)} %fusion.79) | copy-start | bytes 3145732
  98.9 22.0 %copy-start.56 = (f32[1,16,32,128]{2,1,3,0:T(8,128)}, f32[1,16,32,128]{2,1,3,0:T(8,128)S(1)}, u32[]{:S(2)}) copy-start(f32[1,16,32,128]{2,1,3,0:T(8,128)S(1)} %get-tuple-element.95) | copy-start | bytes 786436
  136.4 11.7 %collective-permute-start.4 = (f32[4,16,2,128]{3,1,2,0:T(8,128)S(1)}, f32[4,16,2,128]{3,1,2,0:T(8,128)S(1)}, u32[]{:S(2)}, u32[]{:S(2)}) collective-permute-start(f32[4,16,2,128]{3,1,2,0:T(8,128)S(1)} %copy.317), channel_id=1, source_target_pairs={{8,0},{16,8},{24,16},{32,24},{40,32},{48,40},{56,48},{64,56},{72,6... | collective-permute-start | bytes 196616 | tf_op jit(solution)/shard_map/ppermute | solution.py:25
  139.4 5.8 %collective-permute-start.5 = (f32[4,16,2,128]{3,1,2,0:T(8,128)S(1)}, f32[4,16,2,128]{3,1,2,0:T(8,128)S(1)}, u32[]{:S(2)}, u32[]{:S(2)}) collective-permute-start(f32[4,16,2,128]{3,1,2,0:T(8,128)S(1)} %copy.319), channel_id=1, source_target_pairs={{0,8},{8,16},{16,24},{24,32},{32,40},{40,48},{48,56},{56,64},{64,7... | collective-permute-start | bytes 196616 | tf_op jit(solution)/shard_map/ppermute | solution.py:22
  151.0 7.3 %copy-start.22 = (f32[4,16,2,128]{2,1,3,0:T(8,128)S(1)}, f32[4,16,2,128]{2,1,3,0:T(8,128)}, u32[]{:S(2)}) copy-start(f32[4,16,2,128]{2,1,3,0:T(8,128)} %copy.318) | copy-start | bytes 196612
  152.3 19.5 %collective-permute-start.6 = (f32[4,16,36,2]{2,1,3,0:T(8,128)S(1)}, f32[4,16,36,2]{2,1,3,0:T(8,128)S(1)}, u32[]{:S(2)}, u32[]{:S(2)}) collective-permute-start(f32[4,16,36,2]{2,1,3,0:T(8,128)S(1)} %get-tuple-element.23), channel_id=1, source_target_pairs={{1,0},{2,1},{3,2},{4,3},{5,4},{6,5},{7,6},{0,7},{9,8},{10,9},{11,1... | collective-permute-start | bytes 55304 | tf_op jit(solution)/shard_map/ppermute | solution.py:25
  158.3 13.5 %collective-permute-start.7 = (f32[4,16,36,2]{2,1,3,0:T(8,128)S(1)}, f32[4,16,36,2]{2,1,3,0:T(8,128)S(1)}, u32[]{:S(2)}, u32[]{:S(2)}) collective-permute-start(f32[4,16,36,2]{2,1,3,0:T(8,128)S(1)} %get-tuple-element.24), channel_id=1, source_target_pairs={{0,1},{1,2},{2,3},{3,4},{4,5},{5,6},{6,7},{7,0},{8,9},{9,10},{10,1... | collective-permute-start | bytes 55304 | tf_op jit(solution)/shard_map/ppermute | solution.py:22
  177.6 8.3 %copy-start.27 = (f32[4,16,36,130]{2,1,3,0:T(8,128)}, f32[4,16,36,130]{2,1,3,0:T(8,128)S(1)}, u32[]{:S(2)}) copy-start(f32[4,16,36,130]{2,1,3,0:T(8,128)S(1)} %get-tuple-element.21) | copy-start | bytes 3594244
  177.6 8.3 %copy-start.47 = (f32[4,16,32,128]{2,1,3,0:T(8,128)S(1)}, f32[4,16,32,128]{2,1,3,0:T(8,128)}, u32[]{:S(2)}) copy-start(f32[4,16,32,128]{2,1,3,0:T(8,128)} %get-tuple-element.88) | copy-start | bytes 3145732
  177.6 8.3 %copy-start.48 = (f32[4,16,32,128]{2,1,3,0:T(8,128)S(1)}, f32[4,16,32,128]{2,1,3,0:T(8,128)}, u32[]{:S(2)}) copy-start(f32[4,16,32,128]{2,1,3,0:T(8,128)} %get-tuple-element.89) | copy-start | bytes 3145732
  189.4 16.5 %copy-start.13 = (f32[4,16,32,128]{2,1,3,0:T(8,128)S(1)}, f32[4,16,32,128]{2,1,3,0:T(8,128)}, u32[]{:S(2)}) copy-start(f32[4,16,32,128]{2,1,3,0:T(8,128)} %copy.292) | copy-start | bytes 3145732
  189.4 16.5 %copy-start.57 = (f32[1,16,32,128]{2,1,3,0:T(8,128)S(1)}, f32[1,16,32,128]{2,1,3,0:T(8,128)}, u32[]{:S(2)}) copy-start(f32[1,16,32,128]{2,1,3,0:T(8,128)} %copy-done.56) | copy-start | bytes 786436
  223.0 9.5 %collective-permute-start.8 = (f32[4,16,2,128]{3,1,2,0:T(8,128)S(1)}, f32[4,16,2,128]{3,1,2,0:T(8,128)S(1)}, u32[]{:S(2)}, u32[]{:S(2)}) collective-permute-start(f32[4,16,2,128]{3,1,2,0:T(8,128)S(1)} %copy.323), channel_id=1, source_target_pairs={{8,0},{16,8},{24,16},{32,24},{40,32},{48,40},{56,48},{64,56},{72,6... | collective-permute-start | bytes 196616 | tf_op jit(solution)/shard_map/ppermute | solution.py:25
  223.8 5.8 %collective-permute-start.9 = (f32[4,16,2,128]{3,1,2,0:T(8,128)S(1)}, f32[4,16,2,128]{3,1,2,0:T(8,128)S(1)}, u32[]{:S(2)}, u32[]{:S(2)}) collective-permute-start(f32[4,16,2,128]{3,1,2,0:T(8,128)S(1)} %copy.325), channel_id=1, source_target_pairs={{0,8},{8,16},{16,24},{24,32},{32,40},{40,48},{48,56},{56,64},{64,7... | collective-permute-start | bytes 196616 | tf_op jit(solution)/shard_map/ppermute | solution.py:22
  235.4 7.3 %copy-start.7 = (f32[4,16,32,128]{2,1,3,0:T(8,128)S(1)}, f32[4,16,32,128]{2,1,3,0:T(8,128)}, u32[]{:S(2)}) copy-start(f32[4,16,32,128]{2,1,3,0:T(8,128)} %copy-done.6) | copy-start | bytes 3145732
  235.4 7.3 %copy-start.18 = (f32[4,16,2,128]{2,1,3,0:T(8,128)S(1)}, f32[4,16,2,128]{2,1,3,0:T(8,128)}, u32[]{:S(2)}) copy-start(f32[4,16,2,128]{2,1,3,0:T(8,128)} %copy.326) | copy-start | bytes 196612
  235.4 7.3 %copy-start.23 = (f32[4,16,2,128]{2,1,3,0:T(8,128)S(1)}, f32[4,16,2,128]{2,1,3,0:T(8,128)}, u32[]{:S(2)}) copy-start(f32[4,16,2,128]{2,1,3,0:T(8,128)} %copy.324) | copy-start | bytes 196612
  236.7 19.4 %collective-permute-start.10 = (f32[4,16,36,2]{2,1,3,0:T(8,128)S(1)}, f32[4,16,36,2]{2,1,3,0:T(8,128)S(1)}, u32[]{:S(2)}, u32[]{:S(2)}) collective-permute-start(f32[4,16,36,2]{2,1,3,0:T(8,128)S(1)} %get-tuple-element.19), channel_id=1, source_target_pairs={{1,0},{2,1},{3,2},{4,3},{5,4},{6,5},{7,6},{0,7},{9,8},{10,9},{11,1... | collective-permute-start | bytes 55304 | tf_op jit(solution)/shard_map/ppermute | solution.py:25
  242.7 13.4 %collective-permute-start.11 = (f32[4,16,36,2]{2,1,3,0:T(8,128)S(1)}, f32[4,16,36,2]{2,1,3,0:T(8,128)S(1)}, u32[]{:S(2)}, u32[]{:S(2)}) collective-permute-start(f32[4,16,36,2]{2,1,3,0:T(8,128)S(1)} %get-tuple-element.20), channel_id=1, source_target_pairs={{0,1},{1,2},{2,3},{3,4},{4,5},{5,6},{6,7},{7,0},{8,9},{9,10},{10,1... | collective-permute-start | bytes 55304 | tf_op jit(solution)/shard_map/ppermute | solution.py:22
  261.9 8.3 %copy-start.29 = (f32[4,16,36,130]{2,1,3,0:T(8,128)}, f32[4,16,36,130]{2,1,3,0:T(8,128)S(1)}, u32[]{:S(2)}) copy-start(f32[4,16,36,130]{2,1,3,0:T(8,128)S(1)} %get-tuple-element.17) | copy-start | bytes 3594244
  261.9 8.3 %copy-start.51 = (f32[4,16,32,128]{2,1,3,0:T(8,128)S(1)}, f32[4,16,32,128]{2,1,3,0:T(8,128)}, u32[]{:S(2)}) copy-start(f32[4,16,32,128]{2,1,3,0:T(8,128)} %get-tuple-element.75) | copy-start | bytes 3145732
  261.9 8.3 %copy-start.52 = (f32[4,16,32,128]{2,1,3,0:T(8,128)S(1)}, f32[4,16,32,128]{2,1,3,0:T(8,128)}, u32[]{:S(2)}) copy-start(f32[4,16,32,128]{2,1,3,0:T(8,128)} %get-tuple-element.76) | copy-start | bytes 3145732
  273.4 16.4 %copy-start.14 = (f32[4,16,32,128]{2,1,3,0:T(8,128)S(1)}, f32[4,16,32,128]{2,1,3,0:T(8,128)}, u32[]{:S(2)}) copy-start(f32[4,16,32,128]{2,1,3,0:T(8,128)} %copy.292) | copy-start | bytes 3145732
  305.6 9.5 %collective-permute-start.12 = (f32[4,16,2,128]{3,1,2,0:T(8,128)S(1)}, f32[4,16,2,128]{3,1,2,0:T(8,128)S(1)}, u32[]{:S(2)}, u32[]{:S(2)}) collective-permute-start(f32[4,16,2,128]{3,1,2,0:T(8,128)S(1)} %copy.329), channel_id=1, source_target_pairs={{8,0},{16,8},{24,16},{32,24},{40,32},{48,40},{56,48},{64,56},{72,6... | collective-permute-start | bytes 196616 | tf_op jit(solution)/shard_map/ppermute | solution.py:25
  306.4 5.8 %collective-permute-start.13 = (f32[4,16,2,128]{3,1,2,0:T(8,128)S(1)}, f32[4,16,2,128]{3,1,2,0:T(8,128)S(1)}, u32[]{:S(2)}, u32[]{:S(2)}) collective-permute-start(f32[4,16,2,128]{3,1,2,0:T(8,128)S(1)} %copy.331), channel_id=1, source_target_pairs={{0,8},{8,16},{16,24},{24,32},{32,40},{40,48},{48,56},{56,64},{64,7... | collective-permute-start | bytes 196616 | tf_op jit(solution)/shard_map/ppermute | solution.py:22
  318.0 7.3 %copy-start.1 = (f32[4,16,32,128]{2,1,3,0:T(8,128)S(1)}, f32[4,16,32,128]{2,1,3,0:T(8,128)}, u32[]{:S(2)}) copy-start(f32[4,16,32,128]{2,1,3,0:T(8,128)} %copy-done) | copy-start | bytes 3145732
  318.0 7.3 %copy-start.19 = (f32[4,16,2,128]{2,1,3,0:T(8,128)S(1)}, f32[4,16,2,128]{2,1,3,0:T(8,128)}, u32[]{:S(2)}) copy-start(f32[4,16,2,128]{2,1,3,0:T(8,128)} %copy.332) | copy-start | bytes 196612
  318.0 7.3 %copy-start.24 = (f32[4,16,2,128]{2,1,3,0:T(8,128)S(1)}, f32[4,16,2,128]{2,1,3,0:T(8,128)}, u32[]{:S(2)}) copy-start(f32[4,16,2,128]{2,1,3,0:T(8,128)} %copy.330) | copy-start | bytes 196612
  319.3 19.5 %collective-permute-start.14 = (f32[4,16,36,2]{2,1,3,0:T(8,128)S(1)}, f32[4,16,36,2]{2,1,3,0:T(8,128)S(1)}, u32[]{:S(2)}, u32[]{:S(2)}) collective-permute-start(f32[4,16,36,2]{2,1,3,0:T(8,128)S(1)} %get-tuple-element.15), channel_id=1, source_target_pairs={{1,0},{2,1},{3,2},{4,3},{5,4},{6,5},{7,6},{0,7},{9,8},{10,9},{11,1... | collective-permute-start | bytes 55304 | tf_op jit(solution)/shard_map/ppermute | solution.py:25
  325.3 13.5 %collective-permute-start.15 = (f32[4,16,36,2]{2,1,3,0:T(8,128)S(1)}, f32[4,16,36,2]{2,1,3,0:T(8,128)S(1)}, u32[]{:S(2)}, u32[]{:S(2)}) collective-permute-start(f32[4,16,36,2]{2,1,3,0:T(8,128)S(1)} %get-tuple-element.16), channel_id=1, source_target_pairs={{0,1},{1,2},{2,3},{3,4},{4,5},{5,6},{6,7},{7,0},{8,9},{9,10},{10,1... | collective-permute-start | bytes 55304 | tf_op jit(solution)/shard_map/ppermute | solution.py:22
  344.7 8.3 %copy-start.30 = (f32[4,16,36,130]{2,1,3,0:T(8,128)}, f32[4,16,36,130]{2,1,3,0:T(8,128)S(1)}, u32[]{:S(2)}) copy-start(f32[4,16,36,130]{2,1,3,0:T(8,128)S(1)} %get-tuple-element.13) | copy-start | bytes 3594244
  344.7 8.3 %copy-start.53 = (f32[4,16,32,128]{2,1,3,0:T(8,128)S(1)}, f32[4,16,32,128]{2,1,3,0:T(8,128)}, u32[]{:S(2)}) copy-start(f32[4,16,32,128]{2,1,3,0:T(8,128)} %get-tuple-element.62) | copy-start | bytes 3145732
  344.7 8.3 %copy-start.54 = (f32[4,16,32,128]{2,1,3,0:T(8,128)S(1)}, f32[4,16,32,128]{2,1,3,0:T(8,128)}, u32[]{:S(2)}) copy-start(f32[4,16,32,128]{2,1,3,0:T(8,128)} %get-tuple-element.63) | copy-start | bytes 3145732
  356.1 15.3 %copy-start.58 = (f32[1,16,32,128]{2,1,3,0:T(8,128)}, f32[1,16,32,128]{2,1,3,0:T(8,128)S(1)}, u32[]{:S(2)}) copy-start(f32[1,16,32,128]{2,1,3,0:T(8,128)S(1)} %get-tuple-element.59) | copy-start | bytes 786436
  386.6 9.6 %collective-permute-start.16 = (f32[4,16,2,128]{3,1,2,0:T(8,128)S(1)}, f32[4,16,2,128]{3,1,2,0:T(8,128)S(1)}, u32[]{:S(2)}, u32[]{:S(2)}) collective-permute-start(f32[4,16,2,128]{3,1,2,0:T(8,128)S(1)} %copy.335), channel_id=1, source_target_pairs={{8,0},{16,8},{24,16},{32,24},{40,32},{48,40},{56,48},{64,56},{72,6... | collective-permute-start | bytes 196616 | tf_op jit(solution)/shard_map/ppermute | solution.py:25
  387.5 5.8 %collective-permute-start.17 = (f32[4,16,2,128]{3,1,2,0:T(8,128)S(1)}, f32[4,16,2,128]{3,1,2,0:T(8,128)S(1)}, u32[]{:S(2)}, u32[]{:S(2)}) collective-permute-start(f32[4,16,2,128]{3,1,2,0:T(8,128)S(1)} %copy.337), channel_id=1, source_target_pairs={{0,8},{8,16},{16,24},{24,32},{32,40},{40,48},{48,56},{56,64},{64,7... | collective-permute-start | bytes 196616 | tf_op jit(solution)/shard_map/ppermute | solution.py:22
  399.0 7.3 %copy-start.11 = (f32[4,16,32,128]{2,1,3,0:T(8,128)S(1)}, f32[4,16,32,128]{2,1,3,0:T(8,128)}, u32[]{:S(2)}) copy-start(f32[4,16,32,128]{2,1,3,0:T(8,128)} %copy-done.10) | copy-start | bytes 3145732
  399.0 7.3 %copy-start.17 = (f32[4,16,2,128]{2,1,3,0:T(8,128)S(1)}, f32[4,16,2,128]{2,1,3,0:T(8,128)}, u32[]{:S(2)}) copy-start(f32[4,16,2,128]{2,1,3,0:T(8,128)} %copy.338) | copy-start | bytes 196612
  400.3 20.5 %collective-permute-start.18 = (f32[4,16,36,2]{2,1,3,0:T(8,128)S(1)}, f32[4,16,36,2]{2,1,3,0:T(8,128)S(1)}, u32[]{:S(2)}, u32[]{:S(2)}) collective-permute-start(f32[4,16,36,2]{2,1,3,0:T(8,128)S(1)} %get-tuple-element.11), channel_id=1, source_target_pairs={{1,0},{2,1},{3,2},{4,3},{5,4},{6,5},{7,6},{0,7},{9,8},{10,9},{11,1... | collective-permute-start | bytes 55304 | tf_op jit(solution)/shard_map/ppermute | solution.py:25
  406.4 14.5 %collective-permute-start.19 = (f32[4,16,36,2]{2,1,3,0:T(8,128)S(1)}, f32[4,16,36,2]{2,1,3,0:T(8,128)S(1)}, u32[]{:S(2)}, u32[]{:S(2)}) collective-permute-start(f32[4,16,36,2]{2,1,3,0:T(8,128)S(1)} %get-tuple-element.12), channel_id=1, source_target_pairs={{0,1},{1,2},{2,3},{3,4},{4,5},{5,6},{6,7},{7,0},{8,9},{9,10},{10,1... | collective-permute-start | bytes 55304 | tf_op jit(solution)/shard_map/ppermute | solution.py:22
  429.8 8.3 %copy-start.28 = (f32[4,16,36,130]{2,1,3,0:T(8,128)}, f32[4,16,36,130]{2,1,3,0:T(8,128)S(1)}, u32[]{:S(2)}) copy-start(f32[4,16,36,130]{2,1,3,0:T(8,128)S(1)} %get-tuple-element.9) | copy-start | bytes 3594244
  429.8 8.3 %copy-start.49 = (f32[4,16,32,128]{2,1,3,0:T(8,128)S(1)}, f32[4,16,32,128]{2,1,3,0:T(8,128)}, u32[]{:S(2)}) copy-start(f32[4,16,32,128]{2,1,3,0:T(8,128)} %get-tuple-element.49) | copy-start | bytes 3145732
  429.8 8.3 %copy-start.50 = (f32[4,16,32,128]{2,1,3,0:T(8,128)S(1)}, f32[4,16,32,128]{2,1,3,0:T(8,128)}, u32[]{:S(2)}) copy-start(f32[4,16,32,128]{2,1,3,0:T(8,128)} %get-tuple-element.50) | copy-start | bytes 3145732
  441.5 16.5 %copy-start.2 = (f32[4,16,32,128]{2,1,3,0:T(8,128)S(1)}, f32[4,16,32,128]{2,1,3,0:T(8,128)}, u32[]{:S(2)}) copy-start(f32[4,16,32,128]{2,1,3,0:T(8,128)} %copy-done) | copy-start | bytes 3145732
  441.5 16.5 %copy-start.59 = (f32[1,16,32,128]{2,1,3,0:T(8,128)S(1)}, f32[1,16,32,128]{2,1,3,0:T(8,128)}, u32[]{:S(2)}) copy-start(f32[1,16,32,128]{2,1,3,0:T(8,128)} %copy-done.58) | copy-start | bytes 786436
  474.8 8.8 %collective-permute-start.20 = (f32[4,16,2,128]{3,1,2,0:T(8,128)S(1)}, f32[4,16,2,128]{3,1,2,0:T(8,128)S(1)}, u32[]{:S(2)}, u32[]{:S(2)}) collective-permute-start(f32[4,16,2,128]{3,1,2,0:T(8,128)S(1)} %copy.341), channel_id=1, source_target_pairs={{8,0},{16,8},{24,16},{32,24},{40,32},{48,40},{56,48},{64,56},{72,6... | collective-permute-start | bytes 196616 | tf_op jit(solution)/shard_map/ppermute | solution.py:25
  474.9 5.9 %collective-permute-start.21 = (f32[4,16,2,128]{3,1,2,0:T(8,128)S(1)}, f32[4,16,2,128]{3,1,2,0:T(8,128)S(1)}, u32[]{:S(2)}, u32[]{:S(2)}) collective-permute-start(f32[4,16,2,128]{3,1,2,0:T(8,128)S(1)} %copy.343), channel_id=1, source_target_pairs={{0,8},{8,16},{16,24},{24,32},{32,40},{40,48},{48,56},{56,64},{64,7... | collective-permute-start | bytes 196616 | tf_op jit(solution)/shard_map/ppermute | solution.py:22
  487.9 18.9 %collective-permute-start.22 = (f32[4,16,36,2]{2,1,3,0:T(8,128)S(1)}, f32[4,16,36,2]{2,1,3,0:T(8,128)S(1)}, u32[]{:S(2)}, u32[]{:S(2)}) collective-permute-start(f32[4,16,36,2]{2,1,3,0:T(8,128)S(1)} %get-tuple-element.7), channel_id=1, source_target_pairs={{1,0},{2,1},{3,2},{4,3},{5,4},{6,5},{7,6},{0,7},{9,8},{10,9},{11,1... | collective-permute-start | bytes 55304 | tf_op jit(solution)/shard_map/ppermute | solution.py:25
  493.6 13.2 %collective-permute-start.23 = (f32[4,16,36,2]{2,1,3,0:T(8,128)S(1)}, f32[4,16,36,2]{2,1,3,0:T(8,128)S(1)}, u32[]{:S(2)}, u32[]{:S(2)}) collective-permute-start(f32[4,16,36,2]{2,1,3,0:T(8,128)S(1)} %get-tuple-element.8), channel_id=1, source_target_pairs={{0,1},{1,2},{2,3},{3,4},{4,5},{5,6},{6,7},{7,0},{8,9},{9,10},{10,1... | collective-permute-start | bytes 55304 | tf_op jit(solution)/shard_map/ppermute | solution.py:22
  512.6 8.3 %copy-start.26 = (f32[4,16,36,130]{2,1,3,0:T(8,128)}, f32[4,16,36,130]{2,1,3,0:T(8,128)S(1)}, u32[]{:S(2)}) copy-start(f32[4,16,36,130]{2,1,3,0:T(8,128)S(1)} %get-tuple-element.5) | copy-start | bytes 3594244
  512.7 8.3 %copy-start.45 = (f32[4,16,32,128]{2,1,3,0:T(8,128)S(1)}, f32[4,16,32,128]{2,1,3,0:T(8,128)}, u32[]{:S(2)}) copy-start(f32[4,16,32,128]{2,1,3,0:T(8,128)} %get-tuple-element.36) | copy-start | bytes 3145732
  512.7 8.3 %copy-start.46 = (f32[4,16,32,128]{2,1,3,0:T(8,128)S(1)}, f32[4,16,32,128]{2,1,3,0:T(8,128)}, u32[]{:S(2)}) copy-start(f32[4,16,32,128]{2,1,3,0:T(8,128)} %get-tuple-element.37) | copy-start | bytes 3145732
  524.1 16.2 %copy-start.3 = (f32[4,16,32,128]{2,1,3,0:T(8,128)S(1)}, f32[4,16,32,128]{2,1,3,0:T(8,128)}, u32[]{:S(2)}) copy-start(f32[4,16,32,128]{2,1,3,0:T(8,128)} %copy-done) | copy-start | bytes 3145732
  (32 other events, 142.8 us)
where the time goes:
time: 558 us; the launch traced here: 550 us
  other arithmetic  326 us (58%)
  local copies, waits for them, and re-layouts  165 us (30%)
  starting transfers between devices  45.7 us (8%)
  waiting for transfers between devices  11.7 us (2%)
    div x13, other arithmetic, first_pair(): return (8.0 * (plus_one - minus_one) - (plus_two - minus_two)) / 12.0  136 us
    add x6, other arithmetic, combine(): -advect - pressure_grad + viscosity * laplace - penalty * solid * speed  103 us
    ppermute x12, starting transfers between devices, padded_2(): lax.ppermute(lax.slice_in_dim(block, 0, width, axis=dim), axis, backward)  45 us
    slice x11, local copies, waits for them, and re-layouts, padded_2(): lax.slice_in_dim(block, block.shape[dim] - width, None, axis=dim)  39.8 us
    concatenate x6, other arithmetic, padded_2(): block = jnp.concatenate([low, block, high], axis=dim)  39 us
    unnamed x155, local copies, waits for them, and re-layouts  35.1 us
    ppermute x6, local copies, waits for them, and re-layouts, padded_2(): lax.ppermute(lax.slice_in_dim(block, block.shape[dim] - width, None, axis...  17.4 us
    ppermute x6, local copies, waits for them, and re-layouts, padded_2(): lax.ppermute(lax.slice_in_dim(block, 0, width, axis=dim), axis, backward)  17.3 us
  transfers between devices with their start and end apart: 24, of which 5 were waited for; matrix products, arithmetic and copies ran while one was open for 30% of the time, Pallas kernels for 0%

commit v1 on v0

v1 whole, which is shorter than its diff:
```python
import jax
import jax.numpy as jnp
from jax import lax
from jax.sharding import PartitionSpec as P
from jax.experimental import pallas as pl
from jax.experimental.pallas import tpu as pltpu

STAGES = 6
DEPTH = 2 * STAGES
viscosity = 0.05
penalty = 10.0
forcing = 0.5
sound_sq = 2.25
time_step = 0.2

NF, NZ, NX, NY = 4, 16, 32, 128
ROWS = 64
OWN = 16
TOP = OWN - DEPTH
BOTTOM = OWN + NX
F32 = jnp.float32


def lanes(shape):
    return lax.broadcasted_iota(jnp.int32, shape, len(shape) - 1)


def pack_kernel(par_ref, q_ref, m_ref, xa_ref, xb_ref, ya_ref, yb_ref):
    px = par_ref[0]
    py = par_ref[1]

    def rows_to(dst, start):
        dst[0:NF] = q_ref[:, :, start:start + DEPTH, :]
        dst[NF] = m_ref[:, start:start + DEPTH, :].astype(F32)

    @pl.when(px == 0)
    def _():
        rows_to(xa_ref, NX - DEPTH)
        rows_to(xb_ref, 0)

    @pl.when(px == 1)
    def _():
        rows_to(xa_ref, 0)
        rows_to(xb_ref, NX - DEPTH)

    lane = lanes((NX, NY))
    group = lane // 32
    low = lane % 32 < 16
    even = py == 0

    def field(f, load):
        def packed(zi):
            out = pltpu.roll(load(zi), 16, 1)
            for zq in range(1, 4):
                out = jnp.where(group == zq, pltpu.roll(load(4 * zq + zi), (16 + 32 * zq) % NY, 1), out)
            return out
        for h in range(2):
            first, second = packed(h), packed(h + 2)
            right = jnp.where(low, first, pltpu.roll(second, 16, 1))
            left = jnp.where(low, pltpu.roll(second, NY - 16, 1), first)
            ya_ref[f, h] = jnp.where(even, right, left)
            yb_ref[f, h] = jnp.where(even, left, right)

    for f in range(NF):
        field(f, lambda z, f=f: q_ref[f, z])
    field(NF, lambda z: m_ref[z].astype(F32))


def strip_kernel(par_ref, ya_ref, yb_ref, t_ref, xa_ref, xb_ref):
    px = par_ref[0]
    even = par_ref[1] == 0
    low = lanes((NX, NY)) % 32 < 16
    for f in range(NF + 1):
        for h in range(2):
            a = ya_ref[f, h]
            b = yb_ref[f, h]
            left = jnp.where(even, b, a)
            right = jnp.where(even, a, b)
            t_ref[f, h] = jnp.where(low, left, right)
            t_ref[f, h + 2] = jnp.where(low, pltpu.roll(left, NY - 16, 1), pltpu.roll(right, 16, 1))

    @pl.when(px == 0)
    def _():
        xa_ref[...] = t_ref[:, :, NX - DEPTH:, :]
        xb_ref[...] = t_ref[:, :, :DEPTH, :]

    @pl.when(px == 1)
    def _():
        xa_ref[...] = t_ref[:, :, :DEPTH, :]
        xb_ref[...] = t_ref[:, :, NX - DEPTH:, :]


def update(alpha, beta, center, around, base, solid):
    scale = beta * time_step * 2.0 / 3.0
    nu = beta * viscosity * time_step / 12.0
    u, v, w, p = center
    speed = [-scale * u, -scale * v, -scale * w]
    keep = beta - 90.0 * nu - (beta * time_step * penalty) * solid
    out = []
    p_diff = []
    for plus, minus, plus2, minus2 in around(3):
        p_diff.append((plus - minus) - 0.125 * (plus2 - minus2))
    divergence = None
    for k in range(3):
        near = far = None
        total = center[k] * keep - scale * p_diff[k]
        for d, (plus, minus, plus2, minus2) in enumerate(around(k)):
            diff = (plus - minus) - 0.125 * (plus2 - minus2)
            total = total + speed[d] * diff
            s1, s2 = plus + minus, plus2 + minus2
            near = s1 if near is None else near + s1
            far = s2 if far is None else far + s2
            if d == k:
                divergence = diff if divergence is None else divergence + diff
        total = total + ((16.0 * nu) * near - nu * far)
        if k == 0:
            total = total + beta * time_step * forcing
        out.append(total)
    out.append(beta * p - (sound_sq * scale) * divergence)
    if alpha:
        out = [o + alpha * base(f) for f, o in enumerate(out)]
    return out


def main_kernel(par_ref, q_in, m_in, xa_ref, xb_ref, t_in, ca_ref, cb_ref, out_ref,
                q, s1, s2, solid, tq, t1, t2, tsolid):
    px = par_ref[0]
    lane8 = lanes((8, NY))
    piece = lane8 % 32
    group = lane8 // 32

    for f in range(NF):
        q[f, :, OWN:BOTTOM, :] = q_in[f]
        tq[f, 2:6, OWN:BOTTOM, :] = t_in[f]
    solid[:, OWN:BOTTOM, :] = m_in[...].astype(F32)
    tsolid[:, OWN:BOTTOM, :] = t_in[NF]

    def halos(top, bottom, ctop, cbottom):
        q[:, :, TOP:OWN, :] = top[0:NF]
        q[:, :, BOTTOM:BOTTOM + DEPTH, :] = bottom[0:NF]
        solid[:, TOP:OWN, :] = top[NF]
        solid[:, BOTTOM:BOTTOM + DEPTH, :] = bottom[NF]
        tq[:, 2:6, TOP:OWN, :] = ctop[0:NF]
        tq[:, 2:6, BOTTOM:BOTTOM + DEPTH, :] = cbottom[0:NF]
        tsolid[:, TOP:OWN, :] = ctop[NF]
        tsolid[:, BOTTOM:BOTTOM + DEPTH, :] = cbottom[NF]

    @pl.when(px == 0)
    def _():
        halos(xb_ref, xa_ref, cb_ref, ca_ref)

    @pl.when(px == 1)
    def _():
        halos(xa_ref, xb_ref, ca_ref, cb_ref)

    for f in range(NF):
        for r in range(0, ROWS, 8):
            rr = pl.ds(r, 8)
            for zi in range(4):
                tq[f, (zi + 6) % 8, rr, :] = pltpu.roll(tq[f, zi + 2, rr, :], 96 if zi < 2 else 32, 1)

    def stage(number, cur, tcur, base, tbase, out, tout, alpha, beta):
        start = TOP + 2 * number
        stop = BOTTOM + DEPTH - 2 * number
        tiles = list(range(start, stop, 8))
        last = number == STAGES

        def strips(zi, carry):
            for r in tiles:
                rr = pl.ds(r, 8)

                def around(f):
                    a = tcur[f, zi + 2, rr, :]
                    c = pltpu.roll(cur[f, zi, rr, :], 16, 1)
                    for zq in range(1, 4):
                        c = jnp.where(group == zq, pltpu.roll(cur[f, 4 * zq + zi, rr, :], (16 + 32 * zq) % NY, 1), c)
                    yp = pltpu.roll(jnp.where(piece == 16, c, a), NY - 1, 1)
                    ym = pltpu.roll(jnp.where(piece == 15, c, a), 1, 1)
                    yp2 = pltpu.roll(jnp.where((piece == 16) | (piece == 17), c, a), NY - 2, 1)
                    ym2 = pltpu.roll(jnp.where((piece == 14) | (piece == 15), c, a), 2, 1)
                    x = [tcur[f, zi + 2, pl.ds(r + o, 8), :] for o in (1, -1, 2, -2)]
                    z = [tcur[f, zi + 2 + o, rr, :] for o in (1, -1, 2, -2)]
                    return x, (yp, ym, yp2, ym2), z

                center = [tcur[f, zi + 2, rr, :] for f in range(NF)]
                new = update(alpha, beta, center, around,
                             lambda f: tbase[f, zi + 2, rr, :], tsolid[zi, rr, :])
                ghost = lax.rem(zi + 6, 8)
                turn = jnp.where(zi < 2, 96, 32)
                for f in range(NF):
                    tout[f, zi + 2, rr, :] = new[f]
                    tout[f, ghost, rr, :] = pltpu.roll(new[f], turn, 1)
            return carry

        def main(z, carry):
            zi = lax.rem(z, 4)
            turn = 112 - 32 * (z // 4)
            zs = [lax.rem(z + o, NZ) for o in (1, NZ - 1, 2, NZ - 2)]
            for r in tiles:
                rr = pl.ds(r, 8)

                def around(f):
                    a = cur[f, z, rr, :]
                    e = pltpu.roll(tcur[f, zi + 2, rr, :], turn, 1)
                    yp = pltpu.roll(jnp.where(lane8 == 0, e, a), NY - 1, 1)
                    ym = pltpu.roll(jnp.where(lane8 == NY - 1, e, a), 1, 1)
                    yp2 = pltpu.roll(jnp.where(lane8 < 2, e, a), NY - 2, 1)
                    ym2 = pltpu.roll(jnp.where(lane8 >= NY - 2, e, a), 2, 1)
                    x = [cur[f, z, pl.ds(r + o, 8), :] for o in (1, -1, 2, -2)]
                    zz = [cur[f, k, rr, :] for k in zs]
                    return x, (yp, ym, yp2, ym2), zz

                center = [cur[f, z, rr, :] for f in range(NF)]
                new = update(alpha, beta, center, around,
                             lambda f: base[f, z, rr, :], solid[z, rr, :])
                for f in range(NF):
                    if last:
                        out_ref[f, z, pl.ds(r - OWN, 8), :] = new[f]
                    else:
                        out[f, z, rr, :] = new[f]
            return carry

        if not last:
            lax.fori_loop(0, 4, strips, 0)
        lax.fori_loop(0, NZ, main, 0)

    for step in range(2):
        stage(3 * step + 1, q, tq, q, tq, s1, t1, 0.0, 1.0)
        stage(3 * step + 2, s1, t1, q, tq, s2, t2, 0.75, 0.25)
        stage(3 * step + 3, s2, t2, q, tq, q, tq, 1.0 / 3.0, 2.0 / 3.0)


def call(kernel, outs, scratch=(), scalars=1, inputs=0):
    vmem = pl.BlockSpec(memory_space=pltpu.VMEM)
    return pl.pallas_call(
        kernel,
        out_shape=[jax.ShapeDtypeStruct(s, F32) for s in outs],
        in_specs=[pl.BlockSpec(memory_space=pltpu.SMEM)] * scalars + [vmem] * inputs,
        out_specs=[vmem] * len(outs),
        scratch_shapes=[pltpu.VMEM(s, F32) for s in scratch],
        compiler_params=pltpu.CompilerParams(vmem_limit_bytes=48 * 2 ** 20),
    )


def solution(mesh):
    nx, ny = mesh.shape["gx"], mesh.shape["gy"]

    def pairs(count, parity):
        return [(i, (i + 1) % count if i % 2 == parity else (i - 1) % count) for i in range(count)]

    def body(fields, solid_mask):
        parity = jnp.stack([lax.axis_index("gx") % 2, lax.axis_index("gy") % 2]).astype(jnp.int32)
        xmsg = (NF + 1, NZ, DEPTH, NY)
        ymsg = (NF + 1, 2, NX, NY)
        strip = (NF + 1, 4, NX, NY)
        cmsg = (NF + 1, 4, DEPTH, NY)
        xa, xb, ya, yb = call(pack_kernel, [xmsg, xmsg, ymsg, ymsg], inputs=2)(parity, fields, solid_mask)
        xb = lax.ppermute(xb, "gx", pairs(nx, 1))
        yb = lax.ppermute(yb, "gy", pairs(ny, 1))
        ya = lax.ppermute(ya, "gy", pairs(ny, 0))
        xa = lax.ppermute(xa, "gx", pairs(nx, 0))
        t, ca, cb = call(strip_kernel, [strip, cmsg, cmsg], inputs=2)(parity, ya, yb)
        cb = lax.ppermute(cb, "gx", pairs(nx, 1))
        ca = lax.ppermute(ca, "gx", pairs(nx, 0))
        wide = (NF, NZ, ROWS, NY)
        narrow = (NF, 8, ROWS, NY)
        scratch = [wide] * 3 + [(NZ, ROWS, NY)] + [narrow] * 3 + [(4, ROWS, NY)]
        out, = call(main_kernel, [(NF, NZ, NX, NY)], scratch, inputs=7)(
            parity, fields, solid_mask, xa, xb, t, ca, cb)
        return out

    return jax.shard_map(
        body,
        mesh=mesh,
        in_specs=(P(None, None, "gx", "gy"), P(None, "gx", "gy")),
        out_specs=P(None, None, "gx", "gy"),
        check_vma=False,
    )
```

time: 558 us -> 72.8 us (0.13); the launches traced: 550 us -> 72.4 us
  other arithmetic: 326 us -> 0.07 us
  local copies, waits for them, and re-layouts: 165 us -> 2.81 us
  Pallas kernels: 0 us -> 39.2 us
  starting transfers between devices: 45.7 us -> 12.8 us
  waiting for transfers between devices: 11.7 us -> 17.4 us
    div x13 -> x0, other arithmetic: 136 us -> none  [first_pair(): return (8.0 * (plus_one - minus_one) - (plus_two - minus_two)) / 12.0]
    add x12 -> x0, other arithmetic: 124 us -> none  [the longest x6 103 us: combine(): -advect - pressure_grad + viscosity * laplace - penalty * solid * speed]
    slice x22 -> x0, local copies, waits for them, and re-layouts: 73.2 us -> none  [the longest x11 39.8 us: padded_2(): lax.slice_in_dim(block, block.shape[dim] - width, None, axis=dim)]
    concatenate x8 -> x0, other arithmetic: 44.7 us -> none  [the longest x6 39 us: padded_2(): block = jnp.concatenate([low, block, high], axis=dim)]
    pallas_call x0 -> x3, Pallas kernels: none -> 39.2 us  [the longest x1 36.9 us: body(): call(main_kernel, [(NF, NZ, NX, NY)], scratch, inputs=7)]
    ppermute x12 -> x2, local copies, waits for them, and re-layouts: 34.7 us -> 0.32 us  [the longest x1 0.16 us: body(): xa = lax.ppermute(xa, 'gx', pairs(nx, 0))]
    unnamed x155 -> x6, local copies, waits for them, and re-layouts: 35.1 us -> 2.18 us
    ppermute x24 -> x6, starting transfers between devices: 45.7 us -> 12.8 us  [the longest x1 4.69 us: body(): yb = lax.ppermute(yb, 'gy', pairs(ny, 1))]
  transfers between devices with their start and end apart: 24 -> 6, of which waited for: 5 -> 3; matrix products, arithmetic and copies ran while one was open for 30% -> 1% of each run, Pallas kernels for 0% -> 1%
where the time goes in v1:
time: 72.8 us; the launch traced here: 72.4 us
  Pallas kernels  39.2 us (54%)
  waiting for transfers between devices  17.4 us (24%)
  starting transfers between devices  12.8 us (18%)
  local copies, waits for them, and re-layouts  2.81 us (4%)
    pallas_call x1, Pallas kernels, body(): call(main_kernel, [(NF, NZ, NX, NY)], scratch, inputs=7)  36.9 us
    ppermute x1, waiting for transfers between devices, body(): yb = lax.ppermute(yb, 'gy', pairs(ny, 1))  12.3 us
    ppermute x1, waiting for transfers between devices, body(): cb = lax.ppermute(cb, 'gx', pairs(nx, 1))  4.98 us
    ppermute x1, starting transfers between devices, body(): yb = lax.ppermute(yb, 'gy', pairs(ny, 1))  4.69 us
    ppermute x1, starting transfers between devices, body(): xb = lax.ppermute(xb, 'gx', pairs(nx, 1))  3.54 us
    ppermute x1, starting transfers between devices, body(): cb = lax.ppermute(cb, 'gx', pairs(nx, 1))  2.42 us
    unnamed x6, local copies, waits for them, and re-layouts  2.18 us
    ppermute x1, starting transfers between devices, body(): ya = lax.ppermute(ya, 'gy', pairs(ny, 0))  2 us
  transfers between devices with their start and end apart: 6, of which 3 were waited for; matrix products, arithmetic and copies ran while one was open for 1% of the time, Pallas kernels for 1%

profile of v1, /device:TPU:0, one launch (start us, length us, event | category | flops | bytes accessed | tf_op | source)
XLA Modules:
  0.0 72.4 jit_solution(972809377181450317)
XLA Ops:
  0.0 0.1 pad_add_fusion.par_ref
  0.1 0.0 copy-start
  0.1 1.2 %copy-done = f32[4,16,32,128]{3,2,1,0:T(8,128)S(1)} copy-done((f32[4,16,32,128]{3,2,1,0:T(8,128)S(1)}, f32[4,16,32,128]{3,2,1,0:T(8,128)}, u32[]{:S(2)}) %copy-start) | copy-done | bytes 1048600
  1.3 0.0 copy-start.2
  1.3 0.9 %copy-done.2 = s32[16,32,128]{2,1,0:T(8,128)S(1)} copy-done((s32[16,32,128]{2,1,0:T(8,128)S(1)}, s32[16,32,128]{2,1,0:T(8,128)}, u32[]{:S(2)}) %copy-start.2) | copy-done | bytes 262168
  2.3 1.6 %shard_map.28 = (f32[5,16,12,128]{3,2,1,0:T(8,128)S(1)}, f32[5,16,12,128]{3,2,1,0:T(8,128)S(1)}, f32[5,2,32,128]{3,2,1,0:T(8,128)S(1)}, f32[5,2,32,128]{3,2,1,0:T(8,128)S(1)}) custom-call(s32[2]{0:T(128)S(1)} %pad_add_fusion.par_ref, f32[4,16,32,128]{3,2,1,0:T(8,128)S(1)} %copy-done, s32[16,32,128]{2,1,0:T(8,128)S(1)} %copy-done.2), custom_call_target="tpu_custom_call" | custom-call | tf_op jit(solution)/shard_map/pallas_call | solution.py:257
  3.9 0.2 copy.4
  4.1 3.5 %collective-permute-start.1 = (f32[5,16,12,128]{3,1,2,0:T(8,128)S(1)}, f32[5,16,12,128]{3,1,2,0:T(8,128)S(1)}, u32[]{:S(2)}, u32[]{:S(2)}) collective-permute-start(f32[5,16,12,128]{3,1,2,0:T(8,128)S(1)} %copy.4), channel_id=1, source_target_pairs={{0,120},{8,16},{16,8},{24,32},{32,24},{40,48},{48,40},{56,64},{64,... | collective-permute-start | bytes 1474568 | tf_op jit(solution)/shard_map/ppermute | solution.py:258
  7.6 0.2 copy.3
  7.8 0.1 collective-permute-start
  7.9 2.0 %collective-permute-start.2 = (f32[5,2,32,128]{3,2,1,0:T(8,128)S(1)}, f32[5,2,32,128]{3,2,1,0:T(8,128)S(1)}, u32[]{:S(2)}, u32[]{:S(2)}) collective-permute-start(f32[5,2,32,128]{3,2,1,0:T(8,128)S(1)} %get-tuple-element.14), channel_id=1, source_target_pairs={{0,1},{1,0},{2,3},{3,2},{4,5},{5,4},{6,7},{7,6},{8,9},{9,8},{10,11... | collective-permute-start | bytes 491528 | tf_op jit(solution)/shard_map/ppermute | solution.py:260
  9.9 4.7 %collective-permute-start.3 = (f32[5,2,32,128]{3,2,1,0:T(8,128)S(1)}, f32[5,2,32,128]{3,2,1,0:T(8,128)S(1)}, u32[]{:S(2)}, u32[]{:S(2)}) collective-permute-start(f32[5,2,32,128]{3,2,1,0:T(8,128)S(1)} %get-tuple-element.15), channel_id=1, source_target_pairs={{0,7},{1,2},{2,1},{3,4},{4,3},{5,6},{6,5},{7,0},{8,15},{9,10},{10,... | collective-permute-start | bytes 491528 | tf_op jit(solution)/shard_map/ppermute | solution.py:259
  14.5 0.1 collective-permute-done.2.ya_ref
  14.6 12.3 %collective-permute-done.3.yb_ref = f32[5,2,32,128]{3,2,1,0:T(8,128)S(1)} collective-permute-done((f32[5,2,32,128]{3,2,1,0:T(8,128)S(1)}, f32[5,2,32,128]{3,2,1,0:T(8,128)S(1)}, u32[]{:S(2)}, u32[]{:S(2)}) %collective-permute-start.3) | collective-permute-done | bytes 163872 | tf_op jit(solution)/shard_map/ppermute | solution.py:259
  26.9 0.7 shard_map.29
  27.6 0.1 collective-permute-start.4
  27.7 0.0 copy-start.1
  27.7 2.4 %collective-permute-start.5 = (f32[5,4,12,128]{3,2,1,0:T(8,128)S(1)}, f32[5,4,12,128]{3,2,1,0:T(8,128)S(1)}, u32[]{:S(2)}, u32[]{:S(2)}) collective-permute-start(f32[5,4,12,128]{3,2,1,0:T(8,128)S(1)} %get-tuple-element.18), channel_id=1, source_target_pairs={{0,120},{8,16},{16,8},{24,32},{32,24},{40,48},{48,40},{56,64},{64,... | collective-permute-start | bytes 368648 | tf_op jit(solution)/shard_map/ppermute | solution.py:263
  30.2 0.0 collective-permute-done.1
  30.2 0.2 copy.6.xb_ref
  30.3 0.0 collective-permute-done
  30.4 0.2 copy.5.xa_ref
  30.5 0.0 collective-permute-done.4.ca_ref
  30.5 5.0 %collective-permute-done.5.cb_ref = f32[5,4,12,128]{3,2,1,0:T(8,128)S(1)} collective-permute-done((f32[5,4,12,128]{3,2,1,0:T(8,128)S(1)}, f32[5,4,12,128]{3,2,1,0:T(8,128)S(1)}, u32[]{:S(2)}, u32[]{:S(2)}) %collective-permute-start.5) | collective-permute-done | bytes 122912 | tf_op jit(solution)/shard_map/ppermute | solution.py:263
  35.5 0.0 copy-done.1
  35.5 36.9 %shard_map.30 = f32[4,16,32,128]{3,2,1,0:T(8,128)} custom-call(s32[2]{0:T(128)S(1)} %pad_add_fusion.par_ref, f32[4,16,32,128]{3,2,1,0:T(8,128)S(1)} %copy-done.1, s32[16,32,128]{2,1,0:T(8,128)S(1)} %copy-done.2, f32[5,16,12,128]{3,2,1,0:T(8,128)S(1)} %copy.5.xa_ref, f32[5,16,12,128]{3,2,1,0:T(8,128)S(1)} %copy.6.xb_ref, ...), custom_call_target="tpu_custom_call" | custom-call | tf_op jit(solution)/shard_map/pallas_call | solution.py:268
Async XLA Ops:
  0.1 1.2 %copy-start = (f32[4,16,32,128]{3,2,1,0:T(8,128)S(1)}, f32[4,16,32,128]{3,2,1,0:T(8,128)}, u32[]{:S(2)}) copy-start(f32[4,16,32,128]{3,2,1,0:T(8,128)} %q_in.1) | copy-start | bytes 3145732
  1.3 0.9 %copy-start.2 = (s32[16,32,128]{2,1,0:T(8,128)S(1)}, s32[16,32,128]{2,1,0:T(8,128)}, u32[]{:S(2)}) copy-start(s32[16,32,128]{2,1,0:T(8,128)} %m_in.1) | copy-start | bytes 786436
  4.1 26.1 %collective-permute-start.1 = (f32[5,16,12,128]{3,1,2,0:T(8,128)S(1)}, f32[5,16,12,128]{3,1,2,0:T(8,128)S(1)}, u32[]{:S(2)}, u32[]{:S(2)}) collective-permute-start(f32[5,16,12,128]{3,1,2,0:T(8,128)S(1)} %copy.4), channel_id=1, source_target_pairs={{0,120},{8,16},{16,8},{24,32},{32,24},{40,48},{48,40},{56,64},{64,... | collective-permute-start | bytes 1474568 | tf_op jit(solution)/shard_map/ppermute | solution.py:258
  7.8 22.6 %collective-permute-start = (f32[5,16,12,128]{3,1,2,0:T(8,128)S(1)}, f32[5,16,12,128]{3,1,2,0:T(8,128)S(1)}, u32[]{:S(2)}, u32[]{:S(2)}) collective-permute-start(f32[5,16,12,128]{3,1,2,0:T(8,128)S(1)} %copy.3), channel_id=1, source_target_pairs={{0,8},{8,0},{16,24},{24,16},{32,40},{40,32},{48,56},{56,48},{64,72... | collective-permute-start | bytes 1474568 | tf_op jit(solution)/shard_map/ppermute | solution.py:261
  7.9 6.8 %collective-permute-start.2 = (f32[5,2,32,128]{3,2,1,0:T(8,128)S(1)}, f32[5,2,32,128]{3,2,1,0:T(8,128)S(1)}, u32[]{:S(2)}, u32[]{:S(2)}) collective-permute-start(f32[5,2,32,128]{3,2,1,0:T(8,128)S(1)} %get-tuple-element.14), channel_id=1, source_target_pairs={{0,1},{1,0},{2,3},{3,2},{4,5},{5,4},{6,7},{7,6},{8,9},{9,8},{10,11... | collective-permute-start | bytes 491528 | tf_op jit(solution)/shard_map/ppermute | solution.py:260
  9.9 17.1 %collective-permute-start.3 = (f32[5,2,32,128]{3,2,1,0:T(8,128)S(1)}, f32[5,2,32,128]{3,2,1,0:T(8,128)S(1)}, u32[]{:S(2)}, u32[]{:S(2)}) collective-permute-start(f32[5,2,32,128]{3,2,1,0:T(8,128)S(1)} %get-tuple-element.15), channel_id=1, source_target_pairs={{0,7},{1,2},{2,1},{3,4},{4,3},{5,6},{6,5},{7,0},{8,15},{9,10},{10,... | collective-permute-start | bytes 491528 | tf_op jit(solution)/shard_map/ppermute | solution.py:259
  27.6 2.9 %collective-permute-start.4 = (f32[5,4,12,128]{3,2,1,0:T(8,128)S(1)}, f32[5,4,12,128]{3,2,1,0:T(8,128)S(1)}, u32[]{:S(2)}, u32[]{:S(2)}) collective-permute-start(f32[5,4,12,128]{3,2,1,0:T(8,128)S(1)} %get-tuple-element.17), channel_id=1, source_target_pairs={{0,8},{8,0},{16,24},{24,16},{32,40},{40,32},{48,56},{56,48},{64,72... | collective-permute-start | bytes 368648 | tf_op jit(solution)/shard_map/ppermute | solution.py:264
  27.7 7.8 %copy-start.1 = (f32[4,16,32,128]{3,2,1,0:T(8,128)S(1)}, f32[4,16,32,128]{3,2,1,0:T(8,128)}, u32[]{:S(2)}) copy-start(f32[4,16,32,128]{3,2,1,0:T(8,128)} %q_in.1) | copy-start | bytes 3145732
  27.7 7.8 %collective-permute-start.5 = (f32[5,4,12,128]{3,2,1,0:T(8,128)S(1)}, f32[5,4,12,128]{3,2,1,0:T(8,128)S(1)}, u32[]{:S(2)}, u32[]{:S(2)}) collective-permute-start(f32[5,4,12,128]{3,2,1,0:T(8,128)S(1)} %get-tuple-element.18), channel_id=1, source_target_pairs={{0,120},{8,16},{16,8},{24,32},{32,24},{40,48},{48,40},{56,64},{64,... | collective-permute-start | bytes 368648 | tf_op jit(solution)/shard_map/ppermute | solution.py:263

commit v2 on v1

--- a/solution.py
+++ b/solution.py
@@ -1,5 +1,8 @@
+import functools
+
 import jax
 import jax.numpy as jnp
+import numpy as np
 from jax import lax
 from jax.sharding import PartitionSpec as P
 from jax.experimental import pallas as pl
@@ -96,23 +99,24 @@
     u, v, w, p = center
     speed = [-scale * u, -scale * v, -scale * w]
     keep = beta - 90.0 * nu - (beta * time_step * penalty) * solid
+
+    def first(plus, minus, plus2, minus2):
+        return (plus - minus) - 0.125 * (plus2 - minus2)
+
     out = []
-    p_diff = []
-    for plus, minus, plus2, minus2 in around(3):
-        p_diff.append((plus - minus) - 0.125 * (plus2 - minus2))
+    x, z, dy, _ = around(3)
+    p_diff = [first(*x), dy, first(*z)]
     divergence = None
     for k in range(3):
-        near = far = None
+        x, z, dy, sy = around(k)
+        diffs = [first(*x), dy, first(*z)]
+        near = (x[0] + x[1]) + (z[0] + z[1])
+        far = (x[2] + x[3]) + (z[2] + z[3])
         total = center[k] * keep - scale * p_diff[k]
-        for d, (plus, minus, plus2, minus2) in enumerate(around(k)):
-            diff = (plus - minus) - 0.125 * (plus2 - minus2)
-            total = total + speed[d] * diff
-            s1, s2 = plus + minus, plus2 + minus2
-            near = s1 if near is None else near + s1
-            far = s2 if far is None else far + s2
-            if d == k:
-                divergence = diff if divergence is None else divergence + diff
-        total = total + ((16.0 * nu) * near - nu * far)
+        for d in range(3):
+            total = total + speed[d] * diffs[d]
+        divergence = diffs[k] if divergence is None else divergence + diffs[k]
+        total = total + nu * ((16.0 * near - far) + sy)
         if k == 0:
             total = total + beta * time_step * forcing
         out.append(total)
@@ -122,12 +126,47 @@
     return out
 
 
-def main_kernel(par_ref, q_in, m_in, xa_ref, xb_ref, t_in, ca_ref, cb_ref, out_ref,
-                q, s1, s2, solid, tq, t1, t2, tsolid):
+def y_weights():
+    taps = [(1, 1.0, 16.0), (-1, -1.0, 16.0), (2, -0.125, -1.0), (-2, 0.125, -1.0)]
+    wide = np.zeros((4, 512, 256), np.float32)
+    strip = np.zeros((1280, 256), np.float32)
+    for o, first, second in taps:
+        for j in range(NY):
+            for zq in range(4):
+                c = j + o
+                if 0 <= c < NY:
+                    rows = (c, c + 128)
+                else:
+                    lane = 32 * zq + 16 + (c if c < 0 else c - NY)
+                    rows = (256 + lane, 384 + lane)
+                for r in rows:
+                    wide[zq, r, j] = first
+                    wide[zq, r, j + NY] = second
+            g, place = j // 32, j % 32
+            c = place - 16 if place < 16 else NY + place - 16
+            left = place < 16
+            c += o
+            if c < -16 or c >= NY + 16:
+                continue
+            if (left and c < 0) or (not left and c >= NY):
+                lane = 32 * g + 16 + (c if c < 0 else c - NY)
+                rows = (lane, lane + 128)
+            else:
+                rows = (256 + 256 * g + c, 384 + 256 * g + c)
+            for r in rows:
+                strip[r, j] = first
+                strip[r, j + NY] = second
+    return jnp.asarray(wide, jnp.bfloat16), jnp.asarray(strip, jnp.bfloat16)
+
+
+def split(a):
+    high = a.astype(jnp.bfloat16)
+    return high, (a - high.astype(F32)).astype(jnp.bfloat16)
+
+
+def main_kernel(par_ref, q_in, m_in, xa_ref, xb_ref, t_in, ca_ref, cb_ref, w_ref, ws_ref, out_ref,
+                q, s1, s2, solid, tq, t1, t2, tsolid, yd, ytd):
     px = par_ref[0]
-    lane8 = lanes((8, NY))
-    piece = lane8 % 32
-    group = lane8 // 32
 
     for f in range(NF):
         q[f, :, OWN:BOTTOM, :] = q_in[f]
@@ -163,52 +202,57 @@
         start = TOP + 2 * number
         stop = BOTTOM + DEPTH - 2 * number
         tiles = list(range(start, stop, 8))
+        count = 8 * len(tiles)
         last = number == STAGES
 
-        def strips(zi, carry):
+        def along_y(f, carry):
+            rr = pl.ds(start, count)
+
+            def flat(ref, z):
+                return split(ref[f, z:z + 4, rr, :].reshape(4 * count, NY))
+
+            t = flat(tcur, 2)
+            every = list(t)
+            for zq in range(4):
+                a = flat(cur, 4 * zq)
+                every += a
+                y = jnp.dot(jnp.concatenate(a + t, axis=1), w_ref[zq], preferred_element_type=F32)
+                yd[f, 4 * zq:4 * zq + 4, 0:count, :] = y.reshape(4, count, 2 * NY)
+            if not last:
+                y = jnp.dot(jnp.concatenate(every, axis=1), ws_ref[...], preferred_element_type=F32)
+                ytd[f, :, 0:count, :] = y.reshape(4, count, 2 * NY)
+            return carry
+
+        lax.fori_loop(0, NF, along_y, 0)
+
+        def strips(half, zi, carry):
             for r in tiles:
                 rr = pl.ds(r, 8)
+                yr = pl.ds(r - start, 8)
 
                 def around(f):
-                    a = tcur[f, zi + 2, rr, :]
-                    c = pltpu.roll(cur[f, zi, rr, :], 16, 1)
-                    for zq in range(1, 4):
-                        c = jnp.where(group == zq, pltpu.roll(cur[f, 4 * zq + zi, rr, :], (16 + 32 * zq) % NY, 1), c)
-                    yp = pltpu.roll(jnp.where(piece == 16, c, a), NY - 1, 1)
-                    ym = pltpu.roll(jnp.where(piece == 15, c, a), 1, 1)
-                    yp2 = pltpu.roll(jnp.where((piece == 16) | (piece == 17), c, a), NY - 2, 1)
-                    ym2 = pltpu.roll(jnp.where((piece == 14) | (piece == 15), c, a), 2, 1)
                     x = [tcur[f, zi + 2, pl.ds(r + o, 8), :] for o in (1, -1, 2, -2)]
                     z = [tcur[f, zi + 2 + o, rr, :] for o in (1, -1, 2, -2)]
-                    return x, (yp, ym, yp2, ym2), z
+                    return x, z, ytd[f, zi, yr, 0:NY], ytd[f, zi, yr, NY:]
 
                 center = [tcur[f, zi + 2, rr, :] for f in range(NF)]
                 new = update(alpha, beta, center, around,
                              lambda f: tbase[f, zi + 2, rr, :], tsolid[zi, rr, :])
-                ghost = lax.rem(zi + 6, 8)
-                turn = jnp.where(zi < 2, 96, 32)
                 for f in range(NF):
                     tout[f, zi + 2, rr, :] = new[f]
-                    tout[f, ghost, rr, :] = pltpu.roll(new[f], turn, 1)
+                    tout[f, zi + (6 if half == 0 else -2), rr, :] = pltpu.roll(new[f], 32 if half else 96, 1)
             return carry
 
         def main(z, carry):
-            zi = lax.rem(z, 4)
-            turn = 112 - 32 * (z // 4)
             zs = [lax.rem(z + o, NZ) for o in (1, NZ - 1, 2, NZ - 2)]
             for r in tiles:
                 rr = pl.ds(r, 8)
+                yr = pl.ds(r - start, 8)
 
                 def around(f):
-                    a = cur[f, z, rr, :]
-                    e = pltpu.roll(tcur[f, zi + 2, rr, :], turn, 1)
-                    yp = pltpu.roll(jnp.where(lane8 == 0, e, a), NY - 1, 1)
-                    ym = pltpu.roll(jnp.where(lane8 == NY - 1, e, a), 1, 1)
-                    yp2 = pltpu.roll(jnp.where(lane8 < 2, e, a), NY - 2, 1)
-                    ym2 = pltpu.roll(jnp.where(lane8 >= NY - 2, e, a), 2, 1)
                     x = [cur[f, z, pl.ds(r + o, 8), :] for o in (1, -1, 2, -2)]
                     zz = [cur[f, k, rr, :] for k in zs]
-                    return x, (yp, ym, yp2, ym2), zz
+                    return x, zz, yd[f, z, yr, 0:NY], yd[f, z, yr, NY:]
 
                 center = [cur[f, z, rr, :] for f in range(NF)]
                 new = update(alpha, beta, center, around,
@@ -221,7 +265,8 @@
             return carry
 
         if not last:
-            lax.fori_loop(0, 4, strips, 0)
+            for half in range(2):
+                lax.fori_loop(2 * half, 2 * half + 2, functools.partial(strips, half), 0)
         lax.fori_loop(0, NZ, main, 0)
 
     for step in range(2):
@@ -265,8 +310,9 @@
         wide = (NF, NZ, ROWS, NY)
         narrow = (NF, 8, ROWS, NY)
         scratch = [wide] * 3 + [(NZ, ROWS, NY)] + [narrow] * 3 + [(4, ROWS, NY)]
-        out, = call(main_kernel, [(NF, NZ, NX, NY)], scratch, inputs=7)(
-            parity, fields, solid_mask, xa, xb, t, ca, cb)
+        scratch += [(NF, NZ, 56, 2 * NY), (NF, 4, 56, 2 * NY)]
+        out, = call(main_kernel, [(NF, NZ, NX, NY)], scratch, inputs=9)(
+            parity, fields, solid_mask, xa, xb, t, ca, cb, *y_weights())
         return out
 
     return jax.shard_map(

time: 72.8 us -> 63.1 us (0.87)
  Pallas kernels: 39.2 us -> 29.5 us
    pallas_call x1, Pallas kernels: 36.9 us -> 27.2 us  [body(): call(main_kernel, [(NF, NZ, NX, NY)], scratch, inputs=9)]
    unnamed x6 -> x10, local copies, waits for them, and re-layouts: 2.18 us -> 2.19 us
where the time goes in v2:
time: 63.1 us; the launch traced here: 62.7 us
  Pallas kernels  29.5 us (47%)
  waiting for transfers between devices  17.4 us (28%)
  starting transfers between devices  12.8 us (20%)
  local copies, waits for them, and re-layouts  2.83 us (4%)
    pallas_call x1, Pallas kernels, body(): call(main_kernel, [(NF, NZ, NX, NY)], scratch, inputs=9)  27.2 us
    ppermute x1, waiting for transfers between devices, body(): yb = lax.ppermute(yb, 'gy', pairs(ny, 1))  12.3 us
    ppermute x1, waiting for transfers between devices, body(): cb = lax.ppermute(cb, 'gx', pairs(nx, 1))  5.01 us
    ppermute x1, starting transfers between devices, body(): yb = lax.ppermute(yb, 'gy', pairs(ny, 1))  4.69 us
    ppermute x1, starting transfers between devices, body(): xb = lax.ppermute(xb, 'gx', pairs(nx, 1))  3.54 us
    ppermute x1, starting transfers between devices, body(): cb = lax.ppermute(cb, 'gx', pairs(nx, 1))  2.41 us
    unnamed x10, local copies, waits for them, and re-layouts  2.19 us
    ppermute x1, starting transfers between devices, body(): ya = lax.ppermute(ya, 'gy', pairs(ny, 0))  2 us
  transfers between devices with their start and end apart: 6, of which 3 were waited for; matrix products, arithmetic and copies ran while one was open for 1% of the time, Pallas kernels for 1%

profile of v2, /device:TPU:0, one launch (start us, length us, event | category | flops | bytes accessed | tf_op | source)
XLA Modules:
  0.0 62.7 jit_solution(15385622579120147698)
XLA Ops:
  0.0 0.1 pad_add_fusion.par_ref
  0.1 0.0 copy-start
  0.1 1.2 %copy-done = f32[4,16,32,128]{3,2,1,0:T(8,128)S(1)} copy-done((f32[4,16,32,128]{3,2,1,0:T(8,128)S(1)}, f32[4,16,32,128]{3,2,1,0:T(8,128)}, u32[]{:S(2)}) %copy-start) | copy-done | bytes 1048600
  1.3 0.0 copy-start.2
  1.3 0.9 %copy-done.2 = s32[16,32,128]{2,1,0:T(8,128)S(1)} copy-done((s32[16,32,128]{2,1,0:T(8,128)S(1)}, s32[16,32,128]{2,1,0:T(8,128)}, u32[]{:S(2)}) %copy-start.2) | copy-done | bytes 262168
  2.3 1.6 %shard_map.46 = (f32[5,16,12,128]{3,2,1,0:T(8,128)S(1)}, f32[5,16,12,128]{3,2,1,0:T(8,128)S(1)}, f32[5,2,32,128]{3,2,1,0:T(8,128)S(1)}, f32[5,2,32,128]{3,2,1,0:T(8,128)S(1)}) custom-call(s32[2]{0:T(128)S(1)} %pad_add_fusion.par_ref, f32[4,16,32,128]{3,2,1,0:T(8,128)S(1)} %copy-done, s32[16,32,128]{2,1,0:T(8,128)S(1)} %copy-done.2), custom_call_target="tpu_custom_call" | custom-call | tf_op jit(solution)/shard_map/pallas_call | solution.py:302
  3.9 0.2 copy.6
  4.1 3.5 %collective-permute-start.1 = (f32[5,16,12,128]{3,1,2,0:T(8,128)S(1)}, f32[5,16,12,128]{3,1,2,0:T(8,128)S(1)}, u32[]{:S(2)}, u32[]{:S(2)}) collective-permute-start(f32[5,16,12,128]{3,1,2,0:T(8,128)S(1)} %copy.6), channel_id=1, source_target_pairs={{0,120},{8,16},{16,8},{24,32},{32,24},{40,48},{48,40},{56,64},{64,... | collective-permute-start | bytes 1474568 | tf_op jit(solution)/shard_map/ppermute | solution.py:303
  7.6 0.0 copy-start.4
  7.6 0.2 copy.5
  7.8 0.1 collective-permute-start
  7.9 2.0 %collective-permute-start.2 = (f32[5,2,32,128]{3,2,1,0:T(8,128)S(1)}, f32[5,2,32,128]{3,2,1,0:T(8,128)S(1)}, u32[]{:S(2)}, u32[]{:S(2)}) collective-permute-start(f32[5,2,32,128]{3,2,1,0:T(8,128)S(1)} %get-tuple-element.14), channel_id=1, source_target_pairs={{0,1},{1,0},{2,3},{3,2},{4,5},{5,4},{6,7},{7,6},{8,9},{9,8},{10,11... | collective-permute-start | bytes 491528 | tf_op jit(solution)/shard_map/ppermute | solution.py:305
  9.9 4.7 %collective-permute-start.3 = (f32[5,2,32,128]{3,2,1,0:T(8,128)S(1)}, f32[5,2,32,128]{3,2,1,0:T(8,128)S(1)}, u32[]{:S(2)}, u32[]{:S(2)}) collective-permute-start(f32[5,2,32,128]{3,2,1,0:T(8,128)S(1)} %get-tuple-element.15), channel_id=1, source_target_pairs={{0,7},{1,2},{2,1},{3,4},{4,3},{5,6},{6,5},{7,0},{8,15},{9,10},{10,... | collective-permute-start | bytes 491528 | tf_op jit(solution)/shard_map/ppermute | solution.py:304
  14.5 0.1 collective-permute-done.2.ya_ref
  14.6 12.3 %collective-permute-done.3.yb_ref = f32[5,2,32,128]{3,2,1,0:T(8,128)S(1)} collective-permute-done((f32[5,2,32,128]{3,2,1,0:T(8,128)S(1)}, f32[5,2,32,128]{3,2,1,0:T(8,128)S(1)}, u32[]{:S(2)}, u32[]{:S(2)}) %collective-permute-start.3) | collective-permute-done | bytes 163872 | tf_op jit(solution)/shard_map/ppermute | solution.py:304
  26.9 0.7 %shard_map.47 = (f32[5,4,32,128]{3,2,1,0:T(8,128)S(1)}, f32[5,4,12,128]{3,2,1,0:T(8,128)S(1)}, f32[5,4,12,128]{3,2,1,0:T(8,128)S(1)}) custom-call(s32[2]{0:T(128)S(1)} %pad_add_fusion.par_ref, f32[5,2,32,128]{3,2,1,0:T(8,128)S(1)} %collective-permute-done.2.ya_ref, f32[5,2,32,128]{3,2,1,0:T(8,128)S(1)} %collective-permute-done.3.yb_ref), custom_call_target="tpu_custom_call" | custom-call | tf_op jit(solution)/shard_map/pallas_call | solution.py:307
  27.6 0.1 collective-permute-start.4
  27.7 0.0 copy-start.1
  27.7 0.0 copy-start.3
  27.8 2.4 %collective-permute-start.5 = (f32[5,4,12,128]{3,2,1,0:T(8,128)S(1)}, f32[5,4,12,128]{3,2,1,0:T(8,128)S(1)}, u32[]{:S(2)}, u32[]{:S(2)}) collective-permute-start(f32[5,4,12,128]{3,2,1,0:T(8,128)S(1)} %get-tuple-element.18), channel_id=1, source_target_pairs={{0,120},{8,16},{16,8},{24,32},{32,24},{40,48},{48,40},{56,64},{64,... | collective-permute-start | bytes 368648 | tf_op jit(solution)/shard_map/ppermute | solution.py:308
  30.2 0.0 collective-permute-done.1
  30.2 0.2 copy.8.xb_ref
  30.3 0.0 collective-permute-done
  30.4 0.2 copy.7.xa_ref
  30.5 0.0 collective-permute-done.4.ca_ref
  30.5 5.0 %collective-permute-done.5.cb_ref = f32[5,4,12,128]{3,2,1,0:T(8,128)S(1)} collective-permute-done((f32[5,4,12,128]{3,2,1,0:T(8,128)S(1)}, f32[5,4,12,128]{3,2,1,0:T(8,128)S(1)}, u32[]{:S(2)}, u32[]{:S(2)}) %collective-permute-start.5) | collective-permute-done | bytes 122912 | tf_op jit(solution)/shard_map/ppermute | solution.py:308
  35.5 0.0 copy-done.4
  35.5 0.0 copy-done.1
  35.6 0.0 copy-done.3
  35.6 27.2 %shard_map.48 = f32[4,16,32,128]{3,2,1,0:T(8,128)} custom-call(s32[2]{0:T(128)S(1)} %pad_add_fusion.par_ref, f32[4,16,32,128]{3,2,1,0:T(8,128)S(1)} %copy-done.1, s32[16,32,128]{2,1,0:T(8,128)S(1)} %copy-done.2, f32[5,16,12,128]{3,2,1,0:T(8,128)S(1)} %copy.7.xa_ref, f32[5,16,12,128]{3,2,1,0:T(8,128)S(1)} %copy.8.xb_ref, ...), custom_call_target="tpu_custom_call" | custom-call | tf_op jit(solution)/shard_map/pallas_call | solution.py:314
Async XLA Ops:
  0.1 1.2 %copy-start = (f32[4,16,32,128]{3,2,1,0:T(8,128)S(1)}, f32[4,16,32,128]{3,2,1,0:T(8,128)}, u32[]{:S(2)}) copy-start(f32[4,16,32,128]{3,2,1,0:T(8,128)} %q_in.1) | copy-start | bytes 3145732
  1.3 0.9 %copy-start.2 = (s32[16,32,128]{2,1,0:T(8,128)S(1)}, s32[16,32,128]{2,1,0:T(8,128)}, u32[]{:S(2)}) copy-start(s32[16,32,128]{2,1,0:T(8,128)} %m_in.1) | copy-start | bytes 786436
  4.1 26.1 %collective-permute-start.1 = (f32[5,16,12,128]{3,1,2,0:T(8,128)S(1)}, f32[5,16,12,128]{3,1,2,0:T(8,128)S(1)}, u32[]{:S(2)}, u32[]{:S(2)}) collective-permute-start(f32[5,16,12,128]{3,1,2,0:T(8,128)S(1)} %copy.6), channel_id=1, source_target_pairs={{0,120},{8,16},{16,8},{24,32},{32,24},{40,48},{48,40},{56,64},{64,... | collective-permute-start | bytes 1474568 | tf_op jit(solution)/shard_map/ppermute | solution.py:303
  7.6 27.9 %copy-start.4 = (bf16[1280,256]{1,0:T(8,128)(2,1)S(1)}, bf16[1280,256]{1,0:T(8,128)(2,1)}, u32[]{:S(2)}) copy-start(bf16[1280,256]{1,0:T(8,128)(2,1)} %constant.31.clone.ws_ref) | copy-start | bytes 1966084
  7.8 22.6 %collective-permute-start = (f32[5,16,12,128]{3,1,2,0:T(8,128)S(1)}, f32[5,16,12,128]{3,1,2,0:T(8,128)S(1)}, u32[]{:S(2)}, u32[]{:S(2)}) collective-permute-start(f32[5,16,12,128]{3,1,2,0:T(8,128)S(1)} %copy.5), channel_id=1, source_target_pairs={{0,8},{8,0},{16,24},{24,16},{32,40},{40,32},{48,56},{56,48},{64,72... | collective-permute-start | bytes 1474568 | tf_op jit(solution)/shard_map/ppermute | solution.py:306
  7.9 6.8 %collective-permute-start.2 = (f32[5,2,32,128]{3,2,1,0:T(8,128)S(1)}, f32[5,2,32,128]{3,2,1,0:T(8,128)S(1)}, u32[]{:S(2)}, u32[]{:S(2)}) collective-permute-start(f32[5,2,32,128]{3,2,1,0:T(8,128)S(1)} %get-tuple-element.14), channel_id=1, source_target_pairs={{0,1},{1,0},{2,3},{3,2},{4,5},{5,4},{6,7},{7,6},{8,9},{9,8},{10,11... | collective-permute-start | bytes 491528 | tf_op jit(solution)/shard_map/ppermute | solution.py:305
  9.9 17.1 %collective-permute-start.3 = (f32[5,2,32,128]{3,2,1,0:T(8,128)S(1)}, f32[5,2,32,128]{3,2,1,0:T(8,128)S(1)}, u32[]{:S(2)}, u32[]{:S(2)}) collective-permute-start(f32[5,2,32,128]{3,2,1,0:T(8,128)S(1)} %get-tuple-element.15), channel_id=1, source_target_pairs={{0,7},{1,2},{2,1},{3,4},{4,3},{5,6},{6,5},{7,0},{8,15},{9,10},{10,... | collective-permute-start | bytes 491528 | tf_op jit(solution)/shard_map/ppermute | solution.py:304
  27.6 2.9 %collective-permute-start.4 = (f32[5,4,12,128]{3,2,1,0:T(8,128)S(1)}, f32[5,4,12,128]{3,2,1,0:T(8,128)S(1)}, u32[]{:S(2)}, u32[]{:S(2)}) collective-permute-start(f32[5,4,12,128]{3,2,1,0:T(8,128)S(1)} %get-tuple-element.17), channel_id=1, source_target_pairs={{0,8},{8,0},{16,24},{24,16},{32,40},{40,32},{48,56},{56,48},{64,72... | collective-permute-start | bytes 368648 | tf_op jit(solution)/shard_map/ppermute | solution.py:309
  27.7 7.8 %copy-start.1 = (f32[4,16,32,128]{3,2,1,0:T(8,128)S(1)}, f32[4,16,32,128]{3,2,1,0:T(8,128)}, u32[]{:S(2)}) copy-start(f32[4,16,32,128]{3,2,1,0:T(8,128)} %q_in.1) | copy-start | bytes 3145732
  27.7 7.8 %copy-start.3 = (bf16[4,512,256]{2,1,0:T(8,128)(2,1)S(1)}, bf16[4,512,256]{2,1,0:T(8,128)(2,1)}, u32[]{:S(2)}) copy-start(bf16[4,512,256]{2,1,0:T(8,128)(2,1)} %constant.30.clone.w_ref) | copy-start | bytes 3145732
  27.8 7.8 %collective-permute-start.5 = (f32[5,4,12,128]{3,2,1,0:T(8,128)S(1)}, f32[5,4,12,128]{3,2,1,0:T(8,128)S(1)}, u32[]{:S(2)}, u32[]{:S(2)}) collective-permute-start(f32[5,4,12,128]{3,2,1,0:T(8,128)S(1)} %get-tuple-element.18), channel_id=1, source_target_pairs={{0,120},{8,16},{16,8},{24,32},{32,24},{40,48},{48,40},{56,64},{64,... | collective-permute-start | bytes 368648 | tf_op jit(solution)/shard_map/ppermute | solution.py:308

commit v3 on v2

--- a/solution.py
+++ b/solution.py
@@ -21,6 +21,7 @@
 OWN = 16
 TOP = OWN - DEPTH
 BOTTOM = OWN + NX
+MSG = (NF + 1) * DEPTH - 2
 F32 = jnp.float32
 
 
@@ -28,69 +29,88 @@
     return lax.broadcasted_iota(jnp.int32, shape, len(shape) - 1)
 
 
-def pack_kernel(par_ref, q_ref, m_ref, xa_ref, xb_ref, ya_ref, yb_ref):
-    px = par_ref[0]
-    py = par_ref[1]
-
-    def rows_to(dst, start):
-        dst[0:NF] = q_ref[:, :, start:start + DEPTH, :]
-        dst[NF] = m_ref[:, start:start + DEPTH, :].astype(F32)
-
-    @pl.when(px == 0)
-    def _():
-        rows_to(xa_ref, NX - DEPTH)
-        rows_to(xb_ref, 0)
-
-    @pl.when(px == 1)
-    def _():
-        rows_to(xa_ref, 0)
-        rows_to(xb_ref, NX - DEPTH)
-
+def pack_y_kernel(par_ref, q_hbm, m_hbm, ya_ref, yb_ref, q_ref, m_ref, sems):
+    copies = [pltpu.make_async_copy(m_hbm, m_ref, sems.at[NF])]
+    copies += [pltpu.make_async_copy(q_hbm.at[f], q_ref.at[f], sems.at[f]) for f in range(NF)]
+    for copy in copies:
+        copy.start()
     lane = lanes((NX, NY))
     group = lane // 32
     low = lane % 32 < 16
-    even = py == 0
-
-    def field(f, load):
-        def packed(zi):
-            out = pltpu.roll(load(zi), 16, 1)
-            for zq in range(1, 4):
-                out = jnp.where(group == zq, pltpu.roll(load(4 * zq + zi), (16 + 32 * zq) % NY, 1), out)
-            return out
+    even = par_ref[1] == 0
+
+    def packed(load, zi):
+        out = pltpu.roll(load(zi), 16, 1)
+        for zq in range(1, 4):
+            out = jnp.where(group == zq, pltpu.roll(load(4 * zq + zi), (16 + 32 * zq) % NY, 1), out)
+        return out
+
+    def both(load, h):
+        first, second = packed(load, h), packed(load, h + 2)
+        return (jnp.where(low, first, pltpu.roll(second, 16, 1)),
+                jnp.where(low, pltpu.roll(second, NY - 16, 1), first))
+
+    copies[0].wait()
+    mask = [both(lambda z: m_ref[z].astype(F32), h) for h in range(2)]
+    for f in range(NF):
+        copies[1 + f].wait()
         for h in range(2):
-            first, second = packed(h), packed(h + 2)
-            right = jnp.where(low, first, pltpu.roll(second, 16, 1))
-            left = jnp.where(low, pltpu.roll(second, NY - 16, 1), first)
+            right, left = both(lambda z: q_ref[f, z], h)
+            if f < 3:
+                right = jnp.where(lane % 16 < 4, pltpu.roll(mask[h][0], NY - 4 - 4 * f, 1), right)
+                left = jnp.where(lane % 16 >= 12, pltpu.roll(mask[h][1], 12 - 4 * f, 1), left)
             ya_ref[f, h] = jnp.where(even, right, left)
             yb_ref[f, h] = jnp.where(even, left, right)
 
-    for f in range(NF):
-        field(f, lambda z, f=f: q_ref[f, z])
-    field(NF, lambda z: m_ref[z].astype(F32))
-
-
-def strip_kernel(par_ref, ya_ref, yb_ref, t_ref, xa_ref, xb_ref):
-    px = par_ref[0]
+
+def send_rows(px, layers, q_ref, m_ref, a_ref, b_refs):
+    def put(dst, bottom, first, count):
+        start = NX - DEPTH if bottom else 0
+        mstart = NX - DEPTH + 2 if bottom else 0
+        for z in range(count):
+            for f in range(NF):
+                dst[z * MSG + f * DEPTH:z * MSG + (f + 1) * DEPTH] = q_ref[f, first + z, start:start + DEPTH, :]
+            dst[z * MSG + NF * DEPTH:(z + 1) * MSG] = m_ref[first + z, mstart:mstart + DEPTH - 2, :].astype(F32)
+
+    def send(a_bottom):
+        put(a_ref, a_bottom, 0, layers)
+        part = layers // len(b_refs)
+        for i, b_ref in enumerate(b_refs):
+            put(b_ref, not a_bottom, i * part, part)
+
+    pl.when(px == 0)(lambda: send(True))
+    pl.when(px == 1)(lambda: send(False))
+
+
+def pack_x_kernel(par_ref, q_ref, m_ref, xa_ref, xb_ref, xb2_ref):
+    send_rows(par_ref[0], NZ, q_ref, m_ref, xa_ref, (xb_ref, xb2_ref))
+
+
+def strip_kernel(par_ref, ya_ref, yb_ref, t_ref, ts_ref, xa_ref, xb_ref):
     even = par_ref[1] == 0
-    low = lanes((NX, NY)) % 32 < 16
-    for f in range(NF + 1):
-        for h in range(2):
+    lane = lanes((NX, NY))
+    low = lane % 32 < 16
+    place = lane % 16
+
+    def put(h, left, right):
+        yield h, jnp.where(low, left, right)
+        yield h + 2, jnp.where(low, pltpu.roll(left, NY - 16, 1), pltpu.roll(right, 16, 1))
+
+    for h in range(2):
+        mleft = mright = jnp.zeros((NX, NY), F32)
+        for f in range(NF):
             a = ya_ref[f, h]
             b = yb_ref[f, h]
             left = jnp.where(even, b, a)
             right = jnp.where(even, a, b)
-            t_ref[f, h] = jnp.where(low, left, right)
-            t_ref[f, h + 2] = jnp.where(low, pltpu.roll(left, NY - 16, 1), pltpu.roll(right, 16, 1))
-
-    @pl.when(px == 0)
-    def _():
-        xa_ref[...] = t_ref[:, :, NX - DEPTH:, :]
-        xb_ref[...] = t_ref[:, :, :DEPTH, :]
-
-    @pl.when(px == 1)
-    def _():
-        xa_ref[...] = t_ref[:, :, :DEPTH, :]
-        xb_ref[...] = t_ref[:, :, NX - DEPTH:, :]
+            if f < 3:
+                mleft = jnp.where(place // 4 == f + 1, pltpu.roll(left, 4 + 4 * f, 1), mleft)
+                mright = jnp.where(place // 4 == f, pltpu.roll(right, NY - 12 + 4 * f, 1), mright)
+            for zi, value in put(h, left, right):
+                t_ref[f, zi] = value
+        for zi, value in put(h, mleft, mright):
+            ts_ref[zi] = value
+    send_rows(par_ref[0], 4, t_ref, ts_ref, xa_ref, (xb_ref,))
 
 
 def update(alpha, beta, center, around, base, solid):
@@ -164,7 +184,7 @@
     return high, (a - high.astype(F32)).astype(jnp.bfloat16)
 
 
-def main_kernel(par_ref, q_in, m_in, xa_ref, xb_ref, t_in, ca_ref, cb_ref, w_ref, ws_ref, out_ref,
+def main_kernel(par_ref, q_in, m_in, xa_ref, xb_ref, xb2_ref, t_in, ts_in, ca_ref, cb_ref, w_ref, ws_ref, out_ref,
                 q, s1, s2, solid, tq, t1, t2, tsolid, yd, ytd):
     px = par_ref[0]
 
@@ -172,25 +192,26 @@
         q[f, :, OWN:BOTTOM, :] = q_in[f]
         tq[f, 2:6, OWN:BOTTOM, :] = t_in[f]
     solid[:, OWN:BOTTOM, :] = m_in[...].astype(F32)
-    tsolid[:, OWN:BOTTOM, :] = t_in[NF]
-
-    def halos(top, bottom, ctop, cbottom):
-        q[:, :, TOP:OWN, :] = top[0:NF]
-        q[:, :, BOTTOM:BOTTOM + DEPTH, :] = bottom[0:NF]
-        solid[:, TOP:OWN, :] = top[NF]
-        solid[:, BOTTOM:BOTTOM + DEPTH, :] = bottom[NF]
-        tq[:, 2:6, TOP:OWN, :] = ctop[0:NF]
-        tq[:, 2:6, BOTTOM:BOTTOM + DEPTH, :] = cbottom[0:NF]
-        tsolid[:, TOP:OWN, :] = ctop[NF]
-        tsolid[:, BOTTOM:BOTTOM + DEPTH, :] = cbottom[NF]
-
-    @pl.when(px == 0)
-    def _():
-        halos(xb_ref, xa_ref, cb_ref, ca_ref)
-
-    @pl.when(px == 1)
-    def _():
-        halos(xa_ref, xb_ref, ca_ref, cb_ref)
+    tsolid[:, OWN:BOTTOM, :] = ts_in[...]
+
+    def halo(msgs, layers, shift, fields, mask, top):
+        row = TOP if top else BOTTOM
+        mrow = TOP + 2 if top else BOTTOM
+        part = layers // len(msgs)
+        for z in range(layers):
+            msg, at = msgs[z // part], z % part * MSG
+            for f in range(NF):
+                fields[f, z + shift, row:row + DEPTH, :] = msg[at + f * DEPTH:at + (f + 1) * DEPTH]
+            mask[z, mrow:mrow + DEPTH - 2, :] = msg[at + NF * DEPTH:at + MSG]
+
+    def halos(a_bottom):
+        halo((xa_ref,), NZ, 0, q, solid, not a_bottom)
+        halo((xb_ref, xb2_ref), NZ, 0, q, solid, a_bottom)
+        halo((ca_ref,), 4, 2, tq, tsolid, not a_bottom)
+        halo((cb_ref,), 4, 2, tq, tsolid, a_bottom)
+
+    pl.when(px == 0)(lambda: halos(True))
+    pl.when(px == 1)(lambda: halos(False))
 
     for f in range(NF):
         for r in range(0, ROWS, 8):
@@ -275,15 +296,16 @@
         stage(3 * step + 3, s2, t2, q, tq, q, tq, 1.0 / 3.0, 2.0 / 3.0)
 
 
-def call(kernel, outs, scratch=(), scalars=1, inputs=0):
+def call(kernel, outs, scratch=(), inputs=0, hbm=0, where=pltpu.HBM):
     vmem = pl.BlockSpec(memory_space=pltpu.VMEM)
+    specs = [pl.BlockSpec(memory_space=pltpu.SMEM)] + [pl.BlockSpec(memory_space=where)] * hbm + [vmem] * inputs
     return pl.pallas_call(
         kernel,
         out_shape=[jax.ShapeDtypeStruct(s, F32) for s in outs],
-        in_specs=[pl.BlockSpec(memory_space=pltpu.SMEM)] * scalars + [vmem] * inputs,
+        in_specs=specs,
         out_specs=[vmem] * len(outs),
-        scratch_shapes=[pltpu.VMEM(s, F32) for s in scratch],
-        compiler_params=pltpu.CompilerParams(vmem_limit_bytes=48 * 2 ** 20),
+        scratch_shapes=list(scratch),
+        compiler_params=pltpu.CompilerParams(vmem_limit_bytes=44 * 2 ** 20),
     )
 
 
@@ -295,24 +317,27 @@
 
     def body(fields, solid_mask):
         parity = jnp.stack([lax.axis_index("gx") % 2, lax.axis_index("gy") % 2]).astype(jnp.int32)
-        xmsg = (NF + 1, NZ, DEPTH, NY)
-        ymsg = (NF + 1, 2, NX, NY)
-        strip = (NF + 1, 4, NX, NY)
-        cmsg = (NF + 1, 4, DEPTH, NY)
-        xa, xb, ya, yb = call(pack_kernel, [xmsg, xmsg, ymsg, ymsg], inputs=2)(parity, fields, solid_mask)
-        xb = lax.ppermute(xb, "gx", pairs(nx, 1))
+        ymsg = (NF, 2, NX, NY)
+        own = [pltpu.VMEM((NF, NZ, NX, NY), F32), pltpu.VMEM((NZ, NX, NY), jnp.int32),
+               pltpu.SemaphoreType.DMA((NF + 1,))]
+        ya, yb = call(pack_y_kernel, [ymsg, ymsg], own, hbm=2)(parity, fields, solid_mask)
         yb = lax.ppermute(yb, "gy", pairs(ny, 1))
         ya = lax.ppermute(ya, "gy", pairs(ny, 0))
+        half = (NZ // 2 * MSG, NY)
+        xa, xb, xb2 = call(pack_x_kernel, [(NZ * MSG, NY), half, half], inputs=2)(parity, fields, solid_mask)
+        xb = lax.ppermute(xb, "gx", pairs(nx, 1))
+        xb2 = lax.ppermute(xb2, "gx", pairs(nx, 1))
         xa = lax.ppermute(xa, "gx", pairs(nx, 0))
-        t, ca, cb = call(strip_kernel, [strip, cmsg, cmsg], inputs=2)(parity, ya, yb)
+        t, ts, ca, cb = call(strip_kernel, [(NF, 4, NX, NY), (4, NX, NY), (4 * MSG, NY), (4 * MSG, NY)],
+                             inputs=2)(parity, ya, yb)
         cb = lax.ppermute(cb, "gx", pairs(nx, 1))
         ca = lax.ppermute(ca, "gx", pairs(nx, 0))
         wide = (NF, NZ, ROWS, NY)
         narrow = (NF, 8, ROWS, NY)
         scratch = [wide] * 3 + [(NZ, ROWS, NY)] + [narrow] * 3 + [(4, ROWS, NY)]
         scratch += [(NF, NZ, 56, 2 * NY), (NF, 4, 56, 2 * NY)]
-        out, = call(main_kernel, [(NF, NZ, NX, NY)], scratch, inputs=9)(
-            parity, fields, solid_mask, xa, xb, t, ca, cb, *y_weights())
+        out, = call(main_kernel, [(NF, NZ, NX, NY)], [pltpu.VMEM(s, F32) for s in scratch], inputs=11)(
+            parity, fields, solid_mask, xa, xb, xb2, t, ts, ca, cb, *y_weights())
         return out
 
     return jax.shard_map(

time: 63.1 us -> 57.8 us (0.916)
  waiting for transfers between devices: 17.4 us -> 9.58 us
  starting transfers between devices: 12.8 us -> 15.4 us
  Pallas kernels: 29.5 us -> 30.3 us
  local copies, waits for them, and re-layouts: 2.83 us -> 2.19 us
    ppermute x1, waiting for transfers between devices: 12.3 us -> 0.85 us  [body(): yb = lax.ppermute(yb, 'gy', pairs(ny, 1))]
    ppermute x0 -> x1, waiting for transfers between devices: none -> 5.09 us  [body(): xb2 = lax.ppermute(xb2, 'gx', pairs(nx, 1))]
    ppermute x1, waiting for transfers between devices: 5.01 us -> 2.54 us  [body(): cb = lax.ppermute(cb, 'gx', pairs(nx, 1))]
    ppermute x1, starting transfers between devices: 2.41 us -> 4.3 us  [body(): cb = lax.ppermute(cb, 'gx', pairs(nx, 1))]
    ppermute x0 -> x1, starting transfers between devices: none -> 1.27 us  [body(): xb2 = lax.ppermute(xb2, 'gx', pairs(nx, 1))]
    ppermute x1, waiting for transfers between devices: 0.01 us -> 1.1 us  [body(): xb = lax.ppermute(xb, 'gx', pairs(nx, 1))]
    ppermute x1, starting transfers between devices: 3.54 us -> 2.58 us  [body(): xb = lax.ppermute(xb, 'gx', pairs(nx, 1))]
    pallas_call x3 -> x4, Pallas kernels: 29.5 us -> 30.3 us  [the longest x1 27.2 us: body(): call(main_kernel, [(NF, NZ, NX, NY)], [pltpu.VMEM(s, F32) for s in scratc...]
  transfers between devices with their start and end apart: 6 -> 7, of which waited for: 3 -> 4; matrix products, arithmetic and copies ran while one was open for 1% -> 0% of each run, Pallas kernels for 1% -> 4%
where the time goes in v3:
time: 57.8 us; the launch traced here: 57.6 us
  Pallas kernels  30.3 us (52%)
  starting transfers between devices  15.4 us (27%)
  waiting for transfers between devices  9.58 us (17%)
  local copies, waits for them, and re-layouts  2.19 us (4%)
    pallas_call x1, Pallas kernels, body(): call(main_kernel, [(NF, NZ, NX, NY)], [pltpu.VMEM(s, F32) for s in scratc...  27.2 us
    ppermute x1, waiting for transfers between devices, body(): xb2 = lax.ppermute(xb2, 'gx', pairs(nx, 1))  5.09 us
    ppermute x1, starting transfers between devices, body(): yb = lax.ppermute(yb, 'gy', pairs(ny, 1))  4.98 us
    ppermute x1, starting transfers between devices, body(): cb = lax.ppermute(cb, 'gx', pairs(nx, 1))  4.3 us
    ppermute x1, starting transfers between devices, body(): xb = lax.ppermute(xb, 'gx', pairs(nx, 1))  2.58 us
    ppermute x1, waiting for transfers between devices, body(): cb = lax.ppermute(cb, 'gx', pairs(nx, 1))  2.54 us
    unnamed x10, local copies, waits for them, and re-layouts  2.19 us
    ppermute x1, starting transfers between devices, body(): ya = lax.ppermute(ya, 'gy', pairs(ny, 0))  2.08 us
  transfers between devices with their start and end apart: 7, of which 4 were waited for; matrix products, arithmetic and copies ran while one was open for 0% of the time, Pallas kernels for 4%

profile of v3, /device:TPU:0, one launch (start us, length us, event | category | flops | bytes accessed | tf_op | source)
XLA Modules:
  0.0 57.6 jit_solution(14011034605354337569)
XLA Ops:
  0.0 0.1 pad_add_fusion.par_ref
  0.1 0.0 copy-start
  0.1 1.2 %copy-done = f32[4,16,32,128]{3,2,1,0:T(8,128)S(1)} copy-done((f32[4,16,32,128]{3,2,1,0:T(8,128)S(1)}, f32[4,16,32,128]{3,2,1,0:T(8,128)}, u32[]{:S(2)}) %copy-start) | copy-done | bytes 1048600
  1.3 0.0 copy-start.2
  1.3 0.9 %copy-done.2 = s32[16,32,128]{2,1,0:T(8,128)S(1)} copy-done((s32[16,32,128]{2,1,0:T(8,128)S(1)}, s32[16,32,128]{2,1,0:T(8,128)}, u32[]{:S(2)}) %copy-start.2) | copy-done | bytes 262168
  2.3 0.0 copy-start.3
  2.3 0.0 copy-start.4
  2.3 0.6 %shard_map.46 = (f32[928,128]{1,0:T(8,128)S(1)}, f32[464,128]{1,0:T(8,128)S(1)}, f32[464,128]{1,0:T(8,128)S(1)}) custom-call(s32[2]{0:T(128)S(1)} %pad_add_fusion.par_ref, f32[4,16,32,128]{3,2,1,0:T(8,128)S(1)} %copy-done, s32[16,32,128]{2,1,0:T(8,128)S(1)} %copy-done.2), custom_call_target="tpu_custom_call" | custom-call | tf_op jit(solution)/shard_map/pallas_call | solution.py:327
  2.9 0.0 copy-start.1
  2.9 0.1 collective-permute-start
  3.0 1.7 %shard_map.47 = (f32[4,2,32,128]{3,2,1,0:T(8,128)S(1)}, f32[4,2,32,128]{3,2,1,0:T(8,128)S(1)}) custom-call(s32[2]{0:T(128)S(1)} %pad_add_fusion.par_ref, f32[4,16,32,128]{3,2,1,0:T(8,128)S(1)} %copy-done, s32[16,32,128]{2,1,0:T(8,128)S(1)} %copy-done.2), custom_call_target="tpu_custom_call" | custom-call | tf_op jit(solution)/shard_map/pallas_call | solution.py:323
  4.7 2.1 %collective-permute-start.3 = (f32[4,2,32,128]{3,2,1,0:T(8,128)S(1)}, f32[4,2,32,128]{3,2,1,0:T(8,128)S(1)}, u32[]{:S(2)}, u32[]{:S(2)}) collective-permute-start(f32[4,2,32,128]{3,2,1,0:T(8,128)S(1)} %get-tuple-element.17), channel_id=1, source_target_pairs={{0,1},{1,0},{2,3},{3,2},{4,5},{5,4},{6,7},{7,6},{8,9},{9,8},{10,11... | collective-permute-start | bytes 393224 | tf_op jit(solution)/shard_map/ppermute | solution.py:325
  6.8 5.0 %collective-permute-start.4 = (f32[4,2,32,128]{3,2,1,0:T(8,128)S(1)}, f32[4,2,32,128]{3,2,1,0:T(8,128)S(1)}, u32[]{:S(2)}, u32[]{:S(2)}) collective-permute-start(f32[4,2,32,128]{3,2,1,0:T(8,128)S(1)} %get-tuple-element.18), channel_id=1, source_target_pairs={{0,7},{1,2},{2,1},{3,4},{4,3},{5,6},{6,5},{7,0},{8,15},{9,10},{10,... | collective-permute-start | bytes 393224 | tf_op jit(solution)/shard_map/ppermute | solution.py:324
  11.8 2.6 %collective-permute-start.1 = (f32[464,128]{1,0:T(8,128)S(1)}, f32[464,128]{1,0:T(8,128)S(1)}, u32[]{:S(2)}, u32[]{:S(2)}) collective-permute-start(f32[464,128]{1,0:T(8,128)S(1)} %get-tuple-element.15), channel_id=1, source_target_pairs={{0,120},{8,16},{16,8},{24,32},{32,24},{40,48},{48,40},{56,64},{64,... | collective-permute-start | bytes 712712 | tf_op jit(solution)/shard_map/ppermute | solution.py:328
  14.4 1.3 %collective-permute-start.2 = (f32[464,128]{1,0:T(8,128)S(1)}, f32[464,128]{1,0:T(8,128)S(1)}, u32[]{:S(2)}, u32[]{:S(2)}) collective-permute-start(f32[464,128]{1,0:T(8,128)S(1)} %get-tuple-element.16), channel_id=1, source_target_pairs={{0,120},{8,16},{16,8},{24,32},{32,24},{40,48},{48,40},{56,64},{64,... | collective-permute-start | bytes 712712 | tf_op jit(solution)/shard_map/ppermute | solution.py:329
  15.6 0.0 collective-permute-done.3.ya_ref
  15.6 0.8 %collective-permute-done.4.yb_ref = f32[4,2,32,128]{3,2,1,0:T(8,128)S(1)} collective-permute-done((f32[4,2,32,128]{3,2,1,0:T(8,128)S(1)}, f32[4,2,32,128]{3,2,1,0:T(8,128)S(1)}, u32[]{:S(2)}, u32[]{:S(2)}) %collective-permute-start.4) | collective-permute-done | bytes 131104 | tf_op jit(solution)/shard_map/ppermute | solution.py:324
  16.5 0.8 %shard_map.48 = (f32[4,4,32,128]{3,2,1,0:T(8,128)S(1)}, f32[4,32,128]{2,1,0:T(8,128)S(1)}, f32[232,128]{1,0:T(8,128)S(1)}, f32[232,128]{1,0:T(8,128)S(1)}) custom-call(s32[2]{0:T(128)S(1)} %pad_add_fusion.par_ref, f32[4,2,32,128]{3,2,1,0:T(8,128)S(1)} %collective-permute-done.3.ya_ref, f32[4,2,32,128]{3,2,1,0:T(8,128)S(1)} %collective-permute-done.4.yb_ref), custom_call_target="tpu_custom_call" | custom-call | tf_op jit(solution)/shard_map/pallas_call | solution.py:331
  17.3 0.1 collective-permute-start.5
  17.4 4.3 %collective-permute-start.6 = (f32[232,128]{1,0:T(8,128)S(1)}, f32[232,128]{1,0:T(8,128)S(1)}, u32[]{:S(2)}, u32[]{:S(2)}) collective-permute-start(f32[232,128]{1,0:T(8,128)S(1)} %get-tuple-element.22), channel_id=1, source_target_pairs={{0,120},{8,16},{16,8},{24,32},{32,24},{40,48},{48,40},{56,64},{64,... | collective-permute-start | bytes 356360 | tf_op jit(solution)/shard_map/ppermute | solution.py:333
  21.7 1.1 %collective-permute-done.1.xb_ref = f32[464,128]{1,0:T(8,128)S(1)} collective-permute-done((f32[464,128]{1,0:T(8,128)S(1)}, f32[464,128]{1,0:T(8,128)S(1)}, u32[]{:S(2)}, u32[]{:S(2)}) %collective-permute-start.1) | collective-permute-done | bytes 237600 | tf_op jit(solution)/shard_map/ppermute | solution.py:328
  22.8 5.1 %collective-permute-done.2.xb2_ref = f32[464,128]{1,0:T(8,128)S(1)} collective-permute-done((f32[464,128]{1,0:T(8,128)S(1)}, f32[464,128]{1,0:T(8,128)S(1)}, u32[]{:S(2)}, u32[]{:S(2)}) %collective-permute-start.2) | collective-permute-done | bytes 237600 | tf_op jit(solution)/shard_map/ppermute | solution.py:329
  27.9 0.0 collective-permute-done.5.ca_ref
  27.9 2.5 %collective-permute-done.6.cb_ref = f32[232,128]{1,0:T(8,128)S(1)} collective-permute-done((f32[232,128]{1,0:T(8,128)S(1)}, f32[232,128]{1,0:T(8,128)S(1)}, u32[]{:S(2)}, u32[]{:S(2)}) %collective-permute-start.6) | collective-permute-done | bytes 118816 | tf_op jit(solution)/shard_map/ppermute | solution.py:333
  30.4 0.0 collective-permute-done.xa_ref
  30.4 0.0 copy-done.3
  30.4 0.0 copy-done.4
  30.4 0.0 copy-done.1
  30.5 27.2 %shard_map.49 = f32[4,16,32,128]{3,2,1,0:T(8,128)} custom-call(s32[2]{0:T(128)S(1)} %pad_add_fusion.par_ref, f32[4,16,32,128]{3,2,1,0:T(8,128)S(1)} %copy-done.1, s32[16,32,128]{2,1,0:T(8,128)S(1)} %copy-done.2, f32[928,128]{1,0:T(8,128)S(1)} %collective-permute-done.xa_ref, f32[464,128]{1,0:T(8,128)S(1)} %collective-permute-done.1.xb_ref, ...), custom_call_target="tpu_custom_call" | custom-call | tf_op jit(solution)/shard_map/pallas_call | solution.py:339
Async XLA Ops:
  0.1 1.2 %copy-start = (f32[4,16,32,128]{3,2,1,0:T(8,128)S(1)}, f32[4,16,32,128]{3,2,1,0:T(8,128)}, u32[]{:S(2)}) copy-start(f32[4,16,32,128]{3,2,1,0:T(8,128)} %q_in.1) | copy-start | bytes 3145732
  1.3 0.9 %copy-start.2 = (s32[16,32,128]{2,1,0:T(8,128)S(1)}, s32[16,32,128]{2,1,0:T(8,128)}, u32[]{:S(2)}) copy-start(s32[16,32,128]{2,1,0:T(8,128)} %m_in.1) | copy-start | bytes 786436
  2.3 28.2 %copy-start.3 = (bf16[4,512,256]{2,1,0:T(8,128)(2,1)S(1)}, bf16[4,512,256]{2,1,0:T(8,128)(2,1)}, u32[]{:S(2)}) copy-start(bf16[4,512,256]{2,1,0:T(8,128)(2,1)} %constant.30.clone.w_ref) | copy-start | bytes 3145732
  2.3 28.2 %copy-start.4 = (bf16[1280,256]{1,0:T(8,128)(2,1)S(1)}, bf16[1280,256]{1,0:T(8,128)(2,1)}, u32[]{:S(2)}) copy-start(bf16[1280,256]{1,0:T(8,128)(2,1)} %constant.31.clone.ws_ref) | copy-start | bytes 1966084
  2.9 27.5 %copy-start.1 = (f32[4,16,32,128]{3,2,1,0:T(8,128)S(1)}, f32[4,16,32,128]{3,2,1,0:T(8,128)}, u32[]{:S(2)}) copy-start(f32[4,16,32,128]{3,2,1,0:T(8,128)} %q_in.1) | copy-start | bytes 3145732
  2.9 27.5 %collective-permute-start = (f32[928,128]{1,0:T(8,128)S(1)}, f32[928,128]{1,0:T(8,128)S(1)}, u32[]{:S(2)}, u32[]{:S(2)}) collective-permute-start(f32[928,128]{1,0:T(8,128)S(1)} %get-tuple-element.14), channel_id=1, source_target_pairs={{0,8},{8,0},{16,24},{24,16},{32,40},{40,32},{48,56},{56,48},{64,72... | collective-permute-start | bytes 1425416 | tf_op jit(solution)/shard_map/ppermute | solution.py:330
  4.7 10.9 %collective-permute-start.3 = (f32[4,2,32,128]{3,2,1,0:T(8,128)S(1)}, f32[4,2,32,128]{3,2,1,0:T(8,128)S(1)}, u32[]{:S(2)}, u32[]{:S(2)}) collective-permute-start(f32[4,2,32,128]{3,2,1,0:T(8,128)S(1)} %get-tuple-element.17), channel_id=1, source_target_pairs={{0,1},{1,0},{2,3},{3,2},{4,5},{5,4},{6,7},{7,6},{8,9},{9,8},{10,11... | collective-permute-start | bytes 393224 | tf_op jit(solution)/shard_map/ppermute | solution.py:325
  6.8 9.7 %collective-permute-start.4 = (f32[4,2,32,128]{3,2,1,0:T(8,128)S(1)}, f32[4,2,32,128]{3,2,1,0:T(8,128)S(1)}, u32[]{:S(2)}, u32[]{:S(2)}) collective-permute-start(f32[4,2,32,128]{3,2,1,0:T(8,128)S(1)} %get-tuple-element.18), channel_id=1, source_target_pairs={{0,7},{1,2},{2,1},{3,4},{4,3},{5,6},{6,5},{7,0},{8,15},{9,10},{10,... | collective-permute-start | bytes 393224 | tf_op jit(solution)/shard_map/ppermute | solution.py:324
  11.8 11.0 %collective-permute-start.1 = (f32[464,128]{1,0:T(8,128)S(1)}, f32[464,128]{1,0:T(8,128)S(1)}, u32[]{:S(2)}, u32[]{:S(2)}) collective-permute-start(f32[464,128]{1,0:T(8,128)S(1)} %get-tuple-element.15), channel_id=1, source_target_pairs={{0,120},{8,16},{16,8},{24,32},{32,24},{40,48},{48,40},{56,64},{64,... | collective-permute-start | bytes 712712 | tf_op jit(solution)/shard_map/ppermute | solution.py:328
  14.4 13.5 %collective-permute-start.2 = (f32[464,128]{1,0:T(8,128)S(1)}, f32[464,128]{1,0:T(8,128)S(1)}, u32[]{:S(2)}, u32[]{:S(2)}) collective-permute-start(f32[464,128]{1,0:T(8,128)S(1)} %get-tuple-element.16), channel_id=1, source_target_pairs={{0,120},{8,16},{16,8},{24,32},{32,24},{40,48},{48,40},{56,64},{64,... | collective-permute-start | bytes 712712 | tf_op jit(solution)/shard_map/ppermute | solution.py:329
  17.3 10.6 %collective-permute-start.5 = (f32[232,128]{1,0:T(8,128)S(1)}, f32[232,128]{1,0:T(8,128)S(1)}, u32[]{:S(2)}, u32[]{:S(2)}) collective-permute-start(f32[232,128]{1,0:T(8,128)S(1)} %get-tuple-element.21), channel_id=1, source_target_pairs={{0,8},{8,0},{16,24},{24,16},{32,40},{40,32},{48,56},{56,48},{64,72... | collective-permute-start | bytes 356360 | tf_op jit(solution)/shard_map/ppermute | solution.py:334
  17.4 13.0 %collective-permute-start.6 = (f32[232,128]{1,0:T(8,128)S(1)}, f32[232,128]{1,0:T(8,128)S(1)}, u32[]{:S(2)}, u32[]{:S(2)}) collective-permute-start(f32[232,128]{1,0:T(8,128)S(1)} %get-tuple-element.22), channel_id=1, source_target_pairs={{0,120},{8,16},{16,8},{24,32},{32,24},{40,48},{48,40},{56,64},{64,... | collective-permute-start | bytes 356360 | tf_op jit(solution)/shard_map/ppermute | solution.py:333

commit v4 on v3

v4 whole, which is shorter than its diff:
```python
import functools

import jax
import jax.numpy as jnp
import numpy as np
from jax import lax
from jax.sharding import PartitionSpec as P
from jax.experimental import pallas as pl
from jax.experimental.pallas import tpu as pltpu

STAGES = 6
DEPTH = 2 * STAGES
viscosity = 0.05
penalty = 10.0
forcing = 0.5
sound_sq = 2.25
time_step = 0.2

NF, NZ, NX, NY = 4, 16, 32, 128
ROWS = 64
OWN = 16
TOP = OWN - DEPTH
BOTTOM = OWN + NX
MSG = (NF + 1) * DEPTH - 2
F32 = jnp.float32
FIRST = 8


def lanes(shape):
    return lax.broadcasted_iota(jnp.int32, shape, len(shape) - 1)


def send_rows(px, layers, q_ref, m_ref, a_ref, b_refs):
    def put(dst, bottom, first, count):
        start = NX - DEPTH if bottom else 0
        mstart = NX - DEPTH + 2 if bottom else 0
        for z in range(count):
            for f in range(NF):
                dst[z * MSG + f * DEPTH:z * MSG + (f + 1) * DEPTH] = q_ref[f, first + z, start:start + DEPTH, :]
            dst[z * MSG + NF * DEPTH:(z + 1) * MSG] = m_ref[first + z, mstart:mstart + DEPTH - 2, :].astype(F32)

    def send(a_bottom):
        put(a_ref, a_bottom, 0, layers)
        first = 0
        for b_ref in b_refs:
            count = b_ref.shape[0] // MSG
            put(b_ref, not a_bottom, first, count)
            first += count

    pl.when(px == 0)(lambda: send(True))
    pl.when(px == 1)(lambda: send(False))


def pack_kernel(par_ref, q_hbm, m_hbm, yb_ref, ya_ref, xa_ref, xb_ref, xb2_ref, q_ref, m_ref, sems):
    copies = [pltpu.make_async_copy(m_hbm, m_ref, sems.at[NF])]
    copies += [pltpu.make_async_copy(q_hbm.at[f], q_ref.at[f], sems.at[f]) for f in range(NF)]
    for copy in copies:
        copy.start()
    lane = lanes((NX, NY))
    group = lane // 32
    low = lane % 32 < 16
    even = par_ref[1] == 0

    def packed(load, zi):
        out = pltpu.roll(load(zi), 16, 1)
        for zq in range(1, 4):
            out = jnp.where(group == zq, pltpu.roll(load(4 * zq + zi), (16 + 32 * zq) % NY, 1), out)
        return out

    def both(load, h):
        first, second = packed(load, h), packed(load, h + 2)
        return (jnp.where(low, first, pltpu.roll(second, 16, 1)),
                jnp.where(low, pltpu.roll(second, NY - 16, 1), first))

    copies[0].wait()
    mask = [both(lambda z: m_ref[z].astype(F32), h) for h in range(2)]
    for f in range(NF):
        copies[1 + f].wait()
        for h in range(2):
            right, left = both(lambda z: q_ref[f, z], h)
            if f < 3:
                right = jnp.where(lane % 16 < 4, pltpu.roll(mask[h][0], NY - 4 - 4 * f, 1), right)
                left = jnp.where(lane % 16 >= 12, pltpu.roll(mask[h][1], 12 - 4 * f, 1), left)
            ya_ref[f, h] = jnp.where(even, right, left)
            yb_ref[f, h] = jnp.where(even, left, right)
    send_rows(par_ref[0], NZ, q_ref, m_ref, xa_ref, (xb_ref, xb2_ref))


def fetch_kernel(par_ref, w_hbm, ws_hbm, after_ref, w_ref, ws_ref, sems):
    copies = [pltpu.make_async_copy(w_hbm, w_ref, sems.at[0]), pltpu.make_async_copy(ws_hbm, ws_ref, sems.at[1])]
    for copy in copies:
        copy.start()
    for copy in copies:
        copy.wait()


def strip_kernel(par_ref, yb_ref, ya_ref, t_ref, ts_ref, xa_ref, xb_ref):
    even = par_ref[1] == 0
    lane = lanes((NX, NY))
    low = lane % 32 < 16
    place = lane % 16

    def put(h, left, right):
        yield h, jnp.where(low, left, right)
        yield h + 2, jnp.where(low, pltpu.roll(left, NY - 16, 1), pltpu.roll(right, 16, 1))

    for h in range(2):
        mleft = mright = jnp.zeros((NX, NY), F32)
        for f in range(NF):
            a = ya_ref[f, h]
            b = yb_ref[f, h]
            left = jnp.where(even, b, a)
            right = jnp.where(even, a, b)
            if f < 3:
                mleft = jnp.where(place // 4 == f + 1, pltpu.roll(left, 4 + 4 * f, 1), mleft)
                mright = jnp.where(place // 4 == f, pltpu.roll(right, NY - 12 + 4 * f, 1), mright)
            for zi, value in put(h, left, right):
                t_ref[f, zi] = value
        for zi, value in put(h, mleft, mright):
            ts_ref[zi] = value
    send_rows(par_ref[0], 4, t_ref, ts_ref, xa_ref, (xb_ref,))


def update(alpha, beta, center, around, base, solid):
    scale = beta * time_step * 2.0 / 3.0
    nu = beta * viscosity * time_step / 12.0
    u, v, w, p = center
    speed = [-scale * u, -scale * v, -scale * w]
    keep = beta - 90.0 * nu - (beta * time_step * penalty) * solid

    def first(plus, minus, plus2, minus2):
        return (plus - minus) - 0.125 * (plus2 - minus2)

    out = []
    x, z, dy, _ = around(3)
    p_diff = [first(*x), dy, first(*z)]
    divergence = None
    for k in range(3):
        x, z, dy, sy = around(k)
        diffs = [first(*x), dy, first(*z)]
        near = (x[0] + x[1]) + (z[0] + z[1])
        far = (x[2] + x[3]) + (z[2] + z[3])
        total = center[k] * keep - scale * p_diff[k]
        for d in range(3):
            total = total + speed[d] * diffs[d]
        divergence = diffs[k] if divergence is None else divergence + diffs[k]
        total = total + nu * ((16.0 * near - far) + sy)
        if k == 0:
            total = total + beta * time_step * forcing
        out.append(total)
    out.append(beta * p - (sound_sq * scale) * divergence)
    if alpha:
        out = [o + alpha * base(f) for f, o in enumerate(out)]
    return out


def y_weights():
    taps = [(1, 1.0, 16.0), (-1, -1.0, 16.0), (2, -0.125, -1.0), (-2, 0.125, -1.0)]
    wide = np.zeros((4, 512, 256), np.float32)
    strip = np.zeros((1280, 256), np.float32)
    for o, first, second in taps:
        for j in range(NY):
            for zq in range(4):
                c = j + o
                if 0 <= c < NY:
                    rows = (c, c + 128)
                else:
                    lane = 32 * zq + 16 + (c if c < 0 else c - NY)
                    rows = (256 + lane, 384 + lane)
                for r in rows:
                    wide[zq, r, j] = first
                    wide[zq, r, j + NY] = second
            g, place = j // 32, j % 32
            c = place - 16 if place < 16 else NY + place - 16
            left = place < 16
            c += o
            if c < -16 or c >= NY + 16:
                continue
            if (left and c < 0) or (not left and c >= NY):
                lane = 32 * g + 16 + (c if c < 0 else c - NY)
                rows = (lane, lane + 128)
            else:
                rows = (256 + 256 * g + c, 384 + 256 * g + c)
            for r in rows:
                strip[r, j] = first
                strip[r, j + NY] = second
    return jnp.asarray(wide, jnp.bfloat16), jnp.asarray(strip, jnp.bfloat16)


def split(a):
    high = a.astype(jnp.bfloat16)
    return high, (a - high.astype(F32)).astype(jnp.bfloat16)


EARLY = {1: (4, 3, 24), 2: (8, 2, 16)}
FRAME = {1: ((-12, 2), (28, 2)), 2: ((-8, 2), (24, 2)), 3: ((-6, 6),), 4: ((-4, 5),), 5: ((-2, 5),), 6: ((0, 4),)}
WEIGHTS = [(0.0, 1.0), (0.75, 0.25), (1.0 / 3.0, 2.0 / 3.0)]


def ghosts(strip, rows):
    for f in range(NF):
        for zi in range(4):
            strip[f, (zi + 6) % 8, rows, :] = pltpu.roll(strip[f, zi + 2, rows, :], 96 if zi < 2 else 32, 1)


def stage(number, windows, state, w_ref, ws_ref, yd, ytd, out_ref=None):
    q, s1, s2, solid, tq, t1, t2, tsolid = state
    section = (number - 1) % 3
    alpha, beta = WEIGHTS[section]
    cur, tcur = [(q, tq), (s1, t1), (s2, t2)][section]
    out, tout = [(s1, t1), (s2, t2), (q, tq)][section]
    base, tbase = q, tq
    windows = [(OWN + first, count) for first, count in windows]
    tiles = [first + 8 * i for first, count in windows for i in range(count)]
    rows = 8 * len(tiles)
    last = out_ref is not None

    def flat(ref, f, fields, z):
        parts = [ref[pl.ds(f, fields), pl.ds(z, 4), pl.ds(first, 8 * count), :] for first, count in windows]
        return split(jnp.concatenate(parts, axis=2).reshape(4 * fields * rows, NY))

    def along_y(fields, f, carry):
        t = flat(tcur, f, fields, 2)
        every = list(t)
        for zq in range(4):
            a = flat(cur, f, fields, 4 * zq)
            every += a
            y = jnp.dot(jnp.concatenate(a + t, axis=1), w_ref[zq], preferred_element_type=F32)
            yd[pl.ds(f, fields), 4 * zq:4 * zq + 4, 0:rows, :] = y.reshape(fields, 4, rows, 2 * NY)
        if not last:
            y = jnp.dot(jnp.concatenate(every, axis=1), ws_ref[...], preferred_element_type=F32)
            ytd[pl.ds(f, fields), :, 0:rows, :] = y.reshape(fields, 4, rows, 2 * NY)
        return carry

    if rows < 32:
        along_y(NF, 0, 0)
    else:
        lax.fori_loop(0, NF, functools.partial(along_y, 1), 0)

    def strips(half, zi, carry):
        for i, r in enumerate(tiles):
            rr, yr = pl.ds(r, 8), pl.ds(8 * i, 8)

            def around(f):
                x = [tcur[f, zi + 2, pl.ds(r + o, 8), :] for o in (1, -1, 2, -2)]
                z = [tcur[f, zi + 2 + o, rr, :] for o in (1, -1, 2, -2)]
                return x, z, ytd[f, zi, yr, 0:NY], ytd[f, zi, yr, NY:]

            center = [tcur[f, zi + 2, rr, :] for f in range(NF)]
            new = update(alpha, beta, center, around,
                         lambda f: tbase[f, zi + 2, rr, :], tsolid[zi, rr, :])
            for f in range(NF):
                tout[f, zi + 2, rr, :] = new[f]
                tout[f, zi + (6 if half == 0 else -2), rr, :] = pltpu.roll(new[f], 32 if half else 96, 1)
        return carry

    def main(z, carry):
        zs = [lax.rem(z + o, NZ) for o in (1, NZ - 1, 2, NZ - 2)]
        for i, r in enumerate(tiles):
            rr, yr = pl.ds(r, 8), pl.ds(8 * i, 8)

            def around(f):
                x = [cur[f, z, pl.ds(r + o, 8), :] for o in (1, -1, 2, -2)]
                zz = [cur[f, k, rr, :] for k in zs]
                return x, zz, yd[f, z, yr, 0:NY], yd[f, z, yr, NY:]

            center = [cur[f, z, rr, :] for f in range(NF)]
            new = update(alpha, beta, center, around,
                         lambda f: base[f, z, rr, :], solid[z, rr, :])
            for f in range(NF):
                if last:
                    out_ref[f, z, pl.ds(r - OWN, 8), :] = new[f]
                else:
                    out[f, z, rr, :] = new[f]
        return carry

    if not last:
        for half in range(2):
            lax.fori_loop(2 * half, 2 * half + 2, functools.partial(strips, half), 0)
    lax.fori_loop(0, NZ, main, 0)
    return out, tout


def split(a):
    high = a.astype(jnp.bfloat16)
    return high, (a - high.astype(F32)).astype(jnp.bfloat16)


def own_rows(q_in, m_in, t_in, ts_in, state):
    q, s1, s2, solid, tq, t1, t2, tsolid = state
    for f in range(NF):
        q[f, :, OWN:BOTTOM, :] = q_in[f]
        tq[f, 2:6, OWN:BOTTOM, :] = t_in[f]
    solid[:, OWN:BOTTOM, :] = m_in[...].astype(F32)
    tsolid[:, OWN:BOTTOM, :] = ts_in[...]


def early_kernel(par_ref, q_in, m_in, t_in, ts_in, w_ref, ws_ref, *refs):
    results, state, (yd, ytd) = refs[:2 * len(EARLY)], refs[2 * len(EARLY):-2], refs[-2:]
    own_rows(q_in, m_in, t_in, ts_in, state)
    for r in range(OWN, BOTTOM, 8):
        ghosts(state[4], pl.ds(r, 8))
    for number, (first, tiles, _) in EARLY.items():
        out, tout = stage(number, [(first, tiles)], state, w_ref, ws_ref, yd, ytd)
        rows = pl.ds(OWN + first, 8 * tiles)
        for f in range(NF):
            results[2 * number - 2][f] = out[f, :, rows, :]
            results[2 * number - 1][f] = tout[f, 2:6, rows, :]


def main_kernel(par_ref, q_in, m_in, xa_ref, xb_ref, xb2_ref, t_in, ts_in, ca_ref, cb_ref, w_ref, ws_ref, *refs):
    results, out_ref = refs[:2 * len(EARLY)], refs[2 * len(EARLY)]
    state, (yd, ytd) = refs[2 * len(EARLY) + 1:-2], refs[-2:]
    q, s1, s2, solid, tq, t1, t2, tsolid = state
    px = par_ref[0]
    own_rows(q_in, m_in, t_in, ts_in, state)

    def halo(msgs, shift, fields, mask, top):
        row = TOP if top else BOTTOM
        mrow = TOP + 2 if top else BOTTOM
        places = [(msg, i * MSG) for msg in msgs for i in range(msg.shape[0] // MSG)]
        for z, (msg, at) in enumerate(places):
            for f in range(NF):
                fields[f, z + shift, row:row + DEPTH, :] = msg[at + f * DEPTH:at + (f + 1) * DEPTH]
            mask[z, mrow:mrow + DEPTH - 2, :] = msg[at + NF * DEPTH:at + MSG]

    def halos(a_bottom):
        halo((xa_ref,), 0, q, solid, not a_bottom)
        halo((xb_ref, xb2_ref), 0, q, solid, a_bottom)
        halo((ca_ref,), 2, tq, tsolid, not a_bottom)
        halo((cb_ref,), 2, tq, tsolid, a_bottom)

    pl.when(px == 0)(lambda: halos(True))
    pl.when(px == 1)(lambda: halos(False))
    for r in range(0, ROWS, 8):
        ghosts(tq, pl.ds(r, 8))

    for number in range(1, STAGES + 1):
        out, tout = stage(number, FRAME[number], state, w_ref, ws_ref, yd, ytd,
                          out_ref if number == STAGES else None)
        if number in EARLY:
            first, _, valid = EARLY[number]
            rows = pl.ds(OWN + first, valid)
            for f in range(NF):
                out[f, :, rows, :] = results[2 * number - 2][f, :, 0:valid, :]
                tout[f, 2:6, rows, :] = results[2 * number - 1][f, :, 0:valid, :]
            for r in range(0, valid - valid % 8, 8):
                ghosts(tout, pl.ds(OWN + first + r, 8))
            if valid % 8:
                ghosts(tout, pl.ds(OWN + first + valid - 8, 8))


def call(kernel, outs, scratch=(), inputs=0, hbm=0, vmem_mib=32):
    vmem = pl.BlockSpec(memory_space=pltpu.VMEM)
    specs = [pl.BlockSpec(memory_space=pltpu.SMEM)] + [pl.BlockSpec(memory_space=pl.ANY)] * hbm + [vmem] * inputs
    return pl.pallas_call(
        kernel,
        out_shape=[s if isinstance(s, jax.ShapeDtypeStruct) else jax.ShapeDtypeStruct(s, F32) for s in outs],
        in_specs=specs,
        out_specs=[vmem] * len(outs),
        scratch_shapes=list(scratch),
        compiler_params=pltpu.CompilerParams(vmem_limit_bytes=vmem_mib * 2 ** 20),
    )


def solution(mesh):
    nx, ny = mesh.shape["gx"], mesh.shape["gy"]

    def pairs(count, parity):
        return [(i, (i + 1) % count if i % 2 == parity else (i - 1) % count) for i in range(count)]

    def body(fields, solid_mask):
        parity = jnp.stack([lax.axis_index("gx") % 2, lax.axis_index("gy") % 2]).astype(jnp.int32)
        ymsg = (NF, 2, NX, NY)
        parts = [(-(count * MSG) // 8 * -8, NY) for count in (FIRST, NZ - FIRST)]
        own = [jax.ShapeDtypeStruct(a.shape, a.dtype) for a in (fields, solid_mask)]
        yb, ya, xa, xb, xb2, q, m = call(
            pack_kernel, [ymsg, ymsg, (NZ * MSG, NY)] + parts + own, [pltpu.SemaphoreType.DMA((NF + 1,))],
            hbm=2, vmem_mib=32)(parity, fields, solid_mask)
        yb = lax.ppermute(yb, "gy", pairs(ny, 1))
        ya = lax.ppermute(ya, "gy", pairs(ny, 0))
        xb = lax.ppermute(xb, "gx", pairs(nx, 1))
        xb2 = lax.ppermute(xb2, "gx", pairs(nx, 1))
        xa = lax.ppermute(xa, "gx", pairs(nx, 0))
        t, ts, ca, cb = call(strip_kernel, [(NF, 4, NX, NY), (4, NX, NY), (4 * MSG, NY), (4 * MSG, NY)],
                             inputs=2)(parity, yb, ya)
        w = y_weights()
        w = call(fetch_kernel, [jax.ShapeDtypeStruct(a.shape, a.dtype) for a in w],
                 [pltpu.SemaphoreType.DMA((2,))], hbm=3)(parity, *w, cb)
        cb = lax.ppermute(cb, "gx", pairs(nx, 1))
        ca = lax.ppermute(ca, "gx", pairs(nx, 0))
        wide = (NF, NZ, ROWS, NY)
        narrow = (NF, 8, ROWS, NY)
        scratch = [wide] * 3 + [(NZ, ROWS, NY)] + [narrow] * 3 + [(4, ROWS, NY)]
        scratch += [(NF, NZ, 48, 2 * NY), (NF, 4, 48, 2 * NY)]
        scratch = [pltpu.VMEM(s, F32) for s in scratch]
        parts = []
        for _, tiles, _ in EARLY.values():
            parts += [(NF, NZ, 8 * tiles, NY), (NF, 4, 8 * tiles, NY)]
        early = call(early_kernel, parts, scratch, inputs=6, vmem_mib=32)(parity, q, m, t, ts, *w)
        out, = call(main_kernel, [(NF, NZ, NX, NY)], scratch, inputs=11 + len(parts), vmem_mib=32)(
            parity, q, m, xa, xb, xb2, t, ts, ca, cb, *w, *early)
        return out

    return jax.shard_map(
        body,
        mesh=mesh,
        in_specs=(P(None, None, "gx", "gy"), P(None, "gx", "gy")),
        out_specs=P(None, None, "gx", "gy"),
        check_vma=False,
    )
```

time: 57.8 us -> 54.7 us (0.946)
  waiting for transfers between devices: 9.58 us -> 4.06 us
  Pallas kernels: 30.3 us -> 33.2 us
  starting transfers between devices: 15.4 us -> 13.8 us
  local copies, waits for them, and re-layouts: 2.19 us -> 3.26 us
    ppermute x1, waiting for transfers between devices: 5.09 us -> 0.01 us  [body(): xb2 = lax.ppermute(xb2, 'gx', pairs(nx, 1))]
    pallas_call x3 -> x4, Pallas kernels: 29.5 us -> 32.4 us  [the longest x1 24.6 us: body(): call(main_kernel, [(NF, NZ, NX, NY)], scratch, inputs=11 + len(parts), vm...]
    ppermute x1, starting transfers between devices: 2.08 us -> 0.01 us  [body(): ya = lax.ppermute(ya, 'gy', pairs(ny, 0))]
    ppermute x1, starting transfers between devices: 4.98 us -> 6.66 us  [body(): yb = lax.ppermute(yb, 'gy', pairs(ny, 1))]
    ppermute x1, waiting for transfers between devices: 0.01 us -> 1.2 us  [body(): ya = lax.ppermute(ya, 'gy', pairs(ny, 0))]
    ppermute x1, starting transfers between devices: 4.3 us -> 3.14 us  [body(): cb = lax.ppermute(cb, 'gx', pairs(nx, 1))]
    ppermute x1, waiting for transfers between devices: 1.1 us -> 0.01 us  [body(): xb = lax.ppermute(xb, 'gx', pairs(nx, 1))]
    unnamed x10 -> x8, local copies, waits for them, and re-layouts: 2.19 us -> 3.26 us
  transfers between devices with their start and end apart: 7 -> 7, of which waited for: 4 -> 3; matrix products, arithmetic and copies ran while one was open for 0% -> 0% of each run, Pallas kernels for 4% -> 12%
where the time goes in v4:
time: 54.7 us; the launch traced here: 54.5 us
  Pallas kernels  33.2 us (61%)
  starting transfers between devices  13.8 us (25%)
  waiting for transfers between devices  4.06 us (7%)
  local copies, waits for them, and re-layouts  3.26 us (6%)
    pallas_call x1, Pallas kernels, body(): call(main_kernel, [(NF, NZ, NX, NY)], scratch, inputs=11 + len(parts), vm...  24.6 us
    ppermute x1, starting transfers between devices, body(): yb = lax.ppermute(yb, 'gy', pairs(ny, 1))  6.66 us
    pallas_call x1, Pallas kernels, body(): call(early_kernel, parts, scratch, inputs=6, vmem_mib=32)  5.16 us
    unnamed x8, local copies, waits for them, and re-layouts  3.26 us
    ppermute x1, starting transfers between devices, body(): cb = lax.ppermute(cb, 'gx', pairs(nx, 1))  3.14 us
    ppermute x1, starting transfers between devices, body(): xb = lax.ppermute(xb, 'gx', pairs(nx, 1))  2.8 us
    ppermute x1, waiting for transfers between devices, body(): cb = lax.ppermute(cb, 'gx', pairs(nx, 1))  2.36 us
    pallas_call x1, Pallas kernels, body(): call(pack_kernel, [ymsg, ymsg, (NZ * MSG, NY)] + parts + own, [pltpu.Sema...  1.78 us
  transfers between devices with their start and end apart: 7, of which 3 were waited for; matrix products, arithmetic and copies ran while one was open for 0% of the time, Pallas kernels for 12%

profile of v4, /device:TPU:0, one launch (start us, length us, event | category | flops | bytes accessed | tf_op | source)
XLA Modules:
  0.0 54.5 jit_solution(17107405821573234641)
XLA Ops:
  0.0 0.1 pad_add_fusion.par_ref
  0.1 0.0 copy-start
  0.1 1.2 %copy-done = f32[4,16,32,128]{3,2,1,0:T(8,128)S(1)} copy-done((f32[4,16,32,128]{3,2,1,0:T(8,128)S(1)}, f32[4,16,32,128]{3,2,1,0:T(8,128)}, u32[]{:S(2)}) %copy-start) | copy-done | bytes 1048600
  1.3 0.0 copy-start.3
  1.3 0.9 %copy-done.3 = s32[16,32,128]{2,1,0:T(8,128)S(1)} copy-done((s32[16,32,128]{2,1,0:T(8,128)S(1)}, s32[16,32,128]{2,1,0:T(8,128)}, u32[]{:S(2)}) %copy-start.3) | copy-done | bytes 262168
  2.3 0.0 copy-start.1
  2.3 1.8 %shard_map.46 = (f32[4,2,32,128]{3,2,1,0:T(8,128)S(1)}, f32[4,2,32,128]{3,2,1,0:T(8,128)S(1)}, f32[928,128]{1,0:T(8,128)S(1)}, f32[464,128]{1,0:T(8,128)S(1)}, f...) custom-call(s32[2]{0:T(128)S(1)} %pad_add_fusion.par_ref, ...), custom_call_target="tpu_custom_call" | custom-call | tf_op jit(solution)/shard_map/pallas_call | solution.py:377
  4.0 0.1 collective-permute-start
  4.1 6.7 %collective-permute-start.3 = (f32[4,2,32,128]{3,2,1,0:T(8,128)S(1)}, f32[4,2,32,128]{3,2,1,0:T(8,128)S(1)}, u32[]{:S(2)}, u32[]{:S(2)}) collective-permute-start(f32[4,2,32,128]{3,2,1,0:T(8,128)S(1)} %get-tuple-element.27), channel_id=1, source_target_pairs={{0,7},{1,2},{2,1},{3,4},{4,3},{5,6},{6,5},{7,0},{8,15},{9,10},{10,... | collective-permute-start | bytes 393224 | tf_op jit(solution)/shard_map/ppermute | solution.py:380
  10.8 0.0 collective-permute-start.4
  10.8 2.8 %collective-permute-start.1 = (f32[464,128]{1,0:T(8,128)S(1)}, f32[464,128]{1,0:T(8,128)S(1)}, u32[]{:S(2)}, u32[]{:S(2)}) collective-permute-start(f32[464,128]{1,0:T(8,128)S(1)} %get-tuple-element.25), channel_id=1, source_target_pairs={{0,120},{8,16},{16,8},{24,32},{32,24},{40,48},{48,40},{56,64},{64,... | collective-permute-start | bytes 712712 | tf_op jit(solution)/shard_map/ppermute | solution.py:382
  13.6 1.1 %collective-permute-start.2 = (f32[464,128]{1,0:T(8,128)S(1)}, f32[464,128]{1,0:T(8,128)S(1)}, u32[]{:S(2)}, u32[]{:S(2)}) collective-permute-start(f32[464,128]{1,0:T(8,128)S(1)} %get-tuple-element.26), channel_id=1, source_target_pairs={{0,120},{8,16},{16,8},{24,32},{32,24},{40,48},{48,40},{56,64},{64,... | collective-permute-start | bytes 712712 | tf_op jit(solution)/shard_map/ppermute | solution.py:383
  14.7 0.5 collective-permute-done.3.yb_ref
  15.1 1.2 %collective-permute-done.4.ya_ref = f32[4,2,32,128]{3,2,1,0:T(8,128)S(1)} collective-permute-done((f32[4,2,32,128]{3,2,1,0:T(8,128)S(1)}, f32[4,2,32,128]{3,2,1,0:T(8,128)S(1)}, u32[]{:S(2)}, u32[]{:S(2)}) %collective-permute-start.4) | collective-permute-done | bytes 131104 | tf_op jit(solution)/shard_map/ppermute | solution.py:381
  16.3 0.8 %shard_map.47 = (f32[4,4,32,128]{3,2,1,0:T(8,128)S(1)}, f32[4,32,128]{2,1,0:T(8,128)S(1)}, f32[232,128]{1,0:T(8,128)S(1)}, f32[232,128]{1,0:T(8,128)S(1)}) custom-call(s32[2]{0:T(128)S(1)} %pad_add_fusion.par_ref, f32[4,2,32,128]{3,2,1,0:T(8,128)S(1)} %collective-permute-done.3.yb_ref, f32[4,2,32,128]{3,2,1,0:T(8,128)S(1)} %collective-permute-done.4.ya_ref), custom_call_target="tpu_custom_call" | custom-call | tf_op jit(solution)/shard_map/pallas_call | solution.py:385
  17.2 0.1 collective-permute-start.5
  17.3 3.1 %collective-permute-start.6 = (f32[232,128]{1,0:T(8,128)S(1)}, f32[232,128]{1,0:T(8,128)S(1)}, u32[]{:S(2)}, u32[]{:S(2)}) collective-permute-start(f32[232,128]{1,0:T(8,128)S(1)} %get-tuple-element.32.after_ref), channel_id=1, source_target_pairs={{0,120},{8,16},{16,8},{24,32},{32,24},{40,48},{48,40},{56,64},{64,... | collective-permute-start | bytes 356360 | tf_op jit(solution)/shard_map/ppermute | solution.py:390
  20.4 0.0 copy-done.1
  20.4 0.0 copy-start.2
  20.4 1.1 %copy-done.2 = bf16[1280,256]{1,0:T(8,128)(2,1)S(1)} copy-done((bf16[1280,256]{1,0:T(8,128)(2,1)S(1)}, bf16[1280,256]{1,0:T(8,128)(2,1)}, u32[]{:S(2)}) %copy-start.2) | copy-done | bytes 655384
  21.5 0.8 %shard_map.48 = (bf16[4,512,256]{2,1,0:T(8,128)(2,1)S(1)}, bf16[1280,256]{1,0:T(8,128)(2,1)S(1)}) custom-call(s32[2]{0:T(128)S(1)} %pad_add_fusion.par_ref, bf16[4,512,256]{2,1,0:T(8,128)(2,1)S(1)} %copy-done.1, bf16[1280,256]{1,0:T(8,128)(2,1)S(1)} %copy-done.2, f32[232,128]{1,0:T(8,128)S(1)} %get-tuple-element.32.after_ref), custom_call_target="tpu_custom_call" | custom-call | tf_op jit(solution)/shard_map/pallas_call | solution.py:388
  22.3 5.2 %shard_map.49 = (f32[4,16,24,128]{3,2,1,0:T(8,128)S(1)}, f32[4,4,24,128]{3,2,1,0:T(8,128)S(1)}, f32[4,16,16,128]{3,2,1,0:T(8,128)S(1)}, f32[4,4,16,128]{3,2,1,0:T(8,128)S(1)}) custom-call(s32[2]{0:T(128)S(1)} %pad_add_fusion.par_ref, f32[4,16,32,128]{3,2,1,0:T(8,128)S(1)} %get-tuple-element.22.q_in, s32[16,32,128]{2,1,0:T(8,128)S(1)} %get-tuple-element.23.m_in, ...), custom_call_target="tpu_custom_call" | custom-call | tf_op jit(solution)/shard_map/pallas_call | solution.py:400
  27.5 0.0 collective-permute-done.1.xb_ref
  27.5 0.0 collective-permute-done.2.xb2_ref
  27.5 0.0 collective-permute-done.5.ca_ref
  27.5 2.4 %collective-permute-done.6.cb_ref = f32[232,128]{1,0:T(8,128)S(1)} collective-permute-done((f32[232,128]{1,0:T(8,128)S(1)}, f32[232,128]{1,0:T(8,128)S(1)}, u32[]{:S(2)}, u32[]{:S(2)}) %collective-permute-start.6) | collective-permute-done | bytes 118816 | tf_op jit(solution)/shard_map/ppermute | solution.py:390
  29.9 0.0 collective-permute-done.xa_ref
  29.9 24.6 %shard_map.50 = f32[4,16,32,128]{3,2,1,0:T(8,128)} custom-call(s32[2]{0:T(128)S(1)} %pad_add_fusion.par_ref, f32[4,16,32,128]{3,2,1,0:T(8,128)S(1)} %get-tuple-element.22.q_in, s32[16,32,128]{2,1,0:T(8,128)S(1)} %get-tuple-element.23.m_in, f32[928,128]{1,0:T(8,128)S(1)} %collective-permute-done.xa_ref, f32[464,128]{1,0:T(8,128)S(1)} %collective-permute-done.1.xb_ref, ...), custom_call_target="tpu_custom_call" | custom-call | tf_op jit(solution)/shard_map/pallas_call | solution.py:401
Async XLA Ops:
  0.1 1.2 %copy-start = (f32[4,16,32,128]{3,2,1,0:T(8,128)S(1)}, f32[4,16,32,128]{3,2,1,0:T(8,128)}, u32[]{:S(2)}) copy-start(f32[4,16,32,128]{3,2,1,0:T(8,128)} %q_hbm.1) | copy-start | bytes 3145732
  1.3 0.9 %copy-start.3 = (s32[16,32,128]{2,1,0:T(8,128)S(1)}, s32[16,32,128]{2,1,0:T(8,128)}, u32[]{:S(2)}) copy-start(s32[16,32,128]{2,1,0:T(8,128)} %m_hbm.1) | copy-start | bytes 786436
  2.3 18.1 %copy-start.1 = (bf16[4,512,256]{2,1,0:T(8,128)(2,1)S(1)}, bf16[4,512,256]{2,1,0:T(8,128)(2,1)}, u32[]{:S(2)}) copy-start(bf16[4,512,256]{2,1,0:T(8,128)(2,1)} %constant.30.clone.w_hbm) | copy-start | bytes 3145732
  4.0 25.9 %collective-permute-start = (f32[928,128]{1,0:T(8,128)S(1)}, f32[928,128]{1,0:T(8,128)S(1)}, u32[]{:S(2)}, u32[]{:S(2)}) collective-permute-start(f32[928,128]{1,0:T(8,128)S(1)} %get-tuple-element.24), channel_id=1, source_target_pairs={{0,8},{8,0},{16,24},{24,16},{32,40},{40,32},{48,56},{56,48},{64,72... | collective-permute-start | bytes 1425416 | tf_op jit(solution)/shard_map/ppermute | solution.py:384
  4.1 11.0 %collective-permute-start.3 = (f32[4,2,32,128]{3,2,1,0:T(8,128)S(1)}, f32[4,2,32,128]{3,2,1,0:T(8,128)S(1)}, u32[]{:S(2)}, u32[]{:S(2)}) collective-permute-start(f32[4,2,32,128]{3,2,1,0:T(8,128)S(1)} %get-tuple-element.27), channel_id=1, source_target_pairs={{0,7},{1,2},{2,1},{3,4},{4,3},{5,6},{6,5},{7,0},{8,15},{9,10},{10,... | collective-permute-start | bytes 393224 | tf_op jit(solution)/shard_map/ppermute | solution.py:380
  10.8 5.6 %collective-permute-start.4 = (f32[4,2,32,128]{3,2,1,0:T(8,128)S(1)}, f32[4,2,32,128]{3,2,1,0:T(8,128)S(1)}, u32[]{:S(2)}, u32[]{:S(2)}) collective-permute-start(f32[4,2,32,128]{3,2,1,0:T(8,128)S(1)} %get-tuple-element.28), channel_id=1, source_target_pairs={{0,1},{1,0},{2,3},{3,2},{4,5},{5,4},{6,7},{7,6},{8,9},{9,8},{10,11... | collective-permute-start | bytes 393224 | tf_op jit(solution)/shard_map/ppermute | solution.py:381
  10.8 16.7 %collective-permute-start.1 = (f32[464,128]{1,0:T(8,128)S(1)}, f32[464,128]{1,0:T(8,128)S(1)}, u32[]{:S(2)}, u32[]{:S(2)}) collective-permute-start(f32[464,128]{1,0:T(8,128)S(1)} %get-tuple-element.25), channel_id=1, source_target_pairs={{0,120},{8,16},{16,8},{24,32},{32,24},{40,48},{48,40},{56,64},{64,... | collective-permute-start | bytes 712712 | tf_op jit(solution)/shard_map/ppermute | solution.py:382
  13.6 13.9 %collective-permute-start.2 = (f32[464,128]{1,0:T(8,128)S(1)}, f32[464,128]{1,0:T(8,128)S(1)}, u32[]{:S(2)}, u32[]{:S(2)}) collective-permute-start(f32[464,128]{1,0:T(8,128)S(1)} %get-tuple-element.26), channel_id=1, source_target_pairs={{0,120},{8,16},{16,8},{24,32},{32,24},{40,48},{48,40},{56,64},{64,... | collective-permute-start | bytes 712712 | tf_op jit(solution)/shard_map/ppermute | solution.py:383
  17.2 10.4 %collective-permute-start.5 = (f32[232,128]{1,0:T(8,128)S(1)}, f32[232,128]{1,0:T(8,128)S(1)}, u32[]{:S(2)}, u32[]{:S(2)}) collective-permute-start(f32[232,128]{1,0:T(8,128)S(1)} %get-tuple-element.31), channel_id=1, source_target_pairs={{0,8},{8,0},{16,24},{24,16},{32,40},{40,32},{48,56},{56,48},{64,72... | collective-permute-start | bytes 356360 | tf_op jit(solution)/shard_map/ppermute | solution.py:391
  17.3 12.6 %collective-permute-start.6 = (f32[232,128]{1,0:T(8,128)S(1)}, f32[232,128]{1,0:T(8,128)S(1)}, u32[]{:S(2)}, u32[]{:S(2)}) collective-permute-start(f32[232,128]{1,0:T(8,128)S(1)} %get-tuple-element.32.after_ref), channel_id=1, source_target_pairs={{0,120},{8,16},{16,8},{24,32},{32,24},{40,48},{48,40},{56,64},{64,... | collective-permute-start | bytes 356360 | tf_op jit(solution)/shard_map/ppermute | solution.py:390
  20.4 1.1 %copy-start.2 = (bf16[1280,256]{1,0:T(8,128)(2,1)S(1)}, bf16[1280,256]{1,0:T(8,128)(2,1)}, u32[]{:S(2)}) copy-start(bf16[1280,256]{1,0:T(8,128)(2,1)} %constant.31.clone.ws_hbm) | copy-start | bytes 1966084

commit v5 on v4

--- a/solution.py
+++ b/solution.py
@@ -23,6 +23,7 @@
 BOTTOM = OWN + NX
 MSG = (NF + 1) * DEPTH - 2
 F32 = jnp.float32
+LAYERS = 4
 FIRST = 8
 
 
@@ -37,7 +38,7 @@
         for z in range(count):
             for f in range(NF):
                 dst[z * MSG + f * DEPTH:z * MSG + (f + 1) * DEPTH] = q_ref[f, first + z, start:start + DEPTH, :]
-            dst[z * MSG + NF * DEPTH:(z + 1) * MSG] = m_ref[first + z, mstart:mstart + DEPTH - 2, :].astype(F32)
+            dst[z * MSG + NF * DEPTH:(z + 1) * MSG] = m_ref[first + z, mstart:mstart + DEPTH - 2, :]
 
     def send(a_bottom):
         put(a_ref, a_bottom, 0, layers)
@@ -51,11 +52,7 @@
     pl.when(px == 1)(lambda: send(False))
 
 
-def pack_kernel(par_ref, q_hbm, m_hbm, yb_ref, ya_ref, xa_ref, xb_ref, xb2_ref, q_ref, m_ref, sems):
-    copies = [pltpu.make_async_copy(m_hbm, m_ref, sems.at[NF])]
-    copies += [pltpu.make_async_copy(q_hbm.at[f], q_ref.at[f], sems.at[f]) for f in range(NF)]
-    for copy in copies:
-        copy.start()
+def pack_kernel(par_ref, q_ref, m_ref, yb_ref, ya_ref, xa_ref, xb_ref, xb2_ref):
     lane = lanes((NX, NY))
     group = lane // 32
     low = lane % 32 < 16
@@ -72,10 +69,8 @@
         return (jnp.where(low, first, pltpu.roll(second, 16, 1)),
                 jnp.where(low, pltpu.roll(second, NY - 16, 1), first))
 
-    copies[0].wait()
-    mask = [both(lambda z: m_ref[z].astype(F32), h) for h in range(2)]
+    mask = [both(lambda z: m_ref[z], h) for h in range(2)]
     for f in range(NF):
-        copies[1 + f].wait()
         for h in range(2):
             right, left = both(lambda z: q_ref[f, z], h)
             if f < 3:
@@ -219,65 +214,71 @@
         parts = [ref[pl.ds(f, fields), pl.ds(z, 4), pl.ds(first, 8 * count), :] for first, count in windows]
         return split(jnp.concatenate(parts, axis=2).reshape(4 * fields * rows, NY))
 
-    def along_y(fields, f, carry):
+    def along_y(fields, f, carry, width=2 * NY):
         t = flat(tcur, f, fields, 2)
         every = list(t)
         for zq in range(4):
             a = flat(cur, f, fields, 4 * zq)
             every += a
-            y = jnp.dot(jnp.concatenate(a + t, axis=1), w_ref[zq], preferred_element_type=F32)
-            yd[pl.ds(f, fields), 4 * zq:4 * zq + 4, 0:rows, :] = y.reshape(fields, 4, rows, 2 * NY)
+            y = jnp.dot(jnp.concatenate(a + t, axis=1), w_ref[zq, :, 0:width], preferred_element_type=F32)
+            yd[pl.ds(f, fields), 4 * zq:4 * zq + 4, 0:rows, 0:width] = y.reshape(fields, 4, rows, width)
         if not last:
-            y = jnp.dot(jnp.concatenate(every, axis=1), ws_ref[...], preferred_element_type=F32)
-            ytd[pl.ds(f, fields), :, 0:rows, :] = y.reshape(fields, 4, rows, 2 * NY)
+            y = jnp.dot(jnp.concatenate(every, axis=1), ws_ref[:, 0:width], preferred_element_type=F32)
+            ytd[pl.ds(f, fields), :, 0:rows, 0:width] = y.reshape(fields, 4, rows, width)
         return carry
 
     if rows < 32:
         along_y(NF, 0, 0)
     else:
-        lax.fori_loop(0, NF, functools.partial(along_y, 1), 0)
-
-    def strips(half, zi, carry):
+        lax.fori_loop(0, 3, functools.partial(along_y, 1), 0)
+        along_y(1, 3, 0, NY)
+
+    def strips(half):
+        zi = 2 * half
+        here = slice(zi + 2, zi + 4)
         for i, r in enumerate(tiles):
             rr, yr = pl.ds(r, 8), pl.ds(8 * i, 8)
 
             def around(f):
-                x = [tcur[f, zi + 2, pl.ds(r + o, 8), :] for o in (1, -1, 2, -2)]
-                z = [tcur[f, zi + 2 + o, rr, :] for o in (1, -1, 2, -2)]
-                return x, z, ytd[f, zi, yr, 0:NY], ytd[f, zi, yr, NY:]
-
-            center = [tcur[f, zi + 2, rr, :] for f in range(NF)]
+                planes = [tcur[f, zi + k, rr, :] for k in range(6)]
+                x = [tcur[f, here, pl.ds(r + o, 8), :] for o in (1, -1, 2, -2)]
+                z = [jnp.stack(planes[2 + o:4 + o]) for o in (1, -1, 2, -2)]
+                return x, z, ytd[f, zi:zi + 2, yr, 0:NY], ytd[f, zi:zi + 2, yr, NY:]
+
+            center = [tcur[f, here, rr, :] for f in range(NF)]
             new = update(alpha, beta, center, around,
-                         lambda f: tbase[f, zi + 2, rr, :], tsolid[zi, rr, :])
+                         lambda f: tbase[f, here, rr, :], tsolid[zi:zi + 2, rr, :])
             for f in range(NF):
-                tout[f, zi + 2, rr, :] = new[f]
-                tout[f, zi + (6 if half == 0 else -2), rr, :] = pltpu.roll(new[f], 32 if half else 96, 1)
-        return carry
-
-    def main(z, carry):
-        zs = [lax.rem(z + o, NZ) for o in (1, NZ - 1, 2, NZ - 2)]
+                tout[f, here, rr, :] = new[f]
+                for k in range(2):
+                    tout[f, zi + k + (6 if half == 0 else -2), rr, :] = pltpu.roll(new[f][k], 32 if half else 96, 1)
+
+    def main(step, carry):
+        z = LAYERS * step
+        here = pl.ds(z, LAYERS)
+        zs = [lax.rem(z + NZ + o, NZ) for o in range(-2, LAYERS + 2)]
         for i, r in enumerate(tiles):
             rr, yr = pl.ds(r, 8), pl.ds(8 * i, 8)
-
             def around(f):
-                x = [cur[f, z, pl.ds(r + o, 8), :] for o in (1, -1, 2, -2)]
-                zz = [cur[f, k, rr, :] for k in zs]
-                return x, zz, yd[f, z, yr, 0:NY], yd[f, z, yr, NY:]
-
-            center = [cur[f, z, rr, :] for f in range(NF)]
+                planes = [cur[f, k, rr, :] for k in zs]
+                x = [cur[f, here, pl.ds(r + o, 8), :] for o in (1, -1, 2, -2)]
+                zz = [jnp.stack(planes[2 + o:2 + o + LAYERS]) for o in (1, -1, 2, -2)]
+                return x, zz, yd[f, here, yr, 0:NY], yd[f, here, yr, NY:]
+
+            center = [cur[f, here, rr, :] for f in range(NF)]
             new = update(alpha, beta, center, around,
-                         lambda f: base[f, z, rr, :], solid[z, rr, :])
+                         lambda f: base[f, here, rr, :], solid[here, rr, :])
             for f in range(NF):
                 if last:
-                    out_ref[f, z, pl.ds(r - OWN, 8), :] = new[f]
+                    out_ref[f, here, pl.ds(r - OWN, 8), :] = new[f]
                 else:
-                    out[f, z, rr, :] = new[f]
+                    out[f, here, rr, :] = new[f]
         return carry
 
     if not last:
         for half in range(2):
-            lax.fori_loop(2 * half, 2 * half + 2, functools.partial(strips, half), 0)
-    lax.fori_loop(0, NZ, main, 0)
+            strips(half)
+    lax.fori_loop(0, NZ // LAYERS, main, 0)
     return out, tout
 
 
@@ -291,7 +292,7 @@
     for f in range(NF):
         q[f, :, OWN:BOTTOM, :] = q_in[f]
         tq[f, 2:6, OWN:BOTTOM, :] = t_in[f]
-    solid[:, OWN:BOTTOM, :] = m_in[...].astype(F32)
+    solid[:, OWN:BOTTOM, :] = m_in[...]
     tsolid[:, OWN:BOTTOM, :] = ts_in[...]
 
 
@@ -373,10 +374,8 @@
         parity = jnp.stack([lax.axis_index("gx") % 2, lax.axis_index("gy") % 2]).astype(jnp.int32)
         ymsg = (NF, 2, NX, NY)
         parts = [(-(count * MSG) // 8 * -8, NY) for count in (FIRST, NZ - FIRST)]
-        own = [jax.ShapeDtypeStruct(a.shape, a.dtype) for a in (fields, solid_mask)]
-        yb, ya, xa, xb, xb2, q, m = call(
-            pack_kernel, [ymsg, ymsg, (NZ * MSG, NY)] + parts + own, [pltpu.SemaphoreType.DMA((NF + 1,))],
-            hbm=2, vmem_mib=32)(parity, fields, solid_mask)
+        q, m = fields, solid_mask.astype(F32)
+        yb, ya, xa, xb, xb2 = call(pack_kernel, [ymsg, ymsg, (NZ * MSG, NY)] + parts, inputs=2)(parity, q, m)
         yb = lax.ppermute(yb, "gy", pairs(ny, 1))
         ya = lax.ppermute(ya, "gy", pairs(ny, 0))
         xb = lax.ppermute(xb, "gx", pairs(nx, 1))

time: 54.7 us -> 52.2 us (0.954)
  Pallas kernels: 33.2 us -> 29.5 us
  waiting for transfers between devices: 4.06 us -> 5.2 us
  other arithmetic: 0.07 us -> 1.04 us
  local copies, waits for them, and re-layouts: 3.26 us -> 2.32 us
    pallas_call x1, Pallas kernels: 24.6 us -> 22.1 us  [body(): call(main_kernel, [(NF, NZ, NX, NY)], scratch, inputs=11 + len(parts), vm...]
    pallas_call x1, Pallas kernels: 5.16 us -> 4.03 us  [body(): call(early_kernel, parts, scratch, inputs=6, vmem_mib=32)]
    convert_element_type x0 -> x1, other arithmetic: none -> 0.97 us  [body(): q, m = (fields, solid_mask.astype(F32))]
    ppermute x1, waiting for transfers between devices: 0.01 us -> 0.96 us  [body(): xb2 = lax.ppermute(xb2, 'gx', pairs(nx, 1))]
    unnamed x8, local copies, waits for them, and re-layouts: 3.26 us -> 2.32 us
  transfers between devices with their start and end apart: 7 -> 7, of which waited for: 3 -> 4; matrix products, arithmetic and copies ran while one was open for 0% -> 0% of each run, Pallas kernels for 12% -> 11%
where the time goes in v5:
time: 52.2 us; the launch traced here: 52 us
  Pallas kernels  29.5 us (57%)
  starting transfers between devices  13.8 us (26%)
  waiting for transfers between devices  5.2 us (10%)
  local copies, waits for them, and re-layouts  2.32 us (4%)
  other arithmetic  1.04 us (2%)
    pallas_call x1, Pallas kernels, body(): call(main_kernel, [(NF, NZ, NX, NY)], scratch, inputs=11 + len(parts), vm...  22.1 us
    ppermute x1, starting transfers between devices, body(): yb = lax.ppermute(yb, 'gy', pairs(ny, 1))  6.66 us
    pallas_call x1, Pallas kernels, body(): call(early_kernel, parts, scratch, inputs=6, vmem_mib=32)  4.03 us
    ppermute x1, starting transfers between devices, body(): cb = lax.ppermute(cb, 'gx', pairs(nx, 1))  3.14 us
    ppermute x1, starting transfers between devices, body(): xb = lax.ppermute(xb, 'gx', pairs(nx, 1))  2.8 us
    ppermute x1, waiting for transfers between devices, body(): cb = lax.ppermute(cb, 'gx', pairs(nx, 1))  2.54 us
    unnamed x8, local copies, waits for them, and re-layouts  2.32 us
    pallas_call x1, Pallas kernels, body(): call(pack_kernel, [ymsg, ymsg, (NZ * MSG, NY)] + parts, inputs=2)  1.66 us
  transfers between devices with their start and end apart: 7, of which 4 were waited for; matrix products, arithmetic and copies ran while one was open for 0% of the time, Pallas kernels for 11%

profile of v5, /device:TPU:0, one launch (start us, length us, event | category | flops | bytes accessed | tf_op | source)
XLA Modules:
  0.0 52.0 jit_solution(48846097081496580)
XLA Ops:
  0.0 1.0 %convert_element_type.3.m_ref.m_in = f32[16,32,128]{2,1,0:T(8,128)S(1)} convert(s32[16,32,128]{2,1,0:T(8,128)} %param.5) | non-fusion elementwise | flops 65536 | bytes 524288 | tf_op jit(solution)/shard_map/convert_element_type | solution.py:377
  1.0 0.1 pad_add_fusion.par_ref
  1.1 0.0 copy-start
  1.1 1.2 %copy-done = f32[4,16,32,128]{3,2,1,0:T(8,128)S(1)} copy-done((f32[4,16,32,128]{3,2,1,0:T(8,128)S(1)}, f32[4,16,32,128]{3,2,1,0:T(8,128)}, u32[]{:S(2)}) %copy-start) | copy-done | bytes 1048600
  2.3 0.0 copy-start.2
  2.3 1.7 %shard_map.46 = (f32[4,2,32,128]{3,2,1,0:T(8,128)S(1)}, f32[4,2,32,128]{3,2,1,0:T(8,128)S(1)}, f32[928,128]{1,0:T(8,128)S(1)}, f32[464,128]{1,0:T(8,128)S(1)}, f32[464,128]{1,0:T(8,128)S(1)}) custom-call(s32[2]{0:T(128)S(1)} %pad_add_fusion.par_ref, f32[4,16,32,128]{3,2,1,0:T(8,128)S(1)} %copy-done, f32[16,32,128]{2,1,0:T(8,128)S(1)} %convert_element_type.3.m_ref.m_in), custom_call_target="tpu_custom_call" | custom-call | tf_op jit(solution)/shard_map/pallas_call | solution.py:378
  4.0 0.1 collective-permute-start
  4.1 6.7 %collective-permute-start.3 = (f32[4,2,32,128]{3,2,1,0:T(8,128)S(1)}, f32[4,2,32,128]{3,2,1,0:T(8,128)S(1)}, u32[]{:S(2)}, u32[]{:S(2)}) collective-permute-start(f32[4,2,32,128]{3,2,1,0:T(8,128)S(1)} %get-tuple-element.23), channel_id=1, source_target_pairs={{0,7},{1,2},{2,1},{3,4},{4,3},{5,6},{6,5},{7,0},{8,15},{9,10},{10,... | collective-permute-start | bytes 393224 | tf_op jit(solution)/shard_map/ppermute | solution.py:379
  10.7 0.0 collective-permute-start.4
  10.7 2.8 %collective-permute-start.1 = (f32[464,128]{1,0:T(8,128)S(1)}, f32[464,128]{1,0:T(8,128)S(1)}, u32[]{:S(2)}, u32[]{:S(2)}) collective-permute-start(f32[464,128]{1,0:T(8,128)S(1)} %get-tuple-element.21), channel_id=1, source_target_pairs={{0,120},{8,16},{16,8},{24,32},{32,24},{40,48},{48,40},{56,64},{64,... | collective-permute-start | bytes 712712 | tf_op jit(solution)/shard_map/ppermute | solution.py:381
  13.5 0.0 copy-start.1
  13.5 1.1 %collective-permute-start.2 = (f32[464,128]{1,0:T(8,128)S(1)}, f32[464,128]{1,0:T(8,128)S(1)}, u32[]{:S(2)}, u32[]{:S(2)}) collective-permute-start(f32[464,128]{1,0:T(8,128)S(1)} %get-tuple-element.22), channel_id=1, source_target_pairs={{0,120},{8,16},{16,8},{24,32},{32,24},{40,48},{48,40},{56,64},{64,... | collective-permute-start | bytes 712712 | tf_op jit(solution)/shard_map/ppermute | solution.py:382
  14.6 0.5 collective-permute-done.3.yb_ref
  15.1 1.2 %collective-permute-done.4.ya_ref = f32[4,2,32,128]{3,2,1,0:T(8,128)S(1)} collective-permute-done((f32[4,2,32,128]{3,2,1,0:T(8,128)S(1)}, f32[4,2,32,128]{3,2,1,0:T(8,128)S(1)}, u32[]{:S(2)}, u32[]{:S(2)}) %collective-permute-start.4) | collective-permute-done | bytes 131104 | tf_op jit(solution)/shard_map/ppermute | solution.py:380
  16.3 0.8 %shard_map.47 = (f32[4,4,32,128]{3,2,1,0:T(8,128)S(1)}, f32[4,32,128]{2,1,0:T(8,128)S(1)}, f32[232,128]{1,0:T(8,128)S(1)}, f32[232,128]{1,0:T(8,128)S(1)}) custom-call(s32[2]{0:T(128)S(1)} %pad_add_fusion.par_ref, f32[4,2,32,128]{3,2,1,0:T(8,128)S(1)} %collective-permute-done.3.yb_ref, f32[4,2,32,128]{3,2,1,0:T(8,128)S(1)} %collective-permute-done.4.ya_ref), custom_call_target="tpu_custom_call" | custom-call | tf_op jit(solution)/shard_map/pallas_call | solution.py:384
  17.1 0.1 collective-permute-start.5
  17.2 3.1 %collective-permute-start.6 = (f32[232,128]{1,0:T(8,128)S(1)}, f32[232,128]{1,0:T(8,128)S(1)}, u32[]{:S(2)}, u32[]{:S(2)}) collective-permute-start(f32[232,128]{1,0:T(8,128)S(1)} %get-tuple-element.28.after_ref), channel_id=1, source_target_pairs={{0,120},{8,16},{16,8},{24,32},{32,24},{40,48},{48,40},{56,64},{64,... | collective-permute-start | bytes 356360 | tf_op jit(solution)/shard_map/ppermute | solution.py:389
  20.3 0.0 copy-done.2
  20.3 0.0 copy-start.3
  20.3 1.1 %copy-done.3 = bf16[1280,256]{1,0:T(8,128)(2,1)S(1)} copy-done((bf16[1280,256]{1,0:T(8,128)(2,1)S(1)}, bf16[1280,256]{1,0:T(8,128)(2,1)}, u32[]{:S(2)}) %copy-start.3) | copy-done | bytes 655384
  21.4 0.8 %shard_map.48 = (bf16[4,512,256]{2,1,0:T(8,128)(2,1)S(1)}, bf16[1280,256]{1,0:T(8,128)(2,1)S(1)}) custom-call(s32[2]{0:T(128)S(1)} %pad_add_fusion.par_ref, bf16[4,512,256]{2,1,0:T(8,128)(2,1)S(1)} %copy-done.2, bf16[1280,256]{1,0:T(8,128)(2,1)S(1)} %copy-done.3, f32[232,128]{1,0:T(8,128)S(1)} %get-tuple-element.28.after_ref), custom_call_target="tpu_custom_call" | custom-call | tf_op jit(solution)/shard_map/pallas_call | solution.py:387
  22.3 0.0 copy-done.1
  22.3 4.0 %shard_map.49 = (f32[4,16,24,128]{3,2,1,0:T(8,128)S(1)}, f32[4,4,24,128]{3,2,1,0:T(8,128)S(1)}, f32[4,16,16,128]{3,2,1,0:T(8,128)S(1)}, f32[4,4,16,128]{3,2,1,0:T(8,128)S(1)}) custom-call(s32[2]{0:T(128)S(1)} %pad_add_fusion.par_ref, f32[4,16,32,128]{3,2,1,0:T(8,128)S(1)} %copy-done.1, f32[16,32,128]{2,1,0:T(8,128)S(1)} %convert_element_type.3.m_ref.m_in, ...), custom_call_target="tpu_custom_call" | custom-call | tf_op jit(solution)/shard_map/pallas_call | solution.py:399
  26.3 0.0 collective-permute-done.1.xb_ref
  26.3 1.0 %collective-permute-done.2.xb2_ref = f32[464,128]{1,0:T(8,128)S(1)} collective-permute-done((f32[464,128]{1,0:T(8,128)S(1)}, f32[464,128]{1,0:T(8,128)S(1)}, u32[]{:S(2)}, u32[]{:S(2)}) %collective-permute-start.2) | collective-permute-done | bytes 237600 | tf_op jit(solution)/shard_map/ppermute | solution.py:382
  27.3 0.0 collective-permute-done.5.ca_ref
  27.3 2.5 %collective-permute-done.6.cb_ref = f32[232,128]{1,0:T(8,128)S(1)} collective-permute-done((f32[232,128]{1,0:T(8,128)S(1)}, f32[232,128]{1,0:T(8,128)S(1)}, u32[]{:S(2)}, u32[]{:S(2)}) %collective-permute-start.6) | collective-permute-done | bytes 118816 | tf_op jit(solution)/shard_map/ppermute | solution.py:389
  29.8 0.0 collective-permute-done.xa_ref
  29.8 22.1 %shard_map.50 = f32[4,16,32,128]{3,2,1,0:T(8,128)} custom-call(s32[2]{0:T(128)S(1)} %pad_add_fusion.par_ref, f32[4,16,32,128]{3,2,1,0:T(8,128)S(1)} %copy-done.1, f32[16,32,128]{2,1,0:T(8,128)S(1)} %convert_element_type.3.m_ref.m_in, f32[928,128]{1,0:T(8,128)S(1)} %collective-permute-done.xa_ref, f32[464,128]{1,0:T(8,128)S(1)} %collective-permute-done.1.xb_ref, ...), custom_call_target="tpu_custom_call" | custom-call | tf_op jit(solution)/shard_map/pallas_call | solution.py:400
Async XLA Ops:
  1.1 1.2 %copy-start = (f32[4,16,32,128]{3,2,1,0:T(8,128)S(1)}, f32[4,16,32,128]{3,2,1,0:T(8,128)}, u32[]{:S(2)}) copy-start(f32[4,16,32,128]{3,2,1,0:T(8,128)} %q_in.3) | copy-start | bytes 3145732
  2.3 18.0 %copy-start.2 = (bf16[4,512,256]{2,1,0:T(8,128)(2,1)S(1)}, bf16[4,512,256]{2,1,0:T(8,128)(2,1)}, u32[]{:S(2)}) copy-start(bf16[4,512,256]{2,1,0:T(8,128)(2,1)} %constant.30.clone.w_hbm) | copy-start | bytes 3145732
  4.0 25.9 %collective-permute-start = (f32[928,128]{1,0:T(8,128)S(1)}, f32[928,128]{1,0:T(8,128)S(1)}, u32[]{:S(2)}, u32[]{:S(2)}) collective-permute-start(f32[928,128]{1,0:T(8,128)S(1)} %get-tuple-element.20), channel_id=1, source_target_pairs={{0,8},{8,0},{16,24},{24,16},{32,40},{40,32},{48,56},{56,48},{64,72... | collective-permute-start | bytes 1425416 | tf_op jit(solution)/shard_map/ppermute | solution.py:383
  4.1 11.0 %collective-permute-start.3 = (f32[4,2,32,128]{3,2,1,0:T(8,128)S(1)}, f32[4,2,32,128]{3,2,1,0:T(8,128)S(1)}, u32[]{:S(2)}, u32[]{:S(2)}) collective-permute-start(f32[4,2,32,128]{3,2,1,0:T(8,128)S(1)} %get-tuple-element.23), channel_id=1, source_target_pairs={{0,7},{1,2},{2,1},{3,4},{4,3},{5,6},{6,5},{7,0},{8,15},{9,10},{10,... | collective-permute-start | bytes 393224 | tf_op jit(solution)/shard_map/ppermute | solution.py:379
  10.7 5.6 %collective-permute-start.4 = (f32[4,2,32,128]{3,2,1,0:T(8,128)S(1)}, f32[4,2,32,128]{3,2,1,0:T(8,128)S(1)}, u32[]{:S(2)}, u32[]{:S(2)}) collective-permute-start(f32[4,2,32,128]{3,2,1,0:T(8,128)S(1)} %get-tuple-element.24), channel_id=1, source_target_pairs={{0,1},{1,0},{2,3},{3,2},{4,5},{5,4},{6,7},{7,6},{8,9},{9,8},{10,11... | collective-permute-start | bytes 393224 | tf_op jit(solution)/shard_map/ppermute | solution.py:380
  10.7 15.6 %collective-permute-start.1 = (f32[464,128]{1,0:T(8,128)S(1)}, f32[464,128]{1,0:T(8,128)S(1)}, u32[]{:S(2)}, u32[]{:S(2)}) collective-permute-start(f32[464,128]{1,0:T(8,128)S(1)} %get-tuple-element.21), channel_id=1, source_target_pairs={{0,120},{8,16},{16,8},{24,32},{32,24},{40,48},{48,40},{56,64},{64,... | collective-permute-start | bytes 712712 | tf_op jit(solution)/shard_map/ppermute | solution.py:381
  13.5 8.7 %copy-start.1 = (f32[4,16,32,128]{3,2,1,0:T(8,128)S(1)}, f32[4,16,32,128]{3,2,1,0:T(8,128)}, u32[]{:S(2)}) copy-start(f32[4,16,32,128]{3,2,1,0:T(8,128)} %q_in.3) | copy-start | bytes 3145732
  13.5 13.8 %collective-permute-start.2 = (f32[464,128]{1,0:T(8,128)S(1)}, f32[464,128]{1,0:T(8,128)S(1)}, u32[]{:S(2)}, u32[]{:S(2)}) collective-permute-start(f32[464,128]{1,0:T(8,128)S(1)} %get-tuple-element.22), channel_id=1, source_target_pairs={{0,120},{8,16},{16,8},{24,32},{32,24},{40,48},{48,40},{56,64},{64,... | collective-permute-start | bytes 712712 | tf_op jit(solution)/shard_map/ppermute | solution.py:382
  17.1 10.2 %collective-permute-start.5 = (f32[232,128]{1,0:T(8,128)S(1)}, f32[232,128]{1,0:T(8,128)S(1)}, u32[]{:S(2)}, u32[]{:S(2)}) collective-permute-start(f32[232,128]{1,0:T(8,128)S(1)} %get-tuple-element.27), channel_id=1, source_target_pairs={{0,8},{8,0},{16,24},{24,16},{32,40},{40,32},{48,56},{56,48},{64,72... | collective-permute-start | bytes 356360 | tf_op jit(solution)/shard_map/ppermute | solution.py:390
  17.2 12.6 %collective-permute-start.6 = (f32[232,128]{1,0:T(8,128)S(1)}, f32[232,128]{1,0:T(8,128)S(1)}, u32[]{:S(2)}, u32[]{:S(2)}) collective-permute-start(f32[232,128]{1,0:T(8,128)S(1)} %get-tuple-element.28.after_ref), channel_id=1, source_target_pairs={{0,120},{8,16},{16,8},{24,32},{32,24},{40,48},{48,40},{56,64},{64,... | collective-permute-start | bytes 356360 | tf_op jit(solution)/shard_map/ppermute | solution.py:389
  20.3 1.1 %copy-start.3 = (bf16[1280,256]{1,0:T(8,128)(2,1)S(1)}, bf16[1280,256]{1,0:T(8,128)(2,1)}, u32[]{:S(2)}) copy-start(bf16[1280,256]{1,0:T(8,128)(2,1)} %constant.31.clone.ws_hbm) | copy-start | bytes 1966084

commit v6 on v5

--- a/solution.py
+++ b/solution.py
@@ -187,8 +187,9 @@
     return high, (a - high.astype(F32)).astype(jnp.bfloat16)
 
 
-EARLY = {1: (4, 3, 24), 2: (8, 2, 16)}
-FRAME = {1: ((-12, 2), (28, 2)), 2: ((-8, 2), (24, 2)), 3: ((-6, 6),), 4: ((-4, 5),), 5: ((-2, 5),), 6: ((0, 4),)}
+EARLY = {1: (2, 4, 28), 2: (4, 3, 24), 3: (8, 2, 16)}
+FRAME = {1: ((-10, 2), (26, 2)), 2: ((-8, 2), (24, 2)), 3: ((-6, 2), (22, 2)),
+         4: ((-4, 5),), 5: ((-2, 5),), 6: ((0, 4),)}
 WEIGHTS = [(0.0, 1.0), (0.75, 0.25), (1.0 / 3.0, 2.0 / 3.0)]
 
 

time: 52.2 us -> 51.2 us (0.981)
  waiting for transfers between devices: 5.2 us -> 2.01 us
  Pallas kernels: 29.5 us -> 31.7 us
    pallas_call x1, Pallas kernels: 4.03 us -> 7.2 us  [body(): call(early_kernel, parts, scratch, inputs=6, vmem_mib=32)]
    ppermute x1, waiting for transfers between devices: 2.54 us -> 0.31 us  [body(): cb = lax.ppermute(cb, 'gx', pairs(nx, 1))]
    pallas_call x1, Pallas kernels: 22.1 us -> 21.2 us  [body(): call(main_kernel, [(NF, NZ, NX, NY)], scratch, inputs=11 + len(parts), vm...]
    ppermute x1, waiting for transfers between devices: 0.96 us -> 0.01 us  [body(): xb2 = lax.ppermute(xb2, 'gx', pairs(nx, 1))]
  transfers between devices with their start and end apart: 7 -> 7, of which waited for: 4 -> 3; matrix products, arithmetic and copies ran while one was open for 0% -> 0% of each run, Pallas kernels for 11% -> 17%
where the time goes in v6:
time: 51.2 us; the launch traced here: 51 us
  Pallas kernels  31.7 us (62%)
  starting transfers between devices  13.8 us (27%)
  local copies, waits for them, and re-layouts  2.32 us (5%)
  waiting for transfers between devices  2.01 us (4%)
  other arithmetic  1.04 us (2%)
    pallas_call x1, Pallas kernels, body(): call(main_kernel, [(NF, NZ, NX, NY)], scratch, inputs=11 + len(parts), vm...  21.2 us
    pallas_call x1, Pallas kernels, body(): call(early_kernel, parts, scratch, inputs=6, vmem_mib=32)  7.2 us
    ppermute x1, starting transfers between devices, body(): yb = lax.ppermute(yb, 'gy', pairs(ny, 1))  6.66 us
    ppermute x1, starting transfers between devices, body(): cb = lax.ppermute(cb, 'gx', pairs(nx, 1))  3.14 us
    ppermute x1, starting transfers between devices, body(): xb = lax.ppermute(xb, 'gx', pairs(nx, 1))  2.8 us
    unnamed x8, local copies, waits for them, and re-layouts  2.32 us
    pallas_call x1, Pallas kernels, body(): call(pack_kernel, [ymsg, ymsg, (NZ * MSG, NY)] + parts, inputs=2)  1.67 us
    ppermute x1, waiting for transfers between devices, body(): ya = lax.ppermute(ya, 'gy', pairs(ny, 0))  1.2 us
  transfers between devices with their start and end apart: 7, of which 3 were waited for; matrix products, arithmetic and copies ran while one was open for 0% of the time, Pallas kernels for 17%

profile of v6, /device:TPU:0, one launch (start us, length us, event | category | flops | bytes accessed | tf_op | source)
XLA Modules:
  0.0 51.0 jit_solution(5311951547458037837)
XLA Ops:
  0.0 1.0 %convert_element_type.3.m_ref.m_in = f32[16,32,128]{2,1,0:T(8,128)S(1)} convert(s32[16,32,128]{2,1,0:T(8,128)} %param.5) | non-fusion elementwise | flops 65536 | bytes 524288 | tf_op jit(solution)/shard_map/convert_element_type | solution.py:378
  1.0 0.1 pad_add_fusion.par_ref
  1.1 0.0 copy-start
  1.1 1.2 %copy-done = f32[4,16,32,128]{3,2,1,0:T(8,128)S(1)} copy-done((f32[4,16,32,128]{3,2,1,0:T(8,128)S(1)}, f32[4,16,32,128]{3,2,1,0:T(8,128)}, u32[]{:S(2)}) %copy-start) | copy-done | bytes 1048600
  2.3 0.0 copy-start.2
  2.3 1.7 %shard_map.46 = (f32[4,2,32,128]{3,2,1,0:T(8,128)S(1)}, f32[4,2,32,128]{3,2,1,0:T(8,128)S(1)}, f32[928,128]{1,0:T(8,128)S(1)}, f32[464,128]{1,0:T(8,128)S(1)}, f32[464,128]{1,0:T(8,128)S(1)}) custom-call(s32[2]{0:T(128)S(1)} %pad_add_fusion.par_ref, f32[4,16,32,128]{3,2,1,0:T(8,128)S(1)} %copy-done, f32[16,32,128]{2,1,0:T(8,128)S(1)} %convert_element_type.3.m_ref.m_in), custom_call_target="tpu_custom_call" | custom-call | tf_op jit(solution)/shard_map/pallas_call | solution.py:379
  4.0 0.1 collective-permute-start
  4.1 6.7 %collective-permute-start.3 = (f32[4,2,32,128]{3,2,1,0:T(8,128)S(1)}, f32[4,2,32,128]{3,2,1,0:T(8,128)S(1)}, u32[]{:S(2)}, u32[]{:S(2)}) collective-permute-start(f32[4,2,32,128]{3,2,1,0:T(8,128)S(1)} %get-tuple-element.25), channel_id=1, source_target_pairs={{0,7},{1,2},{2,1},{3,4},{4,3},{5,6},{6,5},{7,0},{8,15},{9,10},{10,... | collective-permute-start | bytes 393224 | tf_op jit(solution)/shard_map/ppermute | solution.py:380
  10.7 0.0 collective-permute-start.4
  10.7 2.8 %collective-permute-start.1 = (f32[464,128]{1,0:T(8,128)S(1)}, f32[464,128]{1,0:T(8,128)S(1)}, u32[]{:S(2)}, u32[]{:S(2)}) collective-permute-start(f32[464,128]{1,0:T(8,128)S(1)} %get-tuple-element.23), channel_id=1, source_target_pairs={{0,120},{8,16},{16,8},{24,32},{32,24},{40,48},{48,40},{56,64},{64,... | collective-permute-start | bytes 712712 | tf_op jit(solution)/shard_map/ppermute | solution.py:382
  13.5 0.0 copy-start.1
  13.5 1.1 %collective-permute-start.2 = (f32[464,128]{1,0:T(8,128)S(1)}, f32[464,128]{1,0:T(8,128)S(1)}, u32[]{:S(2)}, u32[]{:S(2)}) collective-permute-start(f32[464,128]{1,0:T(8,128)S(1)} %get-tuple-element.24), channel_id=1, source_target_pairs={{0,120},{8,16},{16,8},{24,32},{32,24},{40,48},{48,40},{56,64},{64,... | collective-permute-start | bytes 712712 | tf_op jit(solution)/shard_map/ppermute | solution.py:383
  14.6 0.5 collective-permute-done.3.yb_ref
  15.1 1.2 %collective-permute-done.4.ya_ref = f32[4,2,32,128]{3,2,1,0:T(8,128)S(1)} collective-permute-done((f32[4,2,32,128]{3,2,1,0:T(8,128)S(1)}, f32[4,2,32,128]{3,2,1,0:T(8,128)S(1)}, u32[]{:S(2)}, u32[]{:S(2)}) %collective-permute-start.4) | collective-permute-done | bytes 131104 | tf_op jit(solution)/shard_map/ppermute | solution.py:381
  16.3 0.8 %shard_map.47 = (f32[4,4,32,128]{3,2,1,0:T(8,128)S(1)}, f32[4,32,128]{2,1,0:T(8,128)S(1)}, f32[232,128]{1,0:T(8,128)S(1)}, f32[232,128]{1,0:T(8,128)S(1)}) custom-call(s32[2]{0:T(128)S(1)} %pad_add_fusion.par_ref, f32[4,2,32,128]{3,2,1,0:T(8,128)S(1)} %collective-permute-done.3.yb_ref, f32[4,2,32,128]{3,2,1,0:T(8,128)S(1)} %collective-permute-done.4.ya_ref), custom_call_target="tpu_custom_call" | custom-call | tf_op jit(solution)/shard_map/pallas_call | solution.py:385
  17.1 0.1 collective-permute-start.5
  17.2 3.1 %collective-permute-start.6 = (f32[232,128]{1,0:T(8,128)S(1)}, f32[232,128]{1,0:T(8,128)S(1)}, u32[]{:S(2)}, u32[]{:S(2)}) collective-permute-start(f32[232,128]{1,0:T(8,128)S(1)} %get-tuple-element.30.after_ref), channel_id=1, source_target_pairs={{0,120},{8,16},{16,8},{24,32},{32,24},{40,48},{48,40},{56,64},{64,... | collective-permute-start | bytes 356360 | tf_op jit(solution)/shard_map/ppermute | solution.py:390
  20.3 0.0 copy-done.2
  20.3 0.0 copy-start.3
  20.3 1.1 %copy-done.3 = bf16[1280,256]{1,0:T(8,128)(2,1)S(1)} copy-done((bf16[1280,256]{1,0:T(8,128)(2,1)S(1)}, bf16[1280,256]{1,0:T(8,128)(2,1)}, u32[]{:S(2)}) %copy-start.3) | copy-done | bytes 655384
  21.4 0.8 %shard_map.48 = (bf16[4,512,256]{2,1,0:T(8,128)(2,1)S(1)}, bf16[1280,256]{1,0:T(8,128)(2,1)S(1)}) custom-call(s32[2]{0:T(128)S(1)} %pad_add_fusion.par_ref, bf16[4,512,256]{2,1,0:T(8,128)(2,1)S(1)} %copy-done.2, bf16[1280,256]{1,0:T(8,128)(2,1)S(1)} %copy-done.3, f32[232,128]{1,0:T(8,128)S(1)} %get-tuple-element.30.after_ref), custom_call_target="tpu_custom_call" | custom-call | tf_op jit(solution)/shard_map/pallas_call | solution.py:388
  22.3 0.0 copy-done.1
  22.3 7.2 %shard_map.49 = (f32[4,16,32,128]{3,2,1,0:T(8,128)S(1)}, f32[4,4,32,128]{3,2,1,0:T(8,128)S(1)}, f32[4,16,24,128]{3,2,1,0:T(8,128)S(1)}, f32[4,4,24,128]{3,2,1,0:...) custom-call(s32[2]{0:T(128)S(1)} %pad_add_fusion.par_ref, f32[4,16,32,128]{3,2,1,0:T(8,128)S(1)} %copy-done.1, ...), custom_call_target="tpu_custom_call" | custom-call | tf_op jit(solution)/shard_map/pallas_call | solution.py:400
  29.5 0.0 collective-permute-done.1.xb_ref
  29.5 0.0 collective-permute-done.2.xb2_ref
  29.5 0.0 collective-permute-done.5.ca_ref
  29.5 0.3 collective-permute-done.6.cb_ref
  29.8 0.0 collective-permute-done.xa_ref
  29.8 21.2 %shard_map.50 = f32[4,16,32,128]{3,2,1,0:T(8,128)} custom-call(s32[2]{0:T(128)S(1)} %pad_add_fusion.par_ref, f32[4,16,32,128]{3,2,1,0:T(8,128)S(1)} %copy-done.1, f32[16,32,128]{2,1,0:T(8,128)S(1)} %convert_element_type.3.m_ref.m_in, f32[928,128]{1,0:T(8,128)S(1)} %collective-permute-done.xa_ref, f32[464,128]{1,0:T(8,128)S(1)} %collective-permute-done.1.xb_ref, ...), custom_call_target="tpu_custom_call" | custom-call | tf_op jit(solution)/shard_map/pallas_call | solution.py:401
Async XLA Ops:
  1.1 1.2 %copy-start = (f32[4,16,32,128]{3,2,1,0:T(8,128)S(1)}, f32[4,16,32,128]{3,2,1,0:T(8,128)}, u32[]{:S(2)}) copy-start(f32[4,16,32,128]{3,2,1,0:T(8,128)} %q_in.3) | copy-start | bytes 3145732
  2.3 18.0 %copy-start.2 = (bf16[4,512,256]{2,1,0:T(8,128)(2,1)S(1)}, bf16[4,512,256]{2,1,0:T(8,128)(2,1)}, u32[]{:S(2)}) copy-start(bf16[4,512,256]{2,1,0:T(8,128)(2,1)} %constant.30.clone.w_hbm) | copy-start | bytes 3145732
  4.0 25.9 %collective-permute-start = (f32[928,128]{1,0:T(8,128)S(1)}, f32[928,128]{1,0:T(8,128)S(1)}, u32[]{:S(2)}, u32[]{:S(2)}) collective-permute-start(f32[928,128]{1,0:T(8,128)S(1)} %get-tuple-element.22), channel_id=1, source_target_pairs={{0,8},{8,0},{16,24},{24,16},{32,40},{40,32},{48,56},{56,48},{64,72... | collective-permute-start | bytes 1425416 | tf_op jit(solution)/shard_map/ppermute | solution.py:384
  4.1 11.0 %collective-permute-start.3 = (f32[4,2,32,128]{3,2,1,0:T(8,128)S(1)}, f32[4,2,32,128]{3,2,1,0:T(8,128)S(1)}, u32[]{:S(2)}, u32[]{:S(2)}) collective-permute-start(f32[4,2,32,128]{3,2,1,0:T(8,128)S(1)} %get-tuple-element.25), channel_id=1, source_target_pairs={{0,7},{1,2},{2,1},{3,4},{4,3},{5,6},{6,5},{7,0},{8,15},{9,10},{10,... | collective-permute-start | bytes 393224 | tf_op jit(solution)/shard_map/ppermute | solution.py:380
  10.7 5.6 %collective-permute-start.4 = (f32[4,2,32,128]{3,2,1,0:T(8,128)S(1)}, f32[4,2,32,128]{3,2,1,0:T(8,128)S(1)}, u32[]{:S(2)}, u32[]{:S(2)}) collective-permute-start(f32[4,2,32,128]{3,2,1,0:T(8,128)S(1)} %get-tuple-element.26), channel_id=1, source_target_pairs={{0,1},{1,0},{2,3},{3,2},{4,5},{5,4},{6,7},{7,6},{8,9},{9,8},{10,11... | collective-permute-start | bytes 393224 | tf_op jit(solution)/shard_map/ppermute | solution.py:381
  10.7 18.8 %collective-permute-start.1 = (f32[464,128]{1,0:T(8,128)S(1)}, f32[464,128]{1,0:T(8,128)S(1)}, u32[]{:S(2)}, u32[]{:S(2)}) collective-permute-start(f32[464,128]{1,0:T(8,128)S(1)} %get-tuple-element.23), channel_id=1, source_target_pairs={{0,120},{8,16},{16,8},{24,32},{32,24},{40,48},{48,40},{56,64},{64,... | collective-permute-start | bytes 712712 | tf_op jit(solution)/shard_map/ppermute | solution.py:382
  13.5 8.7 %copy-start.1 = (f32[4,16,32,128]{3,2,1,0:T(8,128)S(1)}, f32[4,16,32,128]{3,2,1,0:T(8,128)}, u32[]{:S(2)}) copy-start(f32[4,16,32,128]{3,2,1,0:T(8,128)} %q_in.3) | copy-start | bytes 3145732
  13.5 16.0 %collective-permute-start.2 = (f32[464,128]{1,0:T(8,128)S(1)}, f32[464,128]{1,0:T(8,128)S(1)}, u32[]{:S(2)}, u32[]{:S(2)}) collective-permute-start(f32[464,128]{1,0:T(8,128)S(1)} %get-tuple-element.24), channel_id=1, source_target_pairs={{0,120},{8,16},{16,8},{24,32},{32,24},{40,48},{48,40},{56,64},{64,... | collective-permute-start | bytes 712712 | tf_op jit(solution)/shard_map/ppermute | solution.py:383
  17.1 12.4 %collective-permute-start.5 = (f32[232,128]{1,0:T(8,128)S(1)}, f32[232,128]{1,0:T(8,128)S(1)}, u32[]{:S(2)}, u32[]{:S(2)}) collective-permute-start(f32[232,128]{1,0:T(8,128)S(1)} %get-tuple-element.29), channel_id=1, source_target_pairs={{0,8},{8,0},{16,24},{24,16},{32,40},{40,32},{48,56},{56,48},{64,72... | collective-permute-start | bytes 356360 | tf_op jit(solution)/shard_map/ppermute | solution.py:391
  17.2 12.6 %collective-permute-start.6 = (f32[232,128]{1,0:T(8,128)S(1)}, f32[232,128]{1,0:T(8,128)S(1)}, u32[]{:S(2)}, u32[]{:S(2)}) collective-permute-start(f32[232,128]{1,0:T(8,128)S(1)} %get-tuple-element.30.after_ref), channel_id=1, source_target_pairs={{0,120},{8,16},{16,8},{24,32},{32,24},{40,48},{48,40},{56,64},{64,... | collective-permute-start | bytes 356360 | tf_op jit(solution)/shard_map/ppermute | solution.py:390
  20.3 1.1 %copy-start.3 = (bf16[1280,256]{1,0:T(8,128)(2,1)S(1)}, bf16[1280,256]{1,0:T(8,128)(2,1)}, u32[]{:S(2)}) copy-start(bf16[1280,256]{1,0:T(8,128)(2,1)} %constant.31.clone.ws_hbm) | copy-start | bytes 1966084
